TPU v7x, 32 devices: a whole 2x2x4 slice. The times are simulated.
32 devices in a mesh: fsdp: 8 (over z, x), member: 4 (over y, core).
Axes of the slice: x: 2, y: 2, z: 4, core: 2. Of those that a mesh axis runs over, the one named last changes fastest.
Arguments:
- frames: bfloat16 [4, 1152, 1536], P('member', 'fsdp'), may hold values from -6 to 6
- layer_norm_gain: float32 [1536], replicated, may hold values from 0.25 to 1.75
- input_projection: bfloat16 [1536, 6144], P('fsdp', 'member'), may hold values from -0.15625 to 0.15625
- output_projection: bfloat16 [6144, 1536], P('member', 'fsdp'), may hold values from -0.078125 to 0.078125
- adapter_down_map: bfloat16 [4, 1536, 64], P('member'), may hold values from -0.15625 to 0.15625
- adapter_up_map: bfloat16 [4, 64, 6144], P('member'), may hold values from -0.75 to 0.75
- lengths: int32 [4, 8], P('member', 'fsdp'), may hold values from 90 to 126, as said below
- cotangent: bfloat16 [4, 1152, 1536], P('member', 'fsdp'), may hold values from -0.29882812 to 0.29882812
Outputs:
- down_map_gradient: float32 [4, 1536, 64], P('member')
- up_map_gradient: float32 [4, 64, 6144], P('member')
Inputs may be any that keep to these rules, and one draw needn't show every extreme that they name: `lengths`: each member has at least one utterance of exactly 126 frames.
All inputs are finite; a program needn't handle non-finite values.
Results may differ from a plain program's by a relative error of at most 0.0058.
Values may be sent and summed in bfloat16 or wider, within the bound.
No kernel may reach another device: no remote copies, remote signals or barrier semaphores. Data moves between devices by JAX's collectives and lax.ppermute only.
A program may use at most 128 MiB of HBM per device.

v0:
```python
import jax
import jax.numpy as jnp
from jax import lax
from jax.sharding import PartitionSpec as P

BUCKET = 144


def on_device(
    frames,
    layer_norm_gain,
    input_projection,
    output_projection,
    adapter_down_map,
    adapter_up_map,
    lengths,
    cotangent,
):
    members = lax.axis_size("member")
    values = frames[0].astype(jnp.float32)
    mean = jnp.mean(values, axis=1, keepdims=True)
    var = jnp.mean((values - mean) ** 2, axis=1, keepdims=True)
    normed_input = (layer_norm_gain * (values - mean) / jnp.sqrt(var + 1e-05)).astype(jnp.bfloat16)
    low_rank_state = jnp.dot(
        normed_input, adapter_down_map[0], preferred_element_type=jnp.float32
    ).astype(jnp.bfloat16)
    positions = jnp.arange(BUCKET, dtype=jnp.int32)
    mask = (positions[None, :] < lengths[0][:, None]).reshape(-1)
    masked = cotangent[0] * mask.astype(cotangent.dtype)[:, None]
    rows = normed_input.shape[0]
    up_map_slices = lax.all_to_all(
        adapter_up_map, "member", split_axis=2, concat_axis=0, tiled=True
    )
    stacked_norm, stacked_low, stacked_grad = (
        lax.all_gather(normed_input, "member", axis=0, tiled=True),
        lax.all_gather(low_rank_state, "member", axis=0, tiled=True),
        lax.all_gather(masked, "member", axis=0, tiled=True),
    )
    low_rank_blocks = stacked_low.reshape(members, rows, -1)
    adapter_term = jnp.einsum(
        "dgs,dsb->dgb", low_rank_blocks, up_map_slices, preferred_element_type=jnp.float32
    )
    adapter_term = adapter_term.reshape(members * rows, -1)
    columns = stacked_norm
    pre = adapter_term + jnp.dot(
        columns,
        lax.all_gather(input_projection, "fsdp", axis=0, tiled=True),
        preferred_element_type=jnp.float32,
    )
    columns = stacked_grad
    dhid = 0.5 * lax.dot_general(
        columns,
        lax.all_gather(output_projection, "fsdp", axis=1, tiled=True),
        (((1,), (1,)), ((), ())),
        preferred_element_type=jnp.float32,
    )
    sigma = jax.nn.sigmoid(pre)
    dpre = (dhid * sigma * (1.0 + pre * (1.0 - sigma))).astype(jnp.bfloat16)
    preact_gradient_blocks = dpre.reshape(members, rows, -1)
    up_partial = jnp.einsum(
        "jnz,jnv->jzv", low_rank_blocks, preact_gradient_blocks, preferred_element_type=jnp.float32
    )
    back_partial = jnp.einsum(
        "yha,ywa->yhw", preact_gradient_blocks, up_map_slices, preferred_element_type=jnp.float32
    )
    back = lax.psum_scatter(back_partial, "member", scatter_dimension=0, tiled=True)[0].astype(
        jnp.bfloat16
    )
    down_partial = jnp.dot(normed_input.T, back, preferred_element_type=jnp.float32)
    up_summed = lax.psum(up_partial, "fsdp")
    up_map_gradient = lax.all_to_all(up_summed, "member", split_axis=0, concat_axis=2, tiled=True)
    down_map_gradient = lax.psum(down_partial, "fsdp")
    return (down_map_gradient[None], up_map_gradient)


def solution(mesh):
    in_specs = (
        P("member", "fsdp", None),
        P(),
        P("fsdp", "member"),
        P("member", "fsdp"),
        P("member", None, None),
        P("member", None, None),
        P("member", "fsdp"),
        P("member", "fsdp", None),
    )
    out_specs = (P("member", None, None), P("member", None, None))
    return jax.shard_map(
        on_device, mesh=mesh, in_specs=in_specs, out_specs=out_specs, check_vma=False
    )
```

profile of v0, /device:TPU:0, one launch (start us, length us, event | category | flops | bytes accessed | tf_op | source)
XLA Modules:
  0.0 384.1 jit_solution(4388464174535293673)
XLA Ops:
  7.2 1.2 convert_reduce_fusion
  8.4 1.3 fusion.7
  9.7 2.0 fusion.9
  11.8 0.7 all-gather.12.cloned.1.call-update
  13.2 1.9 bitcast_multiply_fusion
  15.2 0.5 all-gather.8.cloned.1.call-update
  15.7 6.7 %copy.12 = bf16[1,64,6144]{1,0,2:T(2,128)(2,1)S(1)} copy(bf16[1,64,6144]{2,1,0:T(8,128)(2,1)} %param.13) | data formatting | bytes 1572864 | tf_op args[5]
  22.4 0.5 broadcast.58
  22.9 34.4 %reduce.1 = bf16[6144,64]{1,0:T(8,128)(2,1)} reduce(bf16[6144,1,64]{2,1,0:T(2,128)(2,1)S(1)} %bitcast.60, bf16[]{:T(256)} %broadcast.58), dimensions={1}, to_apply=%bitcast.47.reduce_sub_computation | reduce | bytes 1572866
  57.4 4.1 %reshape.87 = bf16[4,2,49152]{2,1,0:T(2,128)(2,1)} reshape(bf16[6144,64]{1,0:T(8,128)(2,1)} %reduce.1) | data formatting | bytes 1572864
  61.5 4.3 %all-to-all-start = ((bf16[4,2,49152]{2,1,0:T(2,128)(2,1)}), bf16[4,2,49152]{2,1,0:T(2,128)(2,1)}, u32[]{:S(2)}, u32[]{:S(2)}) async-start(bf16[4,2,49152]{2,1,0:T(2,128)(2,1)} %reshape.87), calls=%async_computation | async-start | bytes 1572864 | tf_op jit(solution)/shard_map/all_to_all | solution.py:31
  65.8 0.2 fusion.14
  66.0 0.8 copy-done.2
  66.8 0.3 fusion
  67.0 12.4 %all-gather = bf16[4,144,64]{1,2,0:T(8,128)(2,1)S(1)} all-gather(bf16[1,144,64]{1,2,0:T(8,128)(2,1)S(1)} %fusion), channel_id=1, replica_groups=mesh['fsdp'=8,'member'=4] {'member'}, dimensions={0}, use_global_device_ids=true | all-gather | bytes 92160 | tf_op jit(solution)/shard_map/all_gather | solution.py:36
  79.5 2.8 reshape.88
  82.3 1.3 copy.18
  83.6 1.7 copy.14
  85.3 2.5 fusion.12
  87.8 29.7 %all-gather.12.cloned.1.call-done = bf16[1536,1536]{1,0:T(8,128)(2,1)} async-done(((bf16[192,1536]{1,0:T(8,128)(2,1)}), bf16[1536,1536]{1,0:T(8,128)(2,1)}) %all-gather.12.cloned.1.call-update) | async-done | bytes 4718608 | tf_op jit(solution)/shard_map/all_gather | solution.py:47
  117.5 7.6 %fusion.18 = f32[576,1536]{1,0:T(8,128)} fusion(bf16[576,1536]{1,0:T(8,128)(2,1)} %all-gather.10.cloned.1.call-done, bf16[1536,1536]{1,0:T(8,128)(2,1)} %all-gather.12.cloned.1.call-done), kind=kOutput, calls=%fused_computation.29 | convolution fusion | flops 2717908992 | bytes 10027008 | tf_op jit(solution)/shard_map/dot_general | solution.py:45
  125.0 12.9 %all-gather.6.cloned.1.call-done = bf16[576,1536]{1,0:T(8,128)(2,1)} async-done(((bf16[144,1536]{1,0:T(8,128)(2,1)}), bf16[576,1536]{1,0:T(8,128)(2,1)}) %all-gather.6.cloned.1.call-update) | async-done | bytes 1769488 | tf_op jit(solution)/shard_map/all_gather | solution.py:37
  138.0 82.0 %all-gather.8.cloned.1.call-done = bf16[1536,1536]{0,1:T(8,128)(2,1)} async-done(((bf16[1536,192]{0,1:T(8,128)(2,1)}), bf16[1536,1536]{0,1:T(8,128)(2,1)}) %all-gather.8.cloned.1.call-update) | async-done | bytes 4718608 | tf_op jit(solution)/shard_map/all_gather | solution.py:53
  219.9 8.5 %multiply_convert_fusion = bf16[576,1536]{1,0:T(8,128)(2,1)S(1)} fusion(f32[576,1536]{1,0:T(8,128)} %fusion.18, f32[4,144,1536]{2,1,0:T(8,128)} %fusion.12, bf16[576,1536]{1,0:T(8,128)(2,1)} %all-gather.6.cloned.1.call-done, bf16[1536,1536]{0,1:T(8,128)(2,1)} %all-gather.8.cloned.1.call-done), kind=kOutput, calls=%fused_computation.1 | convolution fusion | flops 2727641088 | bytes 15335424 | tf_op jit(solution)/shard_map/dot_general | solution.py:51
  228.5 1.4 fusion.10
  229.9 1.5 fusion.19
  231.5 16.7 %reduce-scatter.2.cloned.1.call-done = f32[1,144,64]{1,2,0:T(8,128)} async-done(((f32[4,144,64]{1,2,0:T(8,128)}), f32[1,144,64]{1,2,0:T(8,128)}) %reduce-scatter.2.cloned.1.call-update) | async-done | bytes 36880 | tf_op jit(solution)/shard_map/reduce_scatter | solution.py:66
  248.2 1.8 convolution_bitcast_fusion
  250.0 101.5 %all-reduce.3.cloned.1.call-done = (f32[1,1536,64]{1,2,0:T(8,128)}, f32[4,64,1536]{2,1,0:T(8,128)}) async-done(((f32[1,1536,64]{1,2,0:T(8,128)}, f32[4,64,1536]{2,1,0:T(8,128)}), (f32[1,1536,64]{1,2,0:T(8,128)}, f32[4,64,1536]{2,1,0:T(8,128)})) %all-reduce.3.cloned.1.call-update) | async-done | bytes 1966096 | tf_op jit(solution)/shard_map/psum | solution.py:72
  351.5 23.7 %all_to_all.36 = f32[4,64,1536]{2,1,0:T(8,128)S(1)} all-to-all(f32[4,64,1536]{2,1,0:T(8,128)} %get-tuple-element.3), channel_id=1, replica_groups=mesh['fsdp'=8,'member'=4] {'member'}, dimensions={0} | all-to-all | bytes 3145728 | tf_op jit(solution)/shard_map/all_to_all | solution.py:71
  375.3 1.3 copy.19
  376.5 0.7 copy.23
  (26 shorter events, 0.3 us)
Async XLA Ops:
  7.2 59.6 %copy-start = (bf16[1,1536,64]{1,2,0:T(8,128)(2,1)S(1)}, bf16[1,1536,64]{1,2,0:T(8,128)(2,1)}, u32[]{:S(2)}) copy-start(bf16[1,1536,64]{1,2,0:T(8,128)(2,1)} %param.12) | copy-start | bytes 589828
  7.2 80.6 %all-gather.10.cloned.1.call-start = ((), (), s32[]{:S(2)}) async-start(), calls=%async_computation.5 | async-start | bytes 2211840 | tf_op jit(solution)/shard_map/all_gather | solution.py:35
  11.8 105.7 %all-gather.12.cloned.1.call-start = ((), (), s32[]{:S(2)}) async-start(), calls=%async_computation.6 | async-start | bytes 5308416 | tf_op jit(solution)/shard_map/all_gather | solution.py:47
  12.5 125.5 %all-gather.6.cloned.1.call-start = ((), (), s32[]{:S(2)}) async-start(), calls=%async_computation.3 | async-start | bytes 2211840 | tf_op jit(solution)/shard_map/all_gather | solution.py:37
  15.2 204.8 %all-gather.8.cloned.1.call-start = ((), (), s32[]{:S(2)}) async-start(), calls=%async_computation.4 | async-start | bytes 5308416 | tf_op jit(solution)/shard_map/all_gather | solution.py:53
  22.9 42.8 %copy-start.5 = (f32[1536]{0:T(1024)S(1)}, f32[1536]{0:T(1024)}, u32[]{:S(2)}) copy-start(f32[1536]{0:T(1024)} %param.9) | copy-start | bytes 18436
  57.4 8.4 %copy-start.1 = (bf16[1,144,1536]{2,1,0:T(8,128)(2,1)S(1)}, bf16[1,144,1536]{2,1,0:T(8,128)(2,1)}, u32[]{:S(2)}) copy-start(bf16[1,144,1536]{2,1,0:T(8,128)(2,1)} %param.8) | copy-start | bytes 1327108
  61.5 18.0 %all-to-all-start = ((bf16[4,2,49152]{2,1,0:T(2,128)(2,1)}), bf16[4,2,49152]{2,1,0:T(2,128)(2,1)}, u32[]{:S(2)}, u32[]{:S(2)}) async-start(bf16[4,2,49152]{2,1,0:T(2,128)(2,1)} %reshape.87), calls=%async_computation | async-start | bytes 1572864 | tf_op jit(solution)/shard_map/all_to_all | solution.py:31
  65.8 182.5 %reduce-scatter.2.cloned.1.call-start = ((), (), s32[]{:S(2)}) async-start(), calls=%async_computation.7 | async-start | bytes 327680 | tf_op jit(solution)/shard_map/reduce_scatter | solution.py:66
  66.0 0.8 copy-start.2
  228.4 19.8 %copy-start.3 = (bf16[144,1536]{1,0:T(8,128)(2,1)S(1)}, bf16[144,1536]{1,0:T(8,128)(2,1)}, u32[]{:S(2)}) copy-start(bf16[144,1536]{1,0:T(8,128)(2,1)} %copy-done.2) | copy-start | bytes 1327108
  229.9 121.6 %all-reduce.3.cloned.1.call-start = ((), (), s32[]{:S(2)}) async-start(), calls=%async_computation.8 | async-start | bytes 3932160 | tf_op jit(solution)/shard_map/psum | solution.py:72
  351.5 25.0 %copy-start.4 = (f32[1,1536,64]{1,2,0:T(8,128)S(1)}, f32[1,1536,64]{1,2,0:T(8,128)}, u32[]{:S(2)}) copy-start(f32[1,1536,64]{1,2,0:T(8,128)} %get-tuple-element.4) | copy-start | bytes 1179652
Sparse Core Ops, SparseCore 0:
  11.9 23.4 all-gather.9
  37.6 79.8 all-gather.11
  119.1 18.8 all-gather.5
  140.0 79.8 all-gather.7
  230.0 18.1 reduce-scatter.1
  252.8 98.6 all-reduce.2
where the time goes:
time: 385 us; the launch traced here: 384 us
  waiting for transfers between devices  244 us (63%)
  other arithmetic  41.1 us (11%)
  blocking collectives  36.2 us (9%)
  matrix products  23.5 us (6%)
  local copies, waits for them, and re-layouts  19.9 us (5%)
  between operations  14.8 us (4%)
  starting transfers between devices  4.47 us (1%)
    psum x1, waiting for transfers between devices, on_device(): down_map_gradient = lax.psum(down_partial, 'fsdp')  102 us
    all_gather x1, waiting for transfers between devices, on_device(): lax.all_gather(output_projection, 'fsdp', axis=1, tiled=True)  82 us
    unnamed x1, other arithmetic  34.4 us
    all_gather x1, waiting for transfers between devices, on_device(): lax.all_gather(input_projection, 'fsdp', axis=0, tiled=True)  29.7 us
    all_to_all x1, blocking collectives, on_device(): lax.all_to_all(up_summed, 'member', split_axis=0, concat_axis=2, tiled=True)  23.7 us
    unnamed x18, local copies, waits for them, and re-layouts  16.9 us
    reduce_scatter x1, waiting for transfers between devices, on_device(): lax.psum_scatter(back_partial, 'member', scatter_dimension=0, tiled=True)[0]  16.7 us
    all_gather x1, waiting for transfers between devices, on_device(): lax.all_gather(masked, 'member', axis=0, tiled=True)  12.9 us
  transfers between devices with their start and end apart: 7, of which 5 were waited for; matrix products, arithmetic and copies ran while one was open for 17% of the time, Pallas kernels for 0%

commit v1 on v0

v1 whole, which is shorter than its diff:
```python
import jax
import jax.numpy as jnp
from jax import lax
from jax.sharding import PartitionSpec as P

BUCKET = 144
LMAX = 126
BF = jnp.bfloat16
F32 = jnp.float32


def normalize(frames, gain):
    values = frames.astype(F32)
    mean = jnp.mean(values, axis=1, keepdims=True)
    var = jnp.mean((values - mean) ** 2, axis=1, keepdims=True)
    return (gain * (values - mean) / jnp.sqrt(var + 1e-05)).astype(BF)


def swish_gradient(pre, dhid):
    sigma = jax.nn.sigmoid(pre)
    return (dhid * sigma * (1.0 + pre * (1.0 - sigma))).astype(BF)


def dot(a, b, dims=((1,), (0,))):
    return lax.dot_general(a, b, (dims, ((), ())), preferred_element_type=F32)


def flip(axis, size, bits):
    return lambda value: lax.ppermute(value, axis, [(i, i ^ bits) for i in range(size)])


def paired_halves(frames, gain, first, second, down_map, up_map, lengths, cotangent):
    f, m = lax.axis_index("fsdp"), lax.axis_index("member")
    low_bit, x = (f >> 1) & 1, f & 1
    y, core = m >> 1, m & 1
    over_x, over_low = flip("fsdp", 8, 1), flip("fsdp", 8, 2)
    over_half, over_both = flip("fsdp", 8, 4), flip("fsdp", 8, 6)
    over_xlow = flip("fsdp", 8, 3)
    over_y, over_core = flip("member", 4, 2), flip("member", 4, 1)

    width = frames.shape[2]
    rank = down_map.shape[2]
    rows = -(-LMAX // 16) * 16
    depth, block = first.shape
    part = block // 4

    normed = normalize(frames[0, :rows], gain)
    low = dot(normed, down_map[0]).astype(BF)
    keep = jnp.arange(rows, dtype=jnp.int32)[:, None] < lengths[0, 0]
    masked = cotangent[0, :rows] * keep.astype(BF)
    own = jnp.concatenate([normed, masked, low, jnp.zeros_like(low)], axis=1)

    both = jnp.concatenate([first, second.T], axis=0)

    def piece(dx, dl):
        return lax.dynamic_slice(both, (0, ((x ^ dx) * 2 + (low_bit ^ dl)) * part), (2 * depth, part))

    w00, w01 = piece(0, 0), piece(0, 1)
    wx = over_x(jnp.stack([piece(1, 0), piece(1, 1)]))
    near = [w00, over_low(w01), over_half(w00), over_both(w01)]
    far = [wx[0], over_low(wx[1]), over_half(wx[0]), over_both(wx[1])]
    pieces = jnp.stack([near[0], far[0], near[1], far[1], near[2], far[2], near[3], far[3]])
    other = over_core(pieces)
    order = f ^ jnp.arange(8)
    mine_first = jnp.concatenate([pieces, other], axis=2)
    weights = jnp.take(mine_first, order, axis=0)
    w_in = weights[:, :depth].reshape(8 * depth, 2 * part)
    w_out = weights[:, depth:].reshape(8 * depth, 2 * part)

    def columns(ym):
        return jnp.concatenate(
            [
                lax.dynamic_slice(
                    up_map[0], (0, (ym * 2 + (core ^ dc)) * block + (x * 2 + low_bit) * part), (rank, part)
                )
                for dc in range(2)
            ],
            axis=1,
        )

    maps = [columns(y), over_y(columns(1 - y))]

    fz, fx, fy = over_low(own), over_x(own), over_y(own)
    fzx, fzy = over_x(fz), over_y(fz)
    fxy = jnp.concatenate([over_x(fy[:, :width]), over_y(fx[:, width:])], axis=1)
    fzxy = over_y(fzx)
    slots = (low_bit * 2 + x) ^ jnp.arange(4)
    members = [
        jnp.take(jnp.stack([own, fx, fz, fzx]), slots, axis=0).reshape(4 * rows, -1),
        jnp.take(jnp.stack([fy, fxy, fzy, fzxy]), slots, axis=0).reshape(4 * rows, -1),
    ]

    ups, backs = [], []
    for packed, up in zip(members, maps):
        n, c, a = packed[:, :width], packed[:, width : 2 * width], packed[:, 2 * width : 2 * width + rank]
        pre = dot(n, w_in) + dot(a, up)
        dhid = 0.5 * dot(c, w_out)
        dpre = swish_gradient(pre, dhid)
        ups.append(dot(a, dpre, ((0,), (0,))))
        backs.append(dot(up, dpre, ((1,), (1,))))

    got = over_y(jnp.concatenate([ups[1], backs[1]], axis=1).astype(BF))
    hidden = 2 * part
    back = (backs[0] + got[:, hidden:].astype(F32)).astype(BF)
    bx, bz, bzx = over_x(back), over_low(back), over_xlow(back)
    up_pair = jnp.stack([ups[0].astype(BF), got[:, :hidden]])
    up_half = over_half(up_pair)
    up_sum = (up_pair.astype(F32) + up_half.astype(F32)).astype(BF)
    back_sum = (
        (back.astype(F32) + bx.astype(F32)) + (bz.astype(F32) + bzx.astype(F32))
    ).astype(BF)
    down = dot(members[0][:, :width], back_sum, ((0,), (1,))).astype(BF)
    down_other = over_half(down)
    ux, uz, uzx = over_x(up_sum), over_low(up_sum), over_xlow(up_sum)
    down_sum = down.astype(F32) + down_other.astype(F32)
    parts = jnp.take(jnp.stack([up_sum, uz, ux, uzx]), (x * 2 + low_bit) ^ jnp.arange(4), axis=0)
    parts = jnp.take(parts, y ^ jnp.arange(2), axis=1)
    parts = parts.reshape(4, 2, rank, 2, part)
    parts = jnp.take(parts, core ^ jnp.arange(2), axis=3)
    up_sum = parts.transpose(2, 1, 3, 0, 4).reshape(rank, -1).astype(F32)
    return (down_sum[None], up_sum[None])


def gathered(frames, gain, first, second, down_map, up_map, lengths, cotangent):
    members = lax.axis_size("member")
    normed = normalize(frames[0], gain)
    low = dot(normed, down_map[0]).astype(BF)
    positions = jnp.arange(BUCKET, dtype=jnp.int32)
    mask = (positions[None, :] < lengths[0][:, None]).reshape(-1)
    masked = cotangent[0] * mask.astype(BF)[:, None]
    rows = normed.shape[0]
    up_slices = lax.all_to_all(up_map, "member", split_axis=2, concat_axis=0, tiled=True)
    all_normed = lax.all_gather(normed, "member", axis=0, tiled=True)
    all_low = lax.all_gather(low, "member", axis=0, tiled=True).reshape(members, rows, -1)
    all_masked = lax.all_gather(masked, "member", axis=0, tiled=True)
    term = jnp.einsum("dgs,dsb->dgb", all_low, up_slices, preferred_element_type=F32)
    pre = term.reshape(members * rows, -1) + dot(
        all_normed, lax.all_gather(first, "fsdp", axis=0, tiled=True)
    )
    dhid = 0.5 * dot(all_masked, lax.all_gather(second, "fsdp", axis=1, tiled=True), ((1,), (1,)))
    dpre = swish_gradient(pre, dhid).reshape(members, rows, -1)
    up_partial = jnp.einsum("jnz,jnv->jzv", all_low, dpre, preferred_element_type=F32)
    back_partial = jnp.einsum("yha,ywa->yhw", dpre, up_slices, preferred_element_type=F32)
    back = lax.psum_scatter(back_partial, "member", scatter_dimension=0, tiled=True)[0].astype(BF)
    up = lax.all_to_all(lax.psum(up_partial, "fsdp"), "member", split_axis=0, concat_axis=2, tiled=True)
    down = lax.psum(dot(normed, back, ((0,), (0,))), "fsdp")
    return (down[None], up)


def solution(mesh):
    in_specs = (
        P("member", "fsdp", None),
        P(),
        P("fsdp", "member"),
        P("member", "fsdp"),
        P("member", None, None),
        P("member", None, None),
        P("member", "fsdp"),
        P("member", "fsdp", None),
    )
    out_specs = (P("member", None, None), P("member", None, None))
    paired = mesh.shape["fsdp"] == 8 and mesh.shape["member"] == 4
    return jax.shard_map(
        paired_halves if paired else gathered,
        mesh=mesh,
        in_specs=in_specs,
        out_specs=out_specs,
        check_vma=False,
    )
```

time: 385 us -> 212 us (0.55)
  waiting for transfers between devices: 244 us -> 103 us
  blocking collectives: 36.2 us -> 0 us
  starting transfers between devices: 4.47 us -> 35.6 us
  between operations: 14.8 us -> 1.72 us
  matrix products: 23.5 us -> 11.2 us
  other arithmetic: 41.1 us -> 29.3 us
  local copies, waits for them, and re-layouts: 19.9 us -> 30.1 us
    all_gather x4 -> x0, waiting for transfers between devices: 125 us -> none  [the longest x1 82 us: on_device(): lax.all_gather(output_projection, 'fsdp', axis=1, tiled=True)]
    ppermute x0 -> x26, waiting for transfers between devices: none -> 103 us  [flip(): lax.ppermute(value, axis, [(i, i ^ bits) for i in range(size)])]
    psum x1 -> x0, waiting for transfers between devices: 102 us -> none  [on_device(): down_map_gradient = lax.psum(down_partial, 'fsdp')]
    ppermute x0 -> x26, starting transfers between devices: none -> 35.6 us  [flip(): lax.ppermute(value, axis, [(i, i ^ bits) for i in range(size)])]
    unnamed x1, other arithmetic: 34.4 us -> 0.76 us
    all_to_all x1 -> x0, blocking collectives: 23.7 us -> none  [on_device(): lax.all_to_all(up_summed, 'member', split_axis=0, concat_axis=2, tiled=True)]
    reduce_scatter x1 -> x0, waiting for transfers between devices: 16.7 us -> none  [on_device(): lax.psum_scatter(back_partial, 'member', scatter_dimension=0, tiled=True)[0]]
    gather x0 -> x7, local copies, waits for them, and re-layouts: none -> 14.9 us  [the longest x1 5.36 us: paired_halves(): weights = jnp.take(mine_first, order, axis=0)]
  transfers between devices with their start and end apart: 7 -> 26, of which waited for: 5 -> 15; matrix products, arithmetic and copies ran while one was open for 17% -> 26% of each run, Pallas kernels for 0% -> 0%
where the time goes in v1:
time: 212 us; the launch traced here: 211 us
  waiting for transfers between devices  103 us (49%)
  starting transfers between devices  35.6 us (17%)
  local copies, waits for them, and re-layouts  30.1 us (14%)
  other arithmetic  29.3 us (14%)
  matrix products  11.2 us (5%)
    ppermute x26, waiting for transfers between devices, flip(): lax.ppermute(value, axis, [(i, i ^ bits) for i in range(size)])  103 us
    ppermute x26, starting transfers between devices, flip(): lax.ppermute(value, axis, [(i, i ^ bits) for i in range(size)])  35.6 us
    dot_general x12, matrix products, dot(): return lax.dot_general(a, b, (dims, ((), ())), preferred_element_type=F32)  11.2 us
    unnamed x25, local copies, waits for them, and re-layouts  6.47 us
    gather x1, local copies, waits for them, and re-layouts, paired_halves(): weights = jnp.take(mine_first, order, axis=0)  5.36 us
    select_n x1, other arithmetic, paired_halves(): jnp.take(jnp.stack([fy, fxy, fzy, fzxy]), slots, axis=0)  5.33 us
    concatenate x1, other arithmetic, paired_halves(): mine_first = jnp.concatenate([pieces, other], axis=2)  4.91 us
    gather x1, local copies, waits for them, and re-layouts, paired_halves(): jnp.take(jnp.stack([fy, fxy, fzy, fzxy]), slots, axis=0)  4.47 us
  transfers between devices with their start and end apart: 26, of which 15 were waited for; matrix products, arithmetic and copies ran while one was open for 26% of the time, Pallas kernels for 0%

profile of v1, /device:TPU:0, one launch (start us, length us, event | category | flops | bytes accessed | tf_op | source)
XLA Modules:
  0.0 210.9 jit_solution(3115220676511683762)
XLA Ops:
  7.1 3.0 %collective-permute-start = (bf16[128,3200]{1,0:T(8,128)(2,1)S(1)}, bf16[128,3200]{1,0:T(8,128)(2,1)S(1)}, u32[]{:S(2)}, u32[]{:S(2)}) collective-permute-start(bf16[128,3200]{1,0:T(8,128)(2,1)S(1)} %concatenate.22), channel_id=1, source_target_pairs={{0,4},{4,0},{8,12},{12,8},{16,20},{20,16},{24,28},{28,24},{1,5},{5... | collective-permute-start | bytes 2457608 | tf_op jit(solution)/shard_map/ppermute | solution.py:29
  11.6 1.6 collective-permute-start.1
  18.8 22.3 %collective-permute-done.3 = bf16[2,384,384]{2,1,0:T(8,128)(2,1)} collective-permute-done((bf16[2,384,384]{2,1,0:T(8,128)(2,1)}, bf16[2,384,384]{2,1,0:T(8,128)(2,1)}, u32[]{:S(2)}, u32[]{:S(2)}) %collective-permute-start.3) | collective-permute-done | bytes 589856 | tf_op jit(solution)/shard_map/ppermute | solution.py:29
  41.1 1.8 slice_bitcast_fusion.1
  42.9 1.8 collective-permute-start.5
  45.3 2.6 %collective-permute-start.6 = (bf16[384,384]{1,0:T(8,128)(2,1)S(1)}, bf16[384,384]{1,0:T(8,128)(2,1)S(1)}, u32[]{:S(2)}, u32[]{:S(2)}) collective-permute-start(bf16[384,384]{1,0:T(8,128)(2,1)S(1)} %get-tuple-element.4), channel_id=1, source_target_pairs={{0,16},{4,20},{8,24},{12,28},{16,0},{20,4},{24,8},{28,12},{1,17},{... | collective-permute-start | bytes 884744 | tf_op jit(solution)/shard_map/ppermute | solution.py:29
  48.7 1.8 collective-permute-start.16
  51.5 4.4 %collective-permute-done.5 = bf16[384,384]{1,0:T(8,128)(2,1)S(1)} collective-permute-done((bf16[384,384]{1,0:T(8,128)(2,1)S(1)}, bf16[384,384]{1,0:T(8,128)(2,1)S(1)}, u32[]{:S(2)}, u32[]{:S(2)}) %collective-permute-start.5) | collective-permute-done | bytes 294944 | tf_op jit(solution)/shard_map/ppermute | solution.py:29
  57.8 20.5 %collective-permute-done.6 = bf16[384,384]{1,0:T(8,128)(2,1)S(1)} collective-permute-done((bf16[384,384]{1,0:T(8,128)(2,1)S(1)}, bf16[384,384]{1,0:T(8,128)(2,1)S(1)}, u32[]{:S(2)}, u32[]{:S(2)}) %collective-permute-start.6) | collective-permute-done | bytes 294944 | tf_op jit(solution)/shard_map/ppermute | solution.py:29
  78.3 2.5 %collective-permute-start.9 = (bf16[384,384]{1,0:T(8,128)(2,1)S(1)}, bf16[384,384]{1,0:T(8,128)(2,1)S(1)}, u32[]{:S(2)}, u32[]{:S(2)}) collective-permute-start(bf16[384,384]{1,0:T(8,128)(2,1)S(1)} %get-tuple-element.16), channel_id=1, source_target_pairs={{0,24},{4,28},{8,16},{12,20},{16,8},{20,12},{24,0},{28,4},{1,25},{... | collective-permute-start | bytes 884744 | tf_op jit(solution)/shard_map/ppermute | solution.py:29
  83.0 11.1 %collective-permute-done.7 = bf16[384,384]{1,0:T(8,128)(2,1)S(1)} collective-permute-done((bf16[384,384]{1,0:T(8,128)(2,1)S(1)}, bf16[384,384]{1,0:T(8,128)(2,1)S(1)}, u32[]{:S(2)}, u32[]{:S(2)}) %collective-permute-start.7) | collective-permute-done | bytes 294944 | tf_op jit(solution)/shard_map/ppermute | solution.py:29
  99.8 4.3 %collective-permute-done.12 = bf16[128,1536]{1,0:T(8,128)(2,1)S(1)} collective-permute-done((bf16[128,1536]{1,0:T(8,128)(2,1)S(1)}, bf16[128,1536]{1,0:T(8,128)(2,1)S(1)}, u32[]{:S(2)}, u32[]{:S(2)}) %collective-permute-start.12) | collective-permute-done | bytes 393248 | tf_op jit(solution)/shard_map/ppermute | solution.py:29
  104.7 2.2 %collective-permute-done.13 = bf16[128,1664]{1,0:T(8,128)(2,1)S(1)} collective-permute-done((bf16[128,1664]{1,0:T(8,128)(2,1)S(1)}, bf16[128,1664]{1,0:T(8,128)(2,1)S(1)}, u32[]{:S(2)}, u32[]{:S(2)}) %collective-permute-start.13) | collective-permute-done | bytes 426016 | tf_op jit(solution)/shard_map/ppermute | solution.py:29
  107.8 3.1 %pad_maximum_fusion.1 = bf16[4,128,3200]{2,1,0:T(8,128)(2,1)} fusion(bf16[1,128,3200]{2,1,0:T(8,128)(2,1)} %bitcast.8, bf16[1,128,3200]{2,1,0:T(8,128)(2,1)} %bitcast.7, bf16[1,128,3200]{2,1,0:T(8,128)(2,1)S(1)} %bitcast.121, bf16[1,128,3200]{2,1,0:T(8,128)(2,1)S(1)} %bitcast.113), kind=kLoop, calls=%fused_computation.8 | loop fusion | flops 4915200 | bytes 6553600 | tf_op jit(solution)/shard_map/stack | solution.py:89
  110.8 2.9 %gather_fusion.4 = bf16[4,128,3200]{2,1,0:T(8,128)(2,1)S(1)} fusion(bf16[4,128,3200]{2,1,0:T(8,128)(2,1)} %pad_maximum_fusion.1, s32[1024]{0:T(1024)S(1)} %pad_clamp_fusion.4), kind=kCustom, calls=%fused_computation.clone | custom fusion | bytes 6553616 | tf_op jit(solution)/shard_map/jit(_take)/gather | solution.py:89
  113.8 10.7 %collective-permute-done.14 = bf16[128,3200]{1,0:T(8,128)(2,1)} collective-permute-done((bf16[128,3200]{1,0:T(8,128)(2,1)}, bf16[128,3200]{1,0:T(8,128)(2,1)}, u32[]{:S(2)}, u32[]{:S(2)}) %collective-permute-start.14) | collective-permute-done | bytes 819232 | tf_op jit(solution)/shard_map/ppermute | solution.py:29
  124.5 12.0 %collective-permute-done.15 = bf16[128,3200]{1,0:T(8,128)(2,1)} collective-permute-done((bf16[128,3200]{1,0:T(8,128)(2,1)}, bf16[128,3200]{1,0:T(8,128)(2,1)}, u32[]{:S(2)}, u32[]{:S(2)}) %collective-permute-start.15) | collective-permute-done | bytes 819232 | tf_op jit(solution)/shard_map/ppermute | solution.py:29
  136.5 3.3 %pad_maximum_fusion.2 = bf16[4,128,3200]{2,1,0:T(8,128)(2,1)} fusion(bf16[1,128,3200]{2,1,0:T(8,128)(2,1)} %bitcast.30, bf16[1,128,3200]{2,1,0:T(8,128)(2,1)} %bitcast.29, bf16[1,128,3200]{2,1,0:T(8,128)(2,1)} %maximum_bitcast_fusion, bf16[1,128,3200]{2,1,0:T(8,128)(2,1)} %bitcast.27), kind=kLoop, calls=%fused_computation.9 | loop fusion | flops 4915200 | bytes 6553600 | tf_op jit(solution)/shard_map/stack | solution.py:90
  139.8 4.5 %gather_fusion.5 = bf16[4,128,3200]{2,1,0:T(8,128)(2,1)} fusion(bf16[4,128,3200]{2,1,0:T(8,128)(2,1)} %pad_maximum_fusion.2, s32[1024]{0:T(1024)S(1)} %pad_clamp_fusion.4), kind=kCustom, calls=%fused_computation.1.clone | custom fusion | bytes 6553616 | tf_op jit(solution)/shard_map/jit(_take)/gather | solution.py:90
  144.3 5.3 %broadcast_select_fusion.1 = (bf16[4,128,3200]{2,1,0:T(8,128)(2,1)}, bf16[4,128,3200]{2,1,0:T(8,128)(2,1)}) fusion(bf16[4,128,3200]{2,1,0:T(8,128)(2,1)} %gather_fusion.5, pred[4]{0:T(512)(128)(4,1)} %get-tuple-element.19, bf16[4,128,3200]{2,1,0:T(8,128)(2,1)S(1)} %gather_fusion.4), kind=kLoop, calls=%fused_computation.10 | loop fusion | flops 3276800 | bytes 13107204 | tf_op jit(solution)/shard_map/jit(_take)/select_n | solution.py:90
  149.6 4.9 %pad_maximum_fusion = bf16[8,384,768]{2,1,0:T(8,128)(2,1)} fusion(bf16[8,384,384]{2,1,0:T(8,128)(2,1)} %collective-permute-done.10, bf16[8,384,384]{2,1,0:T(8,128)(2,1)} %bitcast_dynamic-update-slice_fusion), kind=kLoop, calls=%fused_computation.6 | loop fusion | flops 9437184 | bytes 9437184 | tf_op jit(solution)/shard_map/concatenate | solution.py:65
  154.5 5.4 %gather_fusion = bf16[8,384,768]{2,1,0:T(8,128)(2,1)} fusion(bf16[8,384,768]{2,1,0:T(8,128)(2,1)} %pad_maximum_fusion, s32[1024]{0:T(1024)S(1)} %pad_clamp_fusion.3), kind=kCustom, calls=%fused_computation.2 | custom fusion | bytes 9437216 | tf_op jit(solution)/shard_map/jit(_take)/gather | solution.py:66
  159.9 2.9 %broadcast_select_fusion = bf16[8,384,768]{2,1,0:T(8,128)(2,1)S(1)} fusion(bf16[8,384,768]{2,1,0:T(8,128)(2,1)} %gather_fusion, pred[8]{0:T(512)(128)(4,1)S(1)} %copy-done.9), kind=kLoop, calls=%fused_computation.7 | loop fusion | flops 2359296 | bytes 9437192 | tf_op jit(solution)/shard_map/jit(_take)/select_n | solution.py:66
  173.9 1.6 collective-permute-start.17
  176.6 2.7 %collective-permute-done.17 = bf16[64,1280]{1,0:T(8,128)(2,1)S(1)} collective-permute-done((bf16[64,1280]{1,0:T(8,128)(2,1)S(1)}, bf16[64,1280]{1,0:T(8,128)(2,1)S(1)}, u32[]{:S(2)}, u32[]{:S(2)}) %collective-permute-start.17) | collective-permute-done | bytes 163872 | tf_op jit(solution)/shard_map/ppermute | solution.py:29
  184.4 2.4 %collective-permute-done.19 = bf16[64,512]{1,0:T(8,128)(2,1)S(1)} collective-permute-done((bf16[64,512]{1,0:T(8,128)(2,1)S(1)}, bf16[64,512]{1,0:T(8,128)(2,1)S(1)}, u32[]{:S(2)}, u32[]{:S(2)}) %collective-permute-start.19) | collective-permute-done | bytes 65568 | tf_op jit(solution)/shard_map/ppermute | solution.py:29
  187.4 2.6 %collective-permute-start.21 = (bf16[1536,64]{0,1:T(8,128)(2,1)S(1)}, bf16[1536,64]{0,1:T(8,128)(2,1)S(1)}, u32[]{:S(2)}, u32[]{:S(2)}) collective-permute-start(bf16[1536,64]{0,1:T(8,128)(2,1)S(1)} %convolution_convert_fusion), channel_id=1, source_target_pairs={{0,16},{4,20},{8,24},{12,28},{16,0},{20,4},{24,8},{28,12},{1,17},{... | collective-permute-start | bytes 589832 | tf_op jit(solution)/shard_map/ppermute | solution.py:29
  190.0 4.2 %collective-permute-done.22 = bf16[2,64,768]{2,1,0:T(8,128)(2,1)S(1)} collective-permute-done((bf16[2,64,768]{2,1,0:T(8,128)(2,1)S(1)}, bf16[2,64,768]{2,1,0:T(8,128)(2,1)S(1)}, u32[]{:S(2)}, u32[]{:S(2)}) %collective-permute-start.22) | collective-permute-done | bytes 196640 | tf_op jit(solution)/shard_map/ppermute | solution.py:29
  194.4 2.8 %collective-permute-start.24 = (bf16[2,64,768]{2,1,0:T(8,128)(2,1)S(1)}, bf16[2,64,768]{2,1,0:T(8,128)(2,1)S(1)}, u32[]{:S(2)}, u32[]{:S(2)}) collective-permute-start(bf16[2,64,768]{2,1,0:T(8,128)(2,1)S(1)} %add_convert_fusion), channel_id=1, source_target_pairs={{0,4},{4,0},{8,12},{12,8},{16,20},{20,16},{24,28},{28,24},{1,5},{5... | collective-permute-start | bytes 589832 | tf_op jit(solution)/shard_map/ppermute | solution.py:29
  200.2 2.6 %collective-permute-done.24 = bf16[2,64,768]{2,1,0:T(8,128)(2,1)S(1)} collective-permute-done((bf16[2,64,768]{2,1,0:T(8,128)(2,1)S(1)}, bf16[2,64,768]{2,1,0:T(8,128)(2,1)S(1)}, u32[]{:S(2)}, u32[]{:S(2)}) %collective-permute-start.24) | collective-permute-done | bytes 196640 | tf_op jit(solution)/shard_map/ppermute | solution.py:29
  202.9 2.5 %collective-permute-done.25 = bf16[2,64,768]{2,1,0:T(8,128)(2,1)S(1)} collective-permute-done((bf16[2,64,768]{2,1,0:T(8,128)(2,1)S(1)}, bf16[2,64,768]{2,1,0:T(8,128)(2,1)S(1)}, u32[]{:S(2)}, u32[]{:S(2)}) %collective-permute-start.25) | collective-permute-done | bytes 196640 | tf_op jit(solution)/shard_map/ppermute | solution.py:29
  209.1 1.8 reshape.169
  (114 shorter events, 51.2 us)
Async XLA Ops:
  0.6 3.7 %copy-start = (bf16[1,1536,64]{1,2,0:T(8,128)(2,1)S(1)}, bf16[1,1536,64]{1,2,0:T(8,128)(2,1)}, u32[]{:S(2)}) copy-start(bf16[1,1536,64]{1,2,0:T(8,128)(2,1)} %param.14) | copy-start | bytes 589828
  1.8 4.8 %copy-start.6 = (bf16[1,144,1536]{2,1,0:T(8,128)(2,1)S(1)}, bf16[1,144,1536]{2,1,0:T(8,128)(2,1)}, u32[]{:S(2)}) copy-start(bf16[1,144,1536]{2,1,0:T(8,128)(2,1)} %param.17) | copy-start | bytes 1327108
  4.4 8.8 %copy-start.4 = (bf16[192,1536]{1,0:T(8,128)(2,1)S(1)}, bf16[192,1536]{1,0:T(8,128)(2,1)}, u32[]{:S(2)}) copy-start(bf16[192,1536]{1,0:T(8,128)(2,1)} %param.12) | copy-start | bytes 1769476
  4.4 8.8 %copy-start.5 = (bf16[1536,192]{0,1:T(8,128)(2,1)S(1)}, bf16[1536,192]{0,1:T(8,128)(2,1)}, u32[]{:S(2)}) copy-start(bf16[1536,192]{0,1:T(8,128)(2,1)} %param.13) | copy-start | bytes 1769476
  7.1 41.6 %collective-permute-start = (bf16[128,3200]{1,0:T(8,128)(2,1)S(1)}, bf16[128,3200]{1,0:T(8,128)(2,1)S(1)}, u32[]{:S(2)}, u32[]{:S(2)}) collective-permute-start(bf16[128,3200]{1,0:T(8,128)(2,1)S(1)} %concatenate.22), channel_id=1, source_target_pairs={{0,4},{4,0},{8,12},{12,8},{16,20},{20,16},{24,28},{28,24},{1,5},{5... | collective-permute-start | bytes 2457608 | tf_op jit(solution)/shard_map/ppermute | solution.py:29
  10.1 38.6 %collective-permute-start.11 = (bf16[128,3200]{1,0:T(8,128)(2,1)S(1)}, bf16[128,3200]{1,0:T(8,128)(2,1)}, u32[]{:S(2)}, u32[]{:S(2)}) collective-permute-start(bf16[128,3200]{1,0:T(8,128)(2,1)S(1)} %concatenate.22), channel_id=1, source_target_pairs={{0,2},{1,3},{2,0},{3,1},{4,6},{5,7},{6,4},{7,5},{8,10},{9,11},{10,... | collective-permute-start | bytes 2457608 | tf_op jit(solution)/shard_map/ppermute | solution.py:29
  11.6 69.1 %collective-permute-start.1 = (bf16[128,3200]{1,0:T(8,128)(2,1)S(1)}, bf16[128,3200]{1,0:T(8,128)(2,1)}, u32[]{:S(2)}, u32[]{:S(2)}) collective-permute-start(bf16[128,3200]{1,0:T(8,128)(2,1)S(1)} %concatenate.22), channel_id=1, source_target_pairs={{0,8},{4,12},{8,0},{12,4},{16,24},{20,28},{24,16},{28,20},{1,9},{5... | collective-permute-start | bytes 2457608 | tf_op jit(solution)/shard_map/ppermute | solution.py:29
  14.9 26.2 %collective-permute-start.3 = (bf16[2,384,384]{2,1,0:T(8,128)(2,1)}, bf16[2,384,384]{2,1,0:T(8,128)(2,1)}, u32[]{:S(2)}, u32[]{:S(2)}) collective-permute-start(bf16[2,384,384]{2,1,0:T(8,128)(2,1)} %pad_maximum_fusion.4), channel_id=1, source_target_pairs={{0,4},{4,0},{8,12},{12,8},{16,20},{20,16},{24,28},{28,24},{1,5},{5... | collective-permute-start | bytes 1769480 | tf_op jit(solution)/shard_map/ppermute | solution.py:29
  15.4 29.9 %collective-permute-start.4 = (bf16[384,384]{1,0:T(8,128)(2,1)}, bf16[384,384]{1,0:T(8,128)(2,1)S(1)}, u32[]{:S(2)}, u32[]{:S(2)}) collective-permute-start(bf16[384,384]{1,0:T(8,128)(2,1)} %get-tuple-element.7), channel_id=1, source_target_pairs={{0,8},{4,12},{8,0},{12,4},{16,24},{20,28},{24,16},{28,20},{1,9},{5... | collective-permute-start | bytes 884744 | tf_op jit(solution)/shard_map/ppermute | solution.py:29
  42.9 13.0 %collective-permute-start.5 = (bf16[384,384]{1,0:T(8,128)(2,1)S(1)}, bf16[384,384]{1,0:T(8,128)(2,1)S(1)}, u32[]{:S(2)}, u32[]{:S(2)}) collective-permute-start(bf16[384,384]{1,0:T(8,128)(2,1)S(1)} %get-tuple-element.16), channel_id=1, source_target_pairs={{0,8},{4,12},{8,0},{12,4},{16,24},{20,28},{24,16},{28,20},{1,9},{5... | collective-permute-start | bytes 884744 | tf_op jit(solution)/shard_map/ppermute | solution.py:29
  45.3 33.0 %collective-permute-start.6 = (bf16[384,384]{1,0:T(8,128)(2,1)S(1)}, bf16[384,384]{1,0:T(8,128)(2,1)S(1)}, u32[]{:S(2)}, u32[]{:S(2)}) collective-permute-start(bf16[384,384]{1,0:T(8,128)(2,1)S(1)} %get-tuple-element.4), channel_id=1, source_target_pairs={{0,16},{4,20},{8,24},{12,28},{16,0},{20,4},{24,8},{28,12},{1,17},{... | collective-permute-start | bytes 884744 | tf_op jit(solution)/shard_map/ppermute | solution.py:29
  48.7 47.7 %collective-permute-start.8 = (bf16[384,384]{1,0:T(8,128)(2,1)}, bf16[384,384]{1,0:T(8,128)(2,1)S(1)}, u32[]{:S(2)}, u32[]{:S(2)}) collective-permute-start(bf16[384,384]{1,0:T(8,128)(2,1)} %get-tuple-element.7), channel_id=1, source_target_pairs={{0,24},{4,28},{8,16},{12,20},{16,8},{20,12},{24,0},{28,4},{1,25},{... | collective-permute-start | bytes 884744 | tf_op jit(solution)/shard_map/ppermute | solution.py:29
  48.7 122.1 %collective-permute-start.16 = (bf16[64,768]{1,0:T(8,128)(2,1)S(1)}, bf16[64,768]{1,0:T(8,128)(2,1)S(1)}, u32[]{:S(2)}, u32[]{:S(2)}) collective-permute-start(bf16[64,768]{1,0:T(8,128)(2,1)S(1)} %pad_maximum_fusion.8), channel_id=1, source_target_pairs={{0,2},{1,3},{2,0},{3,1},{4,6},{5,7},{6,4},{7,5},{8,10},{9,11},{10,... | collective-permute-start | bytes 294920 | tf_op jit(solution)/shard_map/ppermute | solution.py:29
  55.9 38.2 %collective-permute-start.7 = (bf16[384,384]{1,0:T(8,128)(2,1)S(1)}, bf16[384,384]{1,0:T(8,128)(2,1)S(1)}, u32[]{:S(2)}, u32[]{:S(2)}) collective-permute-start(bf16[384,384]{1,0:T(8,128)(2,1)S(1)} %get-tuple-element.14), channel_id=1, source_target_pairs={{0,16},{4,20},{8,24},{12,28},{16,0},{20,4},{24,8},{28,12},{1,17},{... | collective-permute-start | bytes 884744 | tf_op jit(solution)/shard_map/ppermute | solution.py:29
  78.3 20.3 %collective-permute-start.9 = (bf16[384,384]{1,0:T(8,128)(2,1)S(1)}, bf16[384,384]{1,0:T(8,128)(2,1)S(1)}, u32[]{:S(2)}, u32[]{:S(2)}) collective-permute-start(bf16[384,384]{1,0:T(8,128)(2,1)S(1)} %get-tuple-element.16), channel_id=1, source_target_pairs={{0,24},{4,28},{8,16},{12,20},{16,8},{20,12},{24,0},{28,4},{1,25},{... | collective-permute-start | bytes 884744 | tf_op jit(solution)/shard_map/ppermute | solution.py:29
  80.7 23.4 %collective-permute-start.2 = (bf16[128,3200]{1,0:T(8,128)(2,1)}, bf16[128,3200]{1,0:T(8,128)(2,1)}, u32[]{:S(2)}, u32[]{:S(2)}) collective-permute-start(bf16[128,3200]{1,0:T(8,128)(2,1)} %collective-permute-done.1), channel_id=1, source_target_pairs={{0,4},{4,0},{8,12},{12,8},{16,20},{20,16},{24,28},{28,24},{1,5},{5... | collective-permute-start | bytes 2457608 | tf_op jit(solution)/shard_map/ppermute | solution.py:29
  94.1 12.8 %collective-permute-start.13 = (bf16[128,1664]{1,0:T(8,128)(2,1)S(1)}, bf16[128,1664]{1,0:T(8,128)(2,1)S(1)}, u32[]{:S(2)}, u32[]{:S(2)}) collective-permute-start(bf16[128,1664]{1,0:T(8,128)(2,1)S(1)} %slice.87), channel_id=1, source_target_pairs={{0,2},{1,3},{2,0},{3,1},{4,6},{5,7},{6,4},{7,5},{8,10},{9,11},{10,... | collective-permute-start | bytes 1277960 | tf_op jit(solution)/shard_map/ppermute | solution.py:29
  96.4 7.8 %collective-permute-start.12 = (bf16[128,1536]{1,0:T(8,128)(2,1)S(1)}, bf16[128,1536]{1,0:T(8,128)(2,1)S(1)}, u32[]{:S(2)}, u32[]{:S(2)}) collective-permute-start(bf16[128,1536]{1,0:T(8,128)(2,1)S(1)} %slice.86), channel_id=1, source_target_pairs={{0,4},{4,0},{8,12},{12,8},{16,20},{20,16},{24,28},{28,24},{1,5},{5... | collective-permute-start | bytes 1179656 | tf_op jit(solution)/shard_map/ppermute | solution.py:29
  98.6 25.9 %collective-permute-start.14 = (bf16[128,3200]{1,0:T(8,128)(2,1)}, bf16[128,3200]{1,0:T(8,128)(2,1)}, u32[]{:S(2)}, u32[]{:S(2)}) collective-permute-start(bf16[128,3200]{1,0:T(8,128)(2,1)} %collective-permute-done.1), channel_id=1, source_target_pairs={{0,2},{1,3},{2,0},{3,1},{4,6},{5,7},{6,4},{7,5},{8,10},{9,11},{10,... | collective-permute-start | bytes 2457608 | tf_op jit(solution)/shard_map/ppermute | solution.py:29
  104.1 45.5 %collective-permute-start.10 = (bf16[8,384,384]{2,1,0:T(8,128)(2,1)}, bf16[8,384,384]{2,1,0:T(8,128)(2,1)}, u32[]{:S(2)}, u32[]{:S(2)}) collective-permute-start(bf16[8,384,384]{2,1,0:T(8,128)(2,1)} %bitcast_dynamic-update-slice_fusion), channel_id=1, source_target_pairs={{0,1},{1,0},{2,3},{3,2},{4,5},{5,4},{6,7},{7,6},{8,9},{9,8},{10,11... | collective-permute-start | bytes 7077896 | tf_op jit(solution)/shard_map/ppermute | solution.py:29
  104.1 32.4 %collective-permute-start.15 = (bf16[128,3200]{1,0:T(8,128)(2,1)}, bf16[128,3200]{1,0:T(8,128)(2,1)}, u32[]{:S(2)}, u32[]{:S(2)}) collective-permute-start(bf16[128,3200]{1,0:T(8,128)(2,1)} %collective-permute-done.2), channel_id=1, source_target_pairs={{0,2},{1,3},{2,0},{3,1},{4,6},{5,7},{6,4},{7,5},{8,10},{9,11},{10,... | collective-permute-start | bytes 2457608 | tf_op jit(solution)/shard_map/ppermute | solution.py:29
  154.5 5.4 %copy-start.9 = (pred[8]{0:T(512)(128)(4,1)S(1)}, pred[8]{0:T(512)(128)(4,1)}, u32[]{:S(2)}) copy-start(pred[8]{0:T(512)(128)(4,1)} %compare_and_fusion.4) | copy-start | bytes 28
  170.8 4.7 %copy-start.7 = (bf16[64,384]{1,0:T(8,128)(2,1)S(1)}, bf16[64,384]{1,0:T(8,128)(2,1)}, u32[]{:S(2)}) copy-start(bf16[64,384]{1,0:T(8,128)(2,1)} %get-tuple-element.11) | copy-start | bytes 147460
  173.9 5.4 %collective-permute-start.17 = (bf16[64,1280]{1,0:T(8,128)(2,1)S(1)}, bf16[64,1280]{1,0:T(8,128)(2,1)S(1)}, u32[]{:S(2)}, u32[]{:S(2)}) collective-permute-start(bf16[64,1280]{1,0:T(8,128)(2,1)S(1)} %pad_maximum_fusion.6), channel_id=1, source_target_pairs={{0,2},{1,3},{2,0},{3,1},{4,6},{5,7},{6,4},{7,5},{8,10},{9,11},{10,... | collective-permute-start | bytes 491528 | tf_op jit(solution)/shard_map/ppermute | solution.py:29
  179.7 4.7 %collective-permute-start.18 = (bf16[64,512]{1,0:T(8,128)(2,1)S(1)}, bf16[64,512]{1,0:T(8,128)(2,1)S(1)}, u32[]{:S(2)}, u32[]{:S(2)}) collective-permute-start(bf16[64,512]{1,0:T(8,128)(2,1)S(1)} %add_convert_fusion.2), channel_id=1, source_target_pairs={{0,4},{4,0},{8,12},{12,8},{16,20},{20,16},{24,28},{28,24},{1,5},{5... | collective-permute-start | bytes 196616 | tf_op jit(solution)/shard_map/ppermute | solution.py:29
  181.2 5.5 %collective-permute-start.19 = (bf16[64,512]{1,0:T(8,128)(2,1)S(1)}, bf16[64,512]{1,0:T(8,128)(2,1)S(1)}, u32[]{:S(2)}, u32[]{:S(2)}) collective-permute-start(bf16[64,512]{1,0:T(8,128)(2,1)S(1)} %add_convert_fusion.2), channel_id=1, source_target_pairs={{0,8},{4,12},{8,0},{12,4},{16,24},{20,28},{24,16},{28,20},{1,9},{5... | collective-permute-start | bytes 196616 | tf_op jit(solution)/shard_map/ppermute | solution.py:29
  181.8 5.2 %collective-permute-start.20 = (bf16[64,512]{1,0:T(8,128)(2,1)S(1)}, bf16[64,512]{1,0:T(8,128)(2,1)S(1)}, u32[]{:S(2)}, u32[]{:S(2)}) collective-permute-start(bf16[64,512]{1,0:T(8,128)(2,1)S(1)} %add_convert_fusion.2), channel_id=1, source_target_pairs={{0,12},{4,8},{8,4},{12,0},{16,28},{20,24},{24,20},{28,16},{1,13},{... | collective-permute-start | bytes 196616 | tf_op jit(solution)/shard_map/ppermute | solution.py:29
  183.2 11.0 %collective-permute-start.22 = (bf16[2,64,768]{2,1,0:T(8,128)(2,1)S(1)}, bf16[2,64,768]{2,1,0:T(8,128)(2,1)S(1)}, u32[]{:S(2)}, u32[]{:S(2)}) collective-permute-start(bf16[2,64,768]{2,1,0:T(8,128)(2,1)S(1)} %pad_maximum_fusion.5), channel_id=1, source_target_pairs={{0,16},{4,20},{8,24},{12,28},{16,0},{20,4},{24,8},{28,12},{1,17},{... | collective-permute-start | bytes 589832 | tf_op jit(solution)/shard_map/ppermute | solution.py:29
  187.4 11.3 %collective-permute-start.21 = (bf16[1536,64]{0,1:T(8,128)(2,1)S(1)}, bf16[1536,64]{0,1:T(8,128)(2,1)S(1)}, u32[]{:S(2)}, u32[]{:S(2)}) collective-permute-start(bf16[1536,64]{0,1:T(8,128)(2,1)S(1)} %convolution_convert_fusion), channel_id=1, source_target_pairs={{0,16},{4,20},{8,24},{12,28},{16,0},{20,4},{24,8},{28,12},{1,17},{... | collective-permute-start | bytes 589832 | tf_op jit(solution)/shard_map/ppermute | solution.py:29
  194.3 5.9 %collective-permute-start.23 = (bf16[2,64,768]{2,1,0:T(8,128)(2,1)S(1)}, bf16[2,64,768]{2,1,0:T(8,128)(2,1)S(1)}, u32[]{:S(2)}, u32[]{:S(2)}) collective-permute-start(bf16[2,64,768]{2,1,0:T(8,128)(2,1)S(1)} %add_convert_fusion), channel_id=1, source_target_pairs={{0,8},{4,12},{8,0},{12,4},{16,24},{20,28},{24,16},{28,20},{1,9},{5... | collective-permute-start | bytes 589832 | tf_op jit(solution)/shard_map/ppermute | solution.py:29
  194.4 8.5 %collective-permute-start.24 = (bf16[2,64,768]{2,1,0:T(8,128)(2,1)S(1)}, bf16[2,64,768]{2,1,0:T(8,128)(2,1)S(1)}, u32[]{:S(2)}, u32[]{:S(2)}) collective-permute-start(bf16[2,64,768]{2,1,0:T(8,128)(2,1)S(1)} %add_convert_fusion), channel_id=1, source_target_pairs={{0,4},{4,0},{8,12},{12,8},{16,20},{20,16},{24,28},{28,24},{1,5},{5... | collective-permute-start | bytes 589832 | tf_op jit(solution)/shard_map/ppermute | solution.py:29
  197.2 8.1 %collective-permute-start.25 = (bf16[2,64,768]{2,1,0:T(8,128)(2,1)S(1)}, bf16[2,64,768]{2,1,0:T(8,128)(2,1)S(1)}, u32[]{:S(2)}, u32[]{:S(2)}) collective-permute-start(bf16[2,64,768]{2,1,0:T(8,128)(2,1)S(1)} %add_convert_fusion), channel_id=1, source_target_pairs={{0,12},{4,8},{8,4},{12,0},{16,28},{20,24},{24,20},{28,16},{1,13},{... | collective-permute-start | bytes 589832 | tf_op jit(solution)/shard_map/ppermute | solution.py:29
  (4 other events, 7.4 us)

commit v2 on v1

v2 whole, which is shorter than its diff:
```python
import jax
import jax.numpy as jnp
from jax import lax
from jax.experimental import pallas as pl
from jax.experimental.pallas import tpu as pltpu
from jax.sharding import PartitionSpec as P

BUCKET = 144
LMAX = 126
BF = jnp.bfloat16
F32 = jnp.float32


def normalize(frames, gain):
    values = frames.astype(F32)
    mean = jnp.mean(values, axis=1, keepdims=True)
    var = jnp.mean((values - mean) ** 2, axis=1, keepdims=True)
    return (gain * (values - mean) / jnp.sqrt(var + 1e-05)).astype(BF)


def swish_gradient(pre, dhid):
    sigma = jax.nn.sigmoid(pre)
    return (dhid * sigma * (1.0 + pre * (1.0 - sigma))).astype(BF)


def dot(a, b, dims=((1,), (0,))):
    return lax.dot_general(a, b, (dims, ((), ())), preferred_element_type=F32)


def flip(axis, size, bits):
    return lambda value: lax.ppermute(value, axis, [(i, i ^ bits) for i in range(size)])


def whole(shape):
    return pl.BlockSpec(shape, lambda: (0,) * len(shape))


def place():
    f, m = lax.axis_index("fsdp"), lax.axis_index("member")
    return f, (f >> 1) & 1, f & 1, m >> 1, m & 1


def lanes(start, size):
    return pl.ds(pl.multiple_of(start, 128), size)


def call(body, ins, outs, args, scratch=(), flops=0):
    size = sum(a.size * a.dtype.itemsize for a in args)
    return pl.pallas_call(
        body,
        in_specs=ins,
        out_specs=[whole(o.shape) for o in outs],
        out_shape=outs,
        scratch_shapes=list(scratch),
        compiler_params=pltpu.CompilerParams(vmem_limit_bytes=40 * 1024 * 1024),
        cost_estimate=pl.CostEstimate(flops=flops, bytes_accessed=size, transcendentals=0),
    )(*args)


def cut_weights(first, second):
    depth, block = first.shape
    part = block // 4
    piece = jax.ShapeDtypeStruct((2 * depth, part), BF)
    pair = jax.ShapeDtypeStruct((2, 2 * depth, part), BF)

    def body(first_ref, second_ref, away_ref, same_ref, flip_ref):
        _, low_bit, x, _, _ = place()
        for dx in (1, 0):
            for dl in (0, 1):
                start = ((x ^ dx) * 2 + (low_bit ^ dl)) * part
                out = away_ref.at[dl] if dx else (same_ref, flip_ref)[dl]
                out[:depth] = first_ref[:, lanes(start, part)]
                out[depth:] = second_ref[lanes(start, part), :].T

    return call(body, [whole(first.shape), whole(second.shape)], [pair, piece, piece], (first, second))


def pack_frames(frames, gain, down_map, up_map, lengths, cotangent, rows, part):
    width, rank = frames.shape[2], down_map.shape[2]
    fold = rank // 16
    lined = 2 * width + 2 * rank

    def body(frames_ref, gain_ref, down_ref, up_ref, lengths_ref, cot_ref, own_ref, cross_ref):
        _, low_bit, x, y, core = place()
        normed = normalize(frames_ref[0, :rows], gain_ref[...])
        keep = lax.broadcasted_iota(jnp.int32, (rows, width), 0) < lengths_ref[0, 0]
        masked = jnp.where(keep, cot_ref[0, :rows].astype(F32), 0.0).astype(BF)
        low = dot(normed, down_ref[0])
        low = jnp.concatenate([low, jnp.zeros_like(low)], axis=1).astype(BF)
        for ref in (own_ref, cross_ref):
            ref[:rows, :width] = normed
            ref[:rows, width : 2 * width] = masked
            ref[:rows, 2 * width :] = low
        for dc in range(2):
            start = ((1 - y) * 2 + (core ^ dc)) * (4 * part) + (x * 2 + low_bit) * part
            columns = up_ref[0, :, lanes(start, part)]
            for i in range(fold):
                at = (2 * i + dc) * part
                cross_ref[rows:, at : at + part] = columns[16 * i : 16 * (i + 1)]
        cross_ref[rows:, 2 * fold * part :] = jnp.zeros((16, lined - 2 * fold * part), BF)

    args = (frames, gain[None], down_map, up_map, lengths, cotangent)
    ins = [whole(a.shape) for a in args]
    ins[4] = pl.BlockSpec(memory_space=pltpu.SMEM)
    outs = [jax.ShapeDtypeStruct((n, lined), BF) for n in (rows, rows + 16)]
    return call(body, ins, outs, args, flops=2 * rows * width * rank)


def work(pieces, swapped, frames, up, width, rank, own):
    depth, part = pieces[0].shape[0] // 2, pieces[0].shape[1]
    rows = frames[1].shape[0]
    lined = frames[1].shape[1]
    codes = (0, 1, 2, 4, 6, 3, 5, 7)
    n_pieces, n_swapped = len(pieces), len(swapped)
    hidden = 2 * part
    count = 4 * rows
    kind = F32 if own else BF

    def body(*refs):
        piece_refs, refs = refs[:n_pieces], refs[n_pieces:]
        swap_refs, refs = refs[:n_swapped], refs[n_swapped:]
        frame_refs, refs = refs[:4], refs[4:]
        (up_ref, out_ref, w_in, w_out, packed, map_ref, sems, frame_sems), = (refs,)
        f, low_bit, x, y, core = place()
        slot = low_bit * 2 + x
        copies = []
        loads = []
        for i, ref in enumerate(frame_refs):
            at = pl.multiple_of((slot ^ i) * rows, 16)
            loads.append(
                pltpu.make_async_copy(ref.at[pl.ds(0, rows)], packed.at[pl.ds(at, rows)], frame_sems.at[i])
            )
        flat = [r.at[j] if len(r.shape) == 3 else r for r in swap_refs for j in range(r.shape[0] if len(r.shape) == 3 else 1)]
        for side, group in enumerate((piece_refs, flat)):
            for i, ref in enumerate(group):
                at = pl.multiple_of((f ^ codes[i]) * depth, 16)
                for k, w in enumerate((w_in, w_out)):
                    copies.append(
                        pltpu.make_async_copy(
                            ref.at[pl.ds(k * depth, depth)],
                            w.at[pl.ds(at, depth), pl.ds(side * part, part)],
                            sems.at[len(copies)],
                        )
                    )
        for copy in loads + copies:
            copy.start()
        if own:
            for dc in range(2):
                start = (y * 2 + (core ^ dc)) * (4 * part) + (x * 2 + low_bit) * part
                map_ref[:, dc * part : (dc + 1) * part] = up_ref[0, :, lanes(start, part)]
        else:
            for i in range(rank // 16):
                map_ref[16 * i : 16 * (i + 1), :] = up_ref[rows:, i * hidden : (i + 1) * hidden]
        for copy in loads + copies:
            copy.wait()
        step = 256 if hidden % 256 == 0 else part
        back = jnp.zeros((rank, count), F32)
        low = packed[:, 2 * width :][:, :rank]
        for at in range(0, hidden, step):
            now = slice(at, at + step)
            pre = dot(packed[:, :width], w_in[:, now]) + dot(low, map_ref[:, now])
            dhid = 0.5 * dot(packed[:, width : 2 * width], w_out[:, now])
            dpre = swish_gradient(pre, dhid)
            out_ref[:, now] = dot(low, dpre, ((0,), (0,))).astype(kind)
            back = back + dot(map_ref[:, now], dpre, ((1,), (1,)))
        out_ref[:, hidden:] = back.astype(kind)

    args = (*pieces, *swapped, *frames, up)
    anywhere = pl.BlockSpec(memory_space=pl.ANY)
    ins = [anywhere] * (len(args) - 1) + [whole(up.shape)]
    scratch = [
        pltpu.VMEM((8 * depth, hidden), BF),
        pltpu.VMEM((8 * depth, hidden), BF),
        pltpu.VMEM((count, lined), BF),
        pltpu.VMEM((rank, hidden), BF),
        pltpu.SemaphoreType.DMA((32,)),
        pltpu.SemaphoreType.DMA((4,)),
    ]
    outs = [jax.ShapeDtypeStruct((rank, hidden + count), kind)]
    return call(body, ins, outs, args, scratch, flops=4 * count * 8 * depth * hidden)[0]


def spread(parts, down, down_other, block):
    _, rank, hidden = parts[0].shape
    part = hidden // 2

    def body(*refs):
        part_refs, (down_ref, other_ref, up_out, down_out) = refs[:4], refs[4:]
        _, low_bit, x, y, core = place()
        slot = x * 2 + low_bit
        for i, ref in enumerate(part_refs):
            for dy in range(2):
                for dc in range(2):
                    start = ((y ^ dy) * 2 + (core ^ dc)) * block + (slot ^ i) * part
                    up_out[0, :, lanes(start, part)] = ref[dy, :, dc * part : (dc + 1) * part].astype(F32)
        down_out[0] = down_ref[...].astype(F32) + other_ref[...].astype(F32)

    args = (*parts, down, down_other)
    outs = [
        jax.ShapeDtypeStruct((1, rank, 4 * block), F32),
        jax.ShapeDtypeStruct((1, *down.shape), F32),
    ]
    return call(body, [whole(a.shape) for a in args], outs, args)


def after(value, *done):
    return lax.optimization_barrier((value, *done))[0]


def paired_halves(frames, gain, first, second, down_map, up_map, lengths, cotangent):
    over_x, over_low = flip("fsdp", 8, 1), flip("fsdp", 8, 2)
    over_half, over_both = flip("fsdp", 8, 4), flip("fsdp", 8, 6)
    over_xlow = flip("fsdp", 8, 3)
    over_y, over_core = flip("member", 4, 2), flip("member", 4, 1)

    width, rank = frames.shape[2], down_map.shape[2]
    rows = -(-LMAX // 16) * 16
    block = first.shape[1]
    part = block // 4
    hidden = 2 * part

    away, w00, w01 = cut_weights(first, second)
    wx = over_x(away)
    z2n = over_half(w00)
    own, cross = pack_frames(frames, gain, down_map, up_map, lengths, cotangent, rows, part)
    fy = over_y(cross)
    fz = over_low(own)
    fx = over_x(after(own, wx))
    z3n = over_both(after(w01, z2n))
    z1n = over_low(after(w01, fz))
    wx0, wx1 = wx[0], wx[1]
    z1f = over_low(after(wx1, z1n))
    fzy = over_y(after(fz, fy))
    z2f = over_half(after(wx0, z3n))
    group1 = over_core(jnp.stack([w00, wx0, z1n, z2n]))
    fzx = over_x(after(fz, fx))
    fxy = over_y(after(fx, fzy))
    z3f = over_both(after(wx1, z2f))
    group2 = over_core(jnp.stack([z3n, z1f, z2f]))
    cut = rows * 5 // 8 // 16 * 16
    fzxy_a = over_x(after(fzy[:cut], fzx))
    fzxy_b = over_y(after(fzx[cut:], fxy))
    group3 = over_core(after(z3f, group2))
    pieces = [w00, wx0, z1n, z2n, z3n, z1f, z2f, z3f]
    swapped = [group1, group2, group3]

    mine = work(pieces, swapped, [own, fx, fz, fzx], up_map, width, rank, True)
    fzxy = jnp.concatenate([fzxy_a, fzxy_b], axis=0)
    theirs = work(pieces, swapped, [fy, fxy, fzy, fzxy], fy, width, rank, False)

    got = over_y(theirs)
    back = (mine[:, hidden:] + got[:, hidden:].astype(F32)).astype(BF)
    bx, bz, bzx = over_x(back), over_low(back), over_xlow(back)
    up_pair = jnp.stack([mine[:, :hidden].astype(BF), got[:, :hidden]])
    up_half = over_half(up_pair)
    up_sum = (up_pair.astype(F32) + up_half.astype(F32)).astype(BF)
    back_sum = (
        (back.astype(F32) + bx.astype(F32)) + (bz.astype(F32) + bzx.astype(F32))
    ).astype(BF)
    slots = (lax.axis_index("fsdp") & 3) ^ jnp.arange(4)
    normed = jnp.take(jnp.stack([v[:, :width] for v in (own, fx, fz, fzx)]), slots, axis=0)
    down = dot(normed.reshape(4 * rows, width), back_sum, ((0,), (1,))).astype(BF)
    down_other = over_half(down)
    ux, uz, uzx = over_x(up_sum), over_low(up_sum), over_xlow(up_sum)
    up_gradient, down_gradient = spread([up_sum, uz, ux, uzx], down, down_other, block)
    return (down_gradient, up_gradient)


def gathered(frames, gain, first, second, down_map, up_map, lengths, cotangent):
    members = lax.axis_size("member")
    normed = normalize(frames[0], gain)
    low = dot(normed, down_map[0]).astype(BF)
    positions = jnp.arange(BUCKET, dtype=jnp.int32)
    mask = (positions[None, :] < lengths[0][:, None]).reshape(-1)
    masked = cotangent[0] * mask.astype(BF)[:, None]
    rows = normed.shape[0]
    up_slices = lax.all_to_all(up_map, "member", split_axis=2, concat_axis=0, tiled=True)
    all_normed = lax.all_gather(normed, "member", axis=0, tiled=True)
    all_low = lax.all_gather(low, "member", axis=0, tiled=True).reshape(members, rows, -1)
    all_masked = lax.all_gather(masked, "member", axis=0, tiled=True)
    term = jnp.einsum("dgs,dsb->dgb", all_low, up_slices, preferred_element_type=F32)
    pre = term.reshape(members * rows, -1) + dot(
        all_normed, lax.all_gather(first, "fsdp", axis=0, tiled=True)
    )
    dhid = 0.5 * dot(all_masked, lax.all_gather(second, "fsdp", axis=1, tiled=True), ((1,), (1,)))
    dpre = swish_gradient(pre, dhid).reshape(members, rows, -1)
    up_partial = jnp.einsum("jnz,jnv->jzv", all_low, dpre, preferred_element_type=F32)
    back_partial = jnp.einsum("yha,ywa->yhw", dpre, up_slices, preferred_element_type=F32)
    back = lax.psum_scatter(back_partial, "member", scatter_dimension=0, tiled=True)[0].astype(BF)
    up = lax.all_to_all(lax.psum(up_partial, "fsdp"), "member", split_axis=0, concat_axis=2, tiled=True)
    down = lax.psum(dot(normed, back, ((0,), (0,))), "fsdp")
    return (down[None], up)


def solution(mesh):
    in_specs = (
        P("member", "fsdp", None),
        P(),
        P("fsdp", "member"),
        P("member", "fsdp"),
        P("member", None, None),
        P("member", None, None),
        P("member", "fsdp"),
        P("member", "fsdp", None),
    )
    out_specs = (P("member", None, None), P("member", None, None))
    paired = mesh.shape["fsdp"] == 8 and mesh.shape["member"] == 4
    return jax.shard_map(
        paired_halves if paired else gathered,
        mesh=mesh,
        in_specs=in_specs,
        out_specs=out_specs,
        check_vma=False,
    )
```

time: 212 us -> 155 us (0.73)
  waiting for transfers between devices: 103 us -> 74.7 us
  other arithmetic: 29.3 us -> 6.48 us
  Pallas kernels: 0 us -> 15.4 us
  local copies, waits for them, and re-layouts: 30.1 us -> 17.2 us
  matrix products: 11.2 us -> 0.63 us
  starting transfers between devices: 35.6 us -> 38.3 us
    ppermute x26 -> x27, waiting for transfers between devices: 103 us -> 74.7 us  [flip(): lax.ppermute(value, axis, [(i, i ^ bits) for i in range(size)])]
    pallas_call x0 -> x5, Pallas kernels: none -> 15.4 us  [call(): pl.pallas_call(body, in_specs=ins, out_specs=[whole(o.shape) for o in out...]
    gather x7 -> x1, local copies, waits for them, and re-layouts: 14.9 us -> 3.22 us  [paired_halves(): jnp.take(jnp.stack([v[:, :width] for v in (own, fx, fz, fzx)]), slots, ax...]
    dot_general x12 -> x1, matrix products: 11.2 us -> 0.63 us  [dot(): return lax.dot_general(a, b, (dims, ((), ())), preferred_element_type=F32)]
    select_n x8 -> x2, other arithmetic: 8.52 us -> 1.62 us  [paired_halves(): jnp.take(jnp.stack([v[:, :width] for v in (own, fx, fz, fzx)]), slots, ax...]
    another operation x7 -> x4, other arithmetic: 8.37 us -> 3.61 us  [the longest x1 1.34 us: paired_halves(): jnp.stack([v[:, :width] for v in (own, fx, fz, fzx)])]
    concatenate x4 -> x1, other arithmetic: 5.73 us -> 1.18 us  [paired_halves(): fzxy = jnp.concatenate([fzxy_a, fzxy_b], axis=0)]
    another operation x2 -> x6, local copies, waits for them, and re-layouts: 0.75 us -> 3.95 us  [the longest x4 3.93 us: paired_halves(): jnp.stack([v[:, :width] for v in (own, fx, fz, fzx)])]
  transfers between devices with their start and end apart: 26 -> 27, of which waited for: 15 -> 12; matrix products, arithmetic and copies ran while one was open for 26% -> 11% of each run, Pallas kernels for 0% -> 5%
where the time goes in v2:
time: 155 us; the launch traced here: 154 us
  waiting for transfers between devices  74.7 us (48%)
  starting transfers between devices  38.3 us (25%)
  local copies, waits for them, and re-layouts  17.2 us (11%)
  Pallas kernels  15.4 us (10%)
  other arithmetic  6.48 us (4%)
  between operations  1.69 us (1%)
    ppermute x27, waiting for transfers between devices, flip(): lax.ppermute(value, axis, [(i, i ^ bits) for i in range(size)])  74.7 us
    ppermute x27, starting transfers between devices, flip(): lax.ppermute(value, axis, [(i, i ^ bits) for i in range(size)])  38.3 us
    pallas_call x5, Pallas kernels, call(): pl.pallas_call(body, in_specs=ins, out_specs=[whole(o.shape) for o in out...  15.4 us
    unnamed x53, local copies, waits for them, and re-layouts  7.31 us
    another operation x4, local copies, waits for them, and re-layouts, paired_halves(): jnp.stack([v[:, :width] for v in (own, fx, fz, fzx)])  3.93 us
    gather x1, local copies, waits for them, and re-layouts, paired_halves(): jnp.take(jnp.stack([v[:, :width] for v in (own, fx, fz, fzx)]), slots, ax...  3.22 us
  transfers between devices with their start and end apart: 27, of which 12 were waited for; matrix products, arithmetic and copies ran while one was open for 11% of the time, Pallas kernels for 5%

profile of v2, /device:TPU:0, one launch (start us, length us, event | category | flops | bytes accessed | tf_op | source)
XLA Modules:
  0.0 154.4 jit_solution(4061173082189691652)
XLA Ops:
  0.7 1.5 copy.10.second_ref
  3.9 2.9 %collective-permute-start = (bf16[2,384,384]{2,1,0:T(8,128)(2,1)}, bf16[2,384,384]{2,1,0:T(8,128)(2,1)S(1)}, u32[]{:S(2)}, u32[]{:S(2)}) collective-permute-start(bf16[2,384,384]{2,1,0:T(8,128)(2,1)} %get-tuple-element.22), channel_id=1, source_target_pairs={{0,4},{4,0},{8,12},{12,8},{16,20},{20,16},{24,28},{28,24},{1,5},{5... | collective-permute-start | bytes 1769480 | tf_op jit(solution)/shard_map/ppermute | solution.py:31
  9.7 1.8 %shard_map.96 = (bf16[128,3200]{1,0:T(8,128)(2,1)}, bf16[144,3200]{1,0:T(8,128)(2,1)}) custom-call(bf16[1,144,1536]{2,1,0:T(8,128)(2,1)S(1)} %copy-done.19, f32[1,1536]{1,0:T(1,128)S(1)} %broadcast_in_dim.17.gain_ref, bf16[1,1536,64]{2,1,0:T(8,128)(2,1)S(1)} %copy.11.down_ref, bf16[1,64,6144]{2,1,0:T(8,128)(2,1)S(1)} %copy-done, ...), custom_call_target="tpu_custom_call" | custom-call | flops 25165824 | bytes 1873924 | tf_op jit(solution)/shard_map/pallas_call | solution.py:49
  11.5 1.6 %collective-permute-start.1 = (bf16[128,3200]{1,0:T(8,128)(2,1)}, bf16[128,3200]{1,0:T(8,128)(2,1)}, u32[]{:S(2)}, u32[]{:S(2)}) collective-permute-start(bf16[128,3200]{1,0:T(8,128)(2,1)} %get-tuple-element.31.refs_11_), channel_id=1, source_target_pairs={{0,8},{4,12},{8,0},{12,4},{16,24},{20,28},{24,16},{28,20},{1,9},{5... | collective-permute-start | bytes 2457608 | tf_op jit(solution)/shard_map/ppermute | solution.py:31
  13.1 2.6 %collective-permute-start.3 = (bf16[384,384]{1,0:T(8,128)(2,1)S(1)}, bf16[384,384]{1,0:T(8,128)(2,1)S(1)}, u32[]{:S(2)}, u32[]{:S(2)}) collective-permute-start(bf16[384,384]{1,0:T(8,128)(2,1)S(1)} %get-tuple-element.21.refs_0_), channel_id=1, source_target_pairs={{0,16},{4,20},{8,24},{12,28},{16,0},{20,4},{24,8},{28,12},{1,17},{... | collective-permute-start | bytes 884744 | tf_op jit(solution)/shard_map/ppermute | solution.py:31
  15.7 1.5 collective-permute-start.13
  17.2 3.2 %collective-permute-done = bf16[2,384,384]{2,1,0:T(8,128)(2,1)S(1)} collective-permute-done((bf16[2,384,384]{2,1,0:T(8,128)(2,1)}, bf16[2,384,384]{2,1,0:T(8,128)(2,1)S(1)}, u32[]{:S(2)}, u32[]{:S(2)}) %collective-permute-start) | collective-permute-done | bytes 589856 | tf_op jit(solution)/shard_map/ppermute | solution.py:31
  20.4 1.7 %collective-permute-start.11 = (bf16[128,3200]{1,0:T(8,128)(2,1)}, bf16[128,3200]{1,0:T(8,128)(2,1)}, u32[]{:S(2)}, u32[]{:S(2)}) collective-permute-start(bf16[128,3200]{1,0:T(8,128)(2,1)} %get-tuple-element.31.refs_11_), channel_id=1, source_target_pairs={{0,4},{4,0},{8,12},{12,8},{16,20},{20,16},{24,28},{28,24},{1,5},{5... | collective-permute-start | bytes 2457608 | tf_op jit(solution)/shard_map/ppermute | solution.py:31
  22.1 1.8 %slice_bitcast_fusion.3 = bf16[1,128,1536]{2,1,0:T(8,128)(2,1)} fusion(bf16[128,3200]{1,0:T(8,128)(2,1)} %get-tuple-element.31.refs_11_), kind=kLoop, calls=%fused_computation.10 | loop fusion | bytes 786432 | tf_op jit(solution)/shard_map/stack | solution.py:261
  24.0 12.9 %collective-permute-done.3.refs_3_ = bf16[384,384]{1,0:T(8,128)(2,1)S(1)} collective-permute-done((bf16[384,384]{1,0:T(8,128)(2,1)S(1)}, bf16[384,384]{1,0:T(8,128)(2,1)S(1)}, u32[]{:S(2)}, u32[]{:S(2)}) %collective-permute-start.3) | collective-permute-done | bytes 294944 | tf_op jit(solution)/shard_map/ppermute | solution.py:31
  36.9 2.5 %collective-permute-start.4 = (bf16[384,384]{1,0:T(8,128)(2,1)S(1)}, bf16[384,384]{1,0:T(8,128)(2,1)S(1)}, u32[]{:S(2)}, u32[]{:S(2)}) collective-permute-start(bf16[384,384]{1,0:T(8,128)(2,1)S(1)} %copy-done.22), channel_id=1, source_target_pairs={{0,24},{4,28},{8,16},{12,20},{16,8},{20,12},{24,0},{28,4},{1,25},{... | collective-permute-start | bytes 884744 | tf_op jit(solution)/shard_map/ppermute | solution.py:31
  39.4 1.5 collective-permute-start.2
  40.8 1.6 %collective-permute-start.14 = (bf16[128,3200]{1,0:T(8,128)(2,1)}, bf16[128,3200]{1,0:T(8,128)(2,1)S(1)}, u32[]{:S(2)}, u32[]{:S(2)}) collective-permute-start(bf16[128,3200]{1,0:T(8,128)(2,1)} %collective-permute-done.1.refs_13_), channel_id=1, source_target_pairs={{0,2},{1,3},{2,0},{3,1},{4,6},{5,7},{6,4},{7,5},{8,10},{9,11},{10,... | collective-permute-start | bytes 2457608 | tf_op jit(solution)/shard_map/ppermute | solution.py:31
  43.2 5.4 %collective-permute-done.4.refs_4_ = bf16[384,384]{1,0:T(8,128)(2,1)S(1)} collective-permute-done((bf16[384,384]{1,0:T(8,128)(2,1)S(1)}, bf16[384,384]{1,0:T(8,128)(2,1)S(1)}, u32[]{:S(2)}, u32[]{:S(2)}) %collective-permute-start.4) | collective-permute-done | bytes 294944 | tf_op jit(solution)/shard_map/ppermute | solution.py:31
  48.7 5.5 %collective-permute-start.6 = (bf16[384,384]{1,0:T(8,128)(2,1)S(1)}, bf16[384,384]{1,0:T(8,128)(2,1)S(1)}, u32[]{:S(2)}, u32[]{:S(2)}) collective-permute-start(bf16[384,384]{1,0:T(8,128)(2,1)S(1)} %get-tuple-element.28.refs_1_), channel_id=1, source_target_pairs={{0,16},{4,20},{8,24},{12,28},{16,0},{20,4},{24,8},{28,12},{1,17},{... | collective-permute-start | bytes 884744 | tf_op jit(solution)/shard_map/ppermute | solution.py:31
  56.5 11.2 %collective-permute-done.6.refs_6_ = bf16[384,384]{1,0:T(8,128)(2,1)S(1)} collective-permute-done((bf16[384,384]{1,0:T(8,128)(2,1)S(1)}, bf16[384,384]{1,0:T(8,128)(2,1)S(1)}, u32[]{:S(2)}, u32[]{:S(2)}) %collective-permute-start.6) | collective-permute-done | bytes 294944 | tf_op jit(solution)/shard_map/ppermute | solution.py:31
  72.6 1.5 collective-permute-start.15
  78.4 3.2 %gather_fusion = bf16[4,128,1536]{2,1,0:T(8,128)(2,1)} fusion(bf16[4,128,1536]{2,1,0:T(8,128)(2,1)} %pad_maximum_fusion, s32[1024]{0:T(1024)S(1)} %pad_clamp_fusion), kind=kCustom, calls=%fused_computation | custom fusion | bytes 3145744 | tf_op jit(solution)/shard_map/jit(_take)/gather | solution.py:261
  82.8 10.3 %collective-permute-done.15.refs_12_ = bf16[128,3200]{1,0:T(8,128)(2,1)} collective-permute-done((bf16[128,3200]{1,0:T(8,128)(2,1)}, bf16[128,3200]{1,0:T(8,128)(2,1)}, u32[]{:S(2)}, u32[]{:S(2)}) %collective-permute-start.15) | collective-permute-done | bytes 819232 | tf_op jit(solution)/shard_map/ppermute | solution.py:31
  93.1 1.5 collective-permute-start.17
  94.7 1.6 %bitcast_select_fusion = bf16[512,1536]{1,0:T(8,128)(2,1)S(1)} fusion(bf16[4,128,1536]{2,1,0:T(8,128)(2,1)} %gather_fusion, pred[512]{0:T(512)(128)(4,1)S(1)} %broadcast_bitcast_fusion), kind=kLoop, calls=%fused_computation.3 | loop fusion | flops 786432 | bytes 3146240 | tf_op jit(solution)/shard_map/jit(_take)/select_n | solution.py:261
  96.4 5.8 %shard_map.97 = f32[64,1280]{1,0:T(8,128)S(1)} custom-call(bf16[384,384]{1,0:T(8,128)(2,1)S(1)} %get-tuple-element.21.refs_0_, bf16[384,384]{1,0:T(8,128)(2,1)S(1)} %copy-done.15, bf16[384,384]{1,0:T(8,128)(2,1)S(1)} %copy-done.7, bf16[384,384]{1,0:T(8,128)(2,1)S(1)} %copy-done.5, bf16[384,384]{1,0:T(8,128)(2,1)S(1)} %copy-done.9, ...), custom_call_target="tpu_custom_call" | custom-call | flops 2415919104 | bytes 8781824 | tf_op jit(solution)/shard_map/pallas_call | solution.py:49
  103.5 5.5 %shard_map.98 = bf16[64,1280]{1,0:T(8,128)(2,1)S(1)} custom-call(bf16[384,384]{1,0:T(8,128)(2,1)S(1)} %get-tuple-element.21.refs_0_, bf16[384,384]{1,0:T(8,128)(2,1)S(1)} %copy-done.15, bf16[384,384]{1,0:T(8,128)(2,1)S(1)} %copy-done.7, bf16[384,384]{1,0:T(8,128)(2,1)S(1)} %copy-done.5, bf16[384,384]{1,0:T(8,128)(2,1)S(1)} %copy-done.9, ...), custom_call_target="tpu_custom_call" | custom-call | flops 2415919104 | bytes 9019392 | tf_op jit(solution)/shard_map/pallas_call | solution.py:49
  109.8 4.5 %collective-permute-done.18 = bf16[64,1280]{1,0:T(8,128)(2,1)S(1)} collective-permute-done((bf16[64,1280]{1,0:T(8,128)(2,1)S(1)}, bf16[64,1280]{1,0:T(8,128)(2,1)S(1)}, u32[]{:S(2)}, u32[]{:S(2)}) %collective-permute-start.18) | collective-permute-done | bytes 163872 | tf_op jit(solution)/shard_map/ppermute | solution.py:31
  114.4 2.0 %collective-permute-start.24 = (bf16[64,512]{1,0:T(8,128)(2,1)S(1)}, bf16[64,512]{1,0:T(8,128)(2,1)S(1)}, u32[]{:S(2)}, u32[]{:S(2)}) collective-permute-start(bf16[64,512]{1,0:T(8,128)(2,1)S(1)} %fusion), channel_id=1, source_target_pairs={{0,8},{4,12},{8,0},{12,4},{16,24},{20,28},{24,16},{28,20},{1,9},{5... | collective-permute-start | bytes 196616 | tf_op jit(solution)/shard_map/ppermute | solution.py:31
  116.4 1.5 collective-permute-start.23
  121.5 1.7 %collective-permute-start.26 = (bf16[1536,64]{1,0:T(8,128)(2,1)S(1)}, bf16[1536,64]{1,0:T(8,128)(2,1)S(1)}, u32[]{:S(2)}, u32[]{:S(2)}) collective-permute-start(bf16[1536,64]{1,0:T(8,128)(2,1)S(1)} %convolution_convert_fusion.refs_4_), channel_id=1, source_target_pairs={{0,16},{4,20},{8,24},{12,28},{16,0},{20,4},{24,8},{28,12},{1,17},{... | collective-permute-start | bytes 589832 | tf_op jit(solution)/shard_map/ppermute | solution.py:31
  123.2 13.5 %collective-permute-done.19 = bf16[2,64,768]{2,1,0:T(8,128)(2,1)S(1)} collective-permute-done((bf16[2,64,768]{2,1,0:T(8,128)(2,1)S(1)}, bf16[2,64,768]{2,1,0:T(8,128)(2,1)S(1)}, u32[]{:S(2)}, u32[]{:S(2)}) %collective-permute-start.19) | collective-permute-done | bytes 196640 | tf_op jit(solution)/shard_map/ppermute | solution.py:31
  137.7 2.5 %collective-permute-start.22 = (bf16[2,64,768]{2,1,0:T(8,128)(2,1)S(1)}, bf16[2,64,768]{2,1,0:T(8,128)(2,1)S(1)}, u32[]{:S(2)}, u32[]{:S(2)}) collective-permute-start(bf16[2,64,768]{2,1,0:T(8,128)(2,1)S(1)} %add_convert_fusion.refs_0_), channel_id=1, source_target_pairs={{0,12},{4,8},{8,4},{12,0},{16,28},{20,24},{24,20},{28,16},{1,13},{... | collective-permute-start | bytes 589832 | tf_op jit(solution)/shard_map/ppermute | solution.py:31
  140.2 3.5 %collective-permute-done.26.refs_5_ = bf16[1536,64]{1,0:T(8,128)(2,1)S(1)} collective-permute-done((bf16[1536,64]{1,0:T(8,128)(2,1)S(1)}, bf16[1536,64]{1,0:T(8,128)(2,1)S(1)}, u32[]{:S(2)}, u32[]{:S(2)}) %collective-permute-start.26) | collective-permute-done | bytes 196640 | tf_op jit(solution)/shard_map/ppermute | solution.py:31
  143.7 4.2 %collective-permute-done.20.refs_1_ = bf16[2,64,768]{2,1,0:T(8,128)(2,1)S(1)} collective-permute-done((bf16[2,64,768]{2,1,0:T(8,128)(2,1)S(1)}, bf16[2,64,768]{2,1,0:T(8,128)(2,1)S(1)}, u32[]{:S(2)}, u32[]{:S(2)}) %collective-permute-start.20) | collective-permute-done | bytes 196640 | tf_op jit(solution)/shard_map/ppermute | solution.py:31
  147.9 4.2 %collective-permute-done.22.refs_3_ = bf16[2,64,768]{2,1,0:T(8,128)(2,1)S(1)} collective-permute-done((bf16[2,64,768]{2,1,0:T(8,128)(2,1)S(1)}, bf16[2,64,768]{2,1,0:T(8,128)(2,1)S(1)}, u32[]{:S(2)}, u32[]{:S(2)}) %collective-permute-start.22) | collective-permute-done | bytes 196640 | tf_op jit(solution)/shard_map/ppermute | solution.py:31
  (104 shorter events, 26.6 us)
Async XLA Ops:
  3.9 16.5 %collective-permute-start = (bf16[2,384,384]{2,1,0:T(8,128)(2,1)}, bf16[2,384,384]{2,1,0:T(8,128)(2,1)S(1)}, u32[]{:S(2)}, u32[]{:S(2)}) collective-permute-start(bf16[2,384,384]{2,1,0:T(8,128)(2,1)} %get-tuple-element.22), channel_id=1, source_target_pairs={{0,4},{4,0},{8,12},{12,8},{16,20},{20,16},{24,28},{28,24},{1,5},{5... | collective-permute-start | bytes 1769480 | tf_op jit(solution)/shard_map/ppermute | solution.py:31
  9.7 27.2 %copy-start.22 = (bf16[384,384]{1,0:T(8,128)(2,1)S(1)}, bf16[384,384]{1,0:T(8,128)(2,1)}, u32[]{:S(2)}) copy-start(bf16[384,384]{1,0:T(8,128)(2,1)} %copy-done.21) | copy-start | bytes 884740
  11.5 27.8 %collective-permute-start.1 = (bf16[128,3200]{1,0:T(8,128)(2,1)}, bf16[128,3200]{1,0:T(8,128)(2,1)}, u32[]{:S(2)}, u32[]{:S(2)}) collective-permute-start(bf16[128,3200]{1,0:T(8,128)(2,1)} %get-tuple-element.31.refs_11_), channel_id=1, source_target_pairs={{0,8},{4,12},{8,0},{12,4},{16,24},{20,28},{24,16},{28,20},{1,9},{5... | collective-permute-start | bytes 2457608 | tf_op jit(solution)/shard_map/ppermute | solution.py:31
  13.1 23.8 %collective-permute-start.3 = (bf16[384,384]{1,0:T(8,128)(2,1)S(1)}, bf16[384,384]{1,0:T(8,128)(2,1)S(1)}, u32[]{:S(2)}, u32[]{:S(2)}) collective-permute-start(bf16[384,384]{1,0:T(8,128)(2,1)S(1)} %get-tuple-element.21.refs_0_), channel_id=1, source_target_pairs={{0,16},{4,20},{8,24},{12,28},{16,0},{20,4},{24,8},{28,12},{1,17},{... | collective-permute-start | bytes 884744 | tf_op jit(solution)/shard_map/ppermute | solution.py:31
  15.7 25.1 %collective-permute-start.13 = (bf16[144,3200]{1,0:T(8,128)(2,1)}, bf16[144,3200]{1,0:T(8,128)(2,1)S(1)}, u32[]{:S(2)}, u32[]{:S(2)}) collective-permute-start(bf16[144,3200]{1,0:T(8,128)(2,1)} %get-tuple-element.33), channel_id=1, source_target_pairs={{0,2},{1,3},{2,0},{3,1},{4,6},{5,7},{6,4},{7,5},{8,10},{9,11},{10,... | collective-permute-start | bytes 2764808 | tf_op jit(solution)/shard_map/ppermute | solution.py:31
  20.4 34.5 %collective-permute-start.11 = (bf16[128,3200]{1,0:T(8,128)(2,1)}, bf16[128,3200]{1,0:T(8,128)(2,1)}, u32[]{:S(2)}, u32[]{:S(2)}) collective-permute-start(bf16[128,3200]{1,0:T(8,128)(2,1)} %get-tuple-element.31.refs_11_), channel_id=1, source_target_pairs={{0,4},{4,0},{8,12},{12,8},{16,20},{20,16},{24,28},{28,24},{1,5},{5... | collective-permute-start | bytes 2457608 | tf_op jit(solution)/shard_map/ppermute | solution.py:31
  36.9 32.2 %copy-start.4 = (bf16[384,384]{1,0:T(8,128)(2,1)}, bf16[384,384]{1,0:T(8,128)(2,1)S(1)}, u32[]{:S(2)}) copy-start(bf16[384,384]{1,0:T(8,128)(2,1)S(1)} %collective-permute-done.3.refs_3_) | copy-start | bytes 884740
  36.9 11.8 %collective-permute-start.4 = (bf16[384,384]{1,0:T(8,128)(2,1)S(1)}, bf16[384,384]{1,0:T(8,128)(2,1)S(1)}, u32[]{:S(2)}, u32[]{:S(2)}) collective-permute-start(bf16[384,384]{1,0:T(8,128)(2,1)S(1)} %copy-done.22), channel_id=1, source_target_pairs={{0,24},{4,28},{8,16},{12,20},{16,8},{20,12},{24,0},{28,4},{1,25},{... | collective-permute-start | bytes 884744 | tf_op jit(solution)/shard_map/ppermute | solution.py:31
  39.4 15.5 %collective-permute-start.2 = (bf16[384,384]{1,0:T(8,128)(2,1)S(1)}, bf16[384,384]{1,0:T(8,128)(2,1)S(1)}, u32[]{:S(2)}, u32[]{:S(2)}) collective-permute-start(bf16[384,384]{1,0:T(8,128)(2,1)S(1)} %copy-done.22), channel_id=1, source_target_pairs={{0,8},{4,12},{8,0},{12,4},{16,24},{20,28},{24,16},{28,20},{1,9},{5... | collective-permute-start | bytes 884744 | tf_op jit(solution)/shard_map/ppermute | solution.py:31
  40.8 31.8 %collective-permute-start.14 = (bf16[128,3200]{1,0:T(8,128)(2,1)}, bf16[128,3200]{1,0:T(8,128)(2,1)S(1)}, u32[]{:S(2)}, u32[]{:S(2)}) collective-permute-start(bf16[128,3200]{1,0:T(8,128)(2,1)} %collective-permute-done.1.refs_13_), channel_id=1, source_target_pairs={{0,2},{1,3},{2,0},{3,1},{4,6},{5,7},{6,4},{7,5},{8,10},{9,11},{10,... | collective-permute-start | bytes 2457608 | tf_op jit(solution)/shard_map/ppermute | solution.py:31
  48.7 21.7 %copy-start.8 = (bf16[384,384]{1,0:T(8,128)(2,1)}, bf16[384,384]{1,0:T(8,128)(2,1)S(1)}, u32[]{:S(2)}) copy-start(bf16[384,384]{1,0:T(8,128)(2,1)S(1)} %collective-permute-done.4.refs_4_) | copy-start | bytes 884740
  48.7 19.1 %collective-permute-start.6 = (bf16[384,384]{1,0:T(8,128)(2,1)S(1)}, bf16[384,384]{1,0:T(8,128)(2,1)S(1)}, u32[]{:S(2)}, u32[]{:S(2)}) collective-permute-start(bf16[384,384]{1,0:T(8,128)(2,1)S(1)} %get-tuple-element.28.refs_1_), channel_id=1, source_target_pairs={{0,16},{4,20},{8,24},{12,28},{16,0},{20,4},{24,8},{28,12},{1,17},{... | collective-permute-start | bytes 884744 | tf_op jit(solution)/shard_map/ppermute | solution.py:31
  54.8 14.2 %copy-start.6 = (bf16[384,384]{1,0:T(8,128)(2,1)}, bf16[384,384]{1,0:T(8,128)(2,1)S(1)}, u32[]{:S(2)}) copy-start(bf16[384,384]{1,0:T(8,128)(2,1)S(1)} %collective-permute-done.2.refs_2_) | copy-start | bytes 884740
  54.9 15.5 %collective-permute-start.5 = (bf16[384,384]{1,0:T(8,128)(2,1)}, bf16[384,384]{1,0:T(8,128)(2,1)S(1)}, u32[]{:S(2)}, u32[]{:S(2)}) collective-permute-start(bf16[384,384]{1,0:T(8,128)(2,1)} %get-tuple-element.29), channel_id=1, source_target_pairs={{0,8},{4,12},{8,0},{12,4},{16,24},{20,28},{24,16},{28,20},{1,9},{5... | collective-permute-start | bytes 884744 | tf_op jit(solution)/shard_map/ppermute | solution.py:31
  54.9 21.1 %collective-permute-start.12 = (bf16[128,3200]{1,0:T(8,128)(2,1)}, bf16[128,3200]{1,0:T(8,128)(2,1)S(1)}, u32[]{:S(2)}, u32[]{:S(2)}) collective-permute-start(bf16[128,3200]{1,0:T(8,128)(2,1)} %collective-permute-done.1.refs_13_), channel_id=1, source_target_pairs={{0,4},{4,0},{8,12},{12,8},{16,20},{20,16},{24,28},{28,24},{1,5},{5... | collective-permute-start | bytes 2457608 | tf_op jit(solution)/shard_map/ppermute | solution.py:31
  67.7 15.0 %collective-permute-start.7 = (bf16[384,384]{1,0:T(8,128)(2,1)}, bf16[384,384]{1,0:T(8,128)(2,1)}, u32[]{:S(2)}, u32[]{:S(2)}) collective-permute-start(bf16[384,384]{1,0:T(8,128)(2,1)} %get-tuple-element.29), channel_id=1, source_target_pairs={{0,24},{4,28},{8,16},{12,20},{16,8},{20,12},{24,0},{28,4},{1,25},{... | collective-permute-start | bytes 884744 | tf_op jit(solution)/shard_map/ppermute | solution.py:31
  70.3 26.0 %collective-permute-start.8 = (bf16[4,384,384]{2,1,0:T(8,128)(2,1)}, bf16[4,384,384]{2,1,0:T(8,128)(2,1)S(1)}, u32[]{:S(2)}, u32[]{:S(2)}) collective-permute-start(bf16[4,384,384]{2,1,0:T(8,128)(2,1)} %pad_maximum_fusion.1), channel_id=1, source_target_pairs={{0,1},{1,0},{2,3},{3,2},{4,5},{5,4},{6,7},{7,6},{8,9},{9,8},{10,11... | collective-permute-start | bytes 3538952 | tf_op jit(solution)/shard_map/ppermute | solution.py:31
  72.1 10.6 %collective-permute-start.9 = (bf16[3,384,384]{2,1,0:T(8,128)(2,1)}, bf16[3,384,384]{2,1,0:T(8,128)(2,1)S(1)}, u32[]{:S(2)}, u32[]{:S(2)}) collective-permute-start(bf16[3,384,384]{2,1,0:T(8,128)(2,1)} %pad_maximum_fusion.2), channel_id=1, source_target_pairs={{0,1},{1,0},{2,3},{3,2},{4,5},{5,4},{6,7},{7,6},{8,9},{9,8},{10,11... | collective-permute-start | bytes 2654216 | tf_op jit(solution)/shard_map/ppermute | solution.py:31
  72.6 20.5 %collective-permute-start.15 = (bf16[128,3200]{1,0:T(8,128)(2,1)}, bf16[128,3200]{1,0:T(8,128)(2,1)}, u32[]{:S(2)}, u32[]{:S(2)}) collective-permute-start(bf16[128,3200]{1,0:T(8,128)(2,1)} %collective-permute-done.11.refs_12_), channel_id=1, source_target_pairs={{0,2},{1,3},{2,0},{3,1},{4,6},{5,7},{6,4},{7,5},{8,10},{9,11},{10,... | collective-permute-start | bytes 2457608 | tf_op jit(solution)/shard_map/ppermute | solution.py:31
  76.0 26.2 %collective-permute-start.16 = (bf16[80,3200]{1,0:T(8,128)(2,1)}, bf16[80,3200]{1,0:T(8,128)(2,1)}, u32[]{:S(2)}, u32[]{:S(2)}) collective-permute-start(bf16[80,3200]{1,0:T(8,128)(2,1)} %slice.54), channel_id=1, source_target_pairs={{0,4},{4,0},{8,12},{12,8},{16,20},{20,16},{24,28},{28,24},{1,5},{5... | collective-permute-start | bytes 1536008 | tf_op jit(solution)/shard_map/ppermute | solution.py:31
  81.6 14.7 %copy-start.15 = (bf16[384,384]{1,0:T(8,128)(2,1)S(1)}, bf16[384,384]{1,0:T(8,128)(2,1)}, u32[]{:S(2)}) copy-start(bf16[384,384]{1,0:T(8,128)(2,1)} %copy-done.14) | copy-start | bytes 884740
  82.7 13.6 %collective-permute-start.10 = (bf16[384,384]{1,0:T(8,128)(2,1)}, bf16[384,384]{1,0:T(8,128)(2,1)S(1)}, u32[]{:S(2)}, u32[]{:S(2)}) collective-permute-start(bf16[384,384]{1,0:T(8,128)(2,1)} %collective-permute-done.7.refs_7_), channel_id=1, source_target_pairs={{0,1},{1,0},{2,3},{3,2},{4,5},{5,4},{6,7},{7,6},{8,9},{9,8},{10,11... | collective-permute-start | bytes 884744 | tf_op jit(solution)/shard_map/ppermute | solution.py:31
  93.1 9.0 %collective-permute-start.17 = (bf16[48,3200]{1,0:T(8,128)(2,1)S(1)}, bf16[48,3200]{1,0:T(8,128)(2,1)S(1)}, u32[]{:S(2)}, u32[]{:S(2)}) collective-permute-start(bf16[48,3200]{1,0:T(8,128)(2,1)S(1)} %slice.55), channel_id=1, source_target_pairs={{0,2},{1,3},{2,0},{3,1},{4,6},{5,7},{6,4},{7,5},{8,10},{9,11},{10,... | collective-permute-start | bytes 921608 | tf_op jit(solution)/shard_map/ppermute | solution.py:31
  109.0 5.4 %collective-permute-start.18 = (bf16[64,1280]{1,0:T(8,128)(2,1)S(1)}, bf16[64,1280]{1,0:T(8,128)(2,1)S(1)}, u32[]{:S(2)}, u32[]{:S(2)}) collective-permute-start(bf16[64,1280]{1,0:T(8,128)(2,1)S(1)} %shard_map.98), channel_id=1, source_target_pairs={{0,2},{1,3},{2,0},{3,1},{4,6},{5,7},{6,4},{7,5},{8,10},{9,11},{10,... | collective-permute-start | bytes 491528 | tf_op jit(solution)/shard_map/ppermute | solution.py:31
  114.4 5.8 %collective-permute-start.25 = (bf16[64,512]{1,0:T(8,128)(2,1)S(1)}, bf16[64,512]{1,0:T(8,128)(2,1)S(1)}, u32[]{:S(2)}, u32[]{:S(2)}) collective-permute-start(bf16[64,512]{1,0:T(8,128)(2,1)S(1)} %fusion), channel_id=1, source_target_pairs={{0,12},{4,8},{8,4},{12,0},{16,28},{20,24},{24,20},{28,16},{1,13},{... | collective-permute-start | bytes 196616 | tf_op jit(solution)/shard_map/ppermute | solution.py:31
  114.4 5.7 %collective-permute-start.24 = (bf16[64,512]{1,0:T(8,128)(2,1)S(1)}, bf16[64,512]{1,0:T(8,128)(2,1)S(1)}, u32[]{:S(2)}, u32[]{:S(2)}) collective-permute-start(bf16[64,512]{1,0:T(8,128)(2,1)S(1)} %fusion), channel_id=1, source_target_pairs={{0,8},{4,12},{8,0},{12,4},{16,24},{20,28},{24,16},{28,20},{1,9},{5... | collective-permute-start | bytes 196616 | tf_op jit(solution)/shard_map/ppermute | solution.py:31
  116.4 4.4 %collective-permute-start.23 = (bf16[64,512]{1,0:T(8,128)(2,1)S(1)}, bf16[64,512]{1,0:T(8,128)(2,1)S(1)}, u32[]{:S(2)}, u32[]{:S(2)}) collective-permute-start(bf16[64,512]{1,0:T(8,128)(2,1)S(1)} %fusion), channel_id=1, source_target_pairs={{0,4},{4,0},{8,12},{12,8},{16,20},{20,16},{24,28},{28,24},{1,5},{5... | collective-permute-start | bytes 196616 | tf_op jit(solution)/shard_map/ppermute | solution.py:31
  117.9 18.7 %collective-permute-start.19 = (bf16[2,64,768]{2,1,0:T(8,128)(2,1)S(1)}, bf16[2,64,768]{2,1,0:T(8,128)(2,1)S(1)}, u32[]{:S(2)}, u32[]{:S(2)}) collective-permute-start(bf16[2,64,768]{2,1,0:T(8,128)(2,1)S(1)} %pad_maximum_fusion.4), channel_id=1, source_target_pairs={{0,16},{4,20},{8,24},{12,28},{16,0},{20,4},{24,8},{28,12},{1,17},{... | collective-permute-start | bytes 589832 | tf_op jit(solution)/shard_map/ppermute | solution.py:31
  121.5 22.2 %collective-permute-start.26 = (bf16[1536,64]{1,0:T(8,128)(2,1)S(1)}, bf16[1536,64]{1,0:T(8,128)(2,1)S(1)}, u32[]{:S(2)}, u32[]{:S(2)}) collective-permute-start(bf16[1536,64]{1,0:T(8,128)(2,1)S(1)} %convolution_convert_fusion.refs_4_), channel_id=1, source_target_pairs={{0,16},{4,20},{8,24},{12,28},{16,0},{20,4},{24,8},{28,12},{1,17},{... | collective-permute-start | bytes 589832 | tf_op jit(solution)/shard_map/ppermute | solution.py:31
  136.7 11.2 %collective-permute-start.20 = (bf16[2,64,768]{2,1,0:T(8,128)(2,1)S(1)}, bf16[2,64,768]{2,1,0:T(8,128)(2,1)S(1)}, u32[]{:S(2)}, u32[]{:S(2)}) collective-permute-start(bf16[2,64,768]{2,1,0:T(8,128)(2,1)S(1)} %add_convert_fusion.refs_0_), channel_id=1, source_target_pairs={{0,8},{4,12},{8,0},{12,4},{16,24},{20,28},{24,16},{28,20},{1,9},{5... | collective-permute-start | bytes 589832 | tf_op jit(solution)/shard_map/ppermute | solution.py:31
  136.8 11.2 %collective-permute-start.21 = (bf16[2,64,768]{2,1,0:T(8,128)(2,1)S(1)}, bf16[2,64,768]{2,1,0:T(8,128)(2,1)S(1)}, u32[]{:S(2)}, u32[]{:S(2)}) collective-permute-start(bf16[2,64,768]{2,1,0:T(8,128)(2,1)S(1)} %add_convert_fusion.refs_0_), channel_id=1, source_target_pairs={{0,4},{4,0},{8,12},{12,8},{16,20},{20,16},{24,28},{28,24},{1,5},{5... | collective-permute-start | bytes 589832 | tf_op jit(solution)/shard_map/ppermute | solution.py:31
  137.7 14.4 %collective-permute-start.22 = (bf16[2,64,768]{2,1,0:T(8,128)(2,1)S(1)}, bf16[2,64,768]{2,1,0:T(8,128)(2,1)S(1)}, u32[]{:S(2)}, u32[]{:S(2)}) collective-permute-start(bf16[2,64,768]{2,1,0:T(8,128)(2,1)S(1)} %add_convert_fusion.refs_0_), channel_id=1, source_target_pairs={{0,12},{4,8},{8,4},{12,0},{16,28},{20,24},{24,20},{28,16},{1,13},{... | collective-permute-start | bytes 589832 | tf_op jit(solution)/shard_map/ppermute | solution.py:31
  (20 other events, 135.9 us)

commit v3 on v2

v3 whole, which is shorter than its diff:
```python
import jax
import jax.numpy as jnp
from jax import lax
from jax.experimental import pallas as pl
from jax.experimental.pallas import tpu as pltpu
from jax.sharding import PartitionSpec as P

BUCKET = 144
LMAX = 126
BF = jnp.bfloat16
F32 = jnp.float32


def normalize(frames, gain):
    values = frames.astype(F32)
    mean = jnp.mean(values, axis=1, keepdims=True)
    var = jnp.mean((values - mean) ** 2, axis=1, keepdims=True)
    return (gain * (values - mean) / jnp.sqrt(var + 1e-05)).astype(BF)


def swish_gradient(pre, dhid):
    sigma = jax.nn.sigmoid(pre)
    return (dhid * sigma * (1.0 + pre * (1.0 - sigma))).astype(BF)


def dot(a, b, dims=((1,), (0,))):
    return lax.dot_general(a, b, (dims, ((), ())), preferred_element_type=F32)


def flip(axis, size, bits):
    return lambda value: lax.ppermute(value, axis, [(i, i ^ bits) for i in range(size)])


def whole(shape):
    return pl.BlockSpec(shape, lambda: (0,) * len(shape))


def place():
    f, m = lax.axis_index("fsdp"), lax.axis_index("member")
    return f, (f >> 1) & 1, f & 1, m >> 1, m & 1


def lanes(start, size):
    return pl.ds(pl.multiple_of(start, 128), size)


def call(body, ins, outs, args, scratch=(), flops=0, size=0, vmem=40):
    return pl.pallas_call(
        body,
        in_specs=ins,
        out_specs=[whole(o.shape) for o in outs],
        out_shape=outs,
        scratch_shapes=list(scratch),
        compiler_params=pltpu.CompilerParams(vmem_limit_bytes=vmem * 1024 * 1024),
        cost_estimate=pl.CostEstimate(flops=flops, bytes_accessed=size, transcendentals=0),
    )(*args)


def prepare(frames, gain, first, turned, down_turned, up_map, lengths, cotangent, rows):
    depth, block = first.shape
    part, half = block // 4, depth // 2
    width, rank = frames.shape[2], down_turned.shape[1]
    fold = rank // 16
    lined = 2 * width + 2 * rank

    def body(frames_ref, gain_ref, first_ref, turned_ref, down_ref, up_ref, lengths_ref, cot_ref, *refs):
        own_ref, cross_ref, side_ref, same_ref, flip_ref, block_ref, masked_ref, map_ref, sems = refs
        _, low_bit, x, y, core = place()
        copies = []

        def load(src, dst):
            copy = pltpu.make_async_copy(src, dst, sems.at[len(copies)])
            copies.append(copy)
            copy.start()

        load(frames_ref.at[0, pl.ds(0, rows)], block_ref)
        load(down_ref.at[0], map_ref)
        load(cot_ref.at[0, pl.ds(0, rows)], masked_ref)
        for dl in (0, 1):
            for dx in (0, 1):
                start = ((x ^ dx) * 2 + (low_bit ^ dl)) * part
                for k in range(4):
                    src = (first_ref, turned_ref)[k // 2].at[pl.ds((k % 2) * half, half), lanes(start, part)]
                    if dx:
                        load(src, side_ref.at[pl.ds(rows, half), pl.ds((4 * dl + k) * part, part)])
                    else:
                        load(src, (same_ref, flip_ref)[dl].at[:, pl.ds(k * part, part)])
        for dc in range(2):
            start = ((1 - y) * 2 + (core ^ dc)) * block + (x * 2 + low_bit) * part
            for i in range(fold):
                load(
                    up_ref.at[0, pl.ds(16 * i, 16), lanes(start, part)],
                    cross_ref.at[pl.ds(rows, 16), pl.ds((2 * i + dc) * part, part)],
                )
        cross_ref[rows:, 2 * fold * part :] = jnp.zeros((16, lined - 2 * fold * part), BF)
        side_ref[rows:, 8 * part :] = jnp.zeros((half, lined - 8 * part), BF)
        copies[0].wait()
        normed = normalize(block_ref[...], gain_ref[...])
        for ref in (own_ref, cross_ref, side_ref):
            ref[:rows, :width] = normed
        copies[1].wait()
        low = dot(normed, map_ref[...], ((1,), (1,)))
        low = jnp.concatenate([low, jnp.zeros_like(low)], axis=1).astype(BF)
        copies[2].wait()
        keep = lax.broadcasted_iota(jnp.int32, (rows, width), 0) < lengths_ref[0, 0]
        masked = jnp.where(keep, masked_ref[...].astype(F32), 0.0).astype(BF)
        for ref in (own_ref, cross_ref, side_ref):
            ref[:rows, width : 2 * width] = masked
            ref[:rows, 2 * width :] = low
        for copy in copies[3:]:
            copy.wait()

    args = (frames, gain, first, turned, down_turned, up_map, lengths, cotangent)
    ins = [pl.BlockSpec(memory_space=pltpu.HBM)] * 8
    ins[1] = whole((width,))
    ins[6] = pl.BlockSpec(memory_space=pltpu.SMEM)
    piece = (half, 4 * part)
    shapes = [(rows, lined), (rows + 16, lined), (rows + half, lined), piece, piece]
    outs = [jax.ShapeDtypeStruct(shape, BF) for shape in shapes]
    scratch = [
        pltpu.VMEM((rows, width), BF),
        pltpu.VMEM((rows, width), BF),
        pltpu.VMEM((rank, width), BF),
        pltpu.SemaphoreType.DMA((19 + 2 * fold,)),
    ]
    return call(body, ins, outs, args, scratch, vmem=62)


def work(weights, frames, up, width, rank, own):
    if own:
        pieces, swapped = weights
        depth, part = pieces[0].shape[0] * 2, pieces[0].shape[1] // 4
    else:
        pieces, swapped = [], []
        depth, part = weights[0].shape[0] // 8, weights[0].shape[1] // 2
    rows, lined = frames[2].shape
    codes = (0, 1, 4, 6, 2, 5, 3, 7)
    n_pieces, n_swapped = len(pieces), len(swapped)
    hidden = 2 * part
    count = 4 * rows

    def body(*refs):
        piece_refs, refs = refs[:n_pieces], refs[n_pieces:]
        swap_refs, refs = refs[:n_swapped], refs[n_swapped:]
        if own:
            *frame_refs, up_ref, up_out, back_out, w_in, w_out, packed, map_ref, sems, frame_sems = refs
        else:
            w_in, w_out, *frame_refs, up_ref, out_ref, packed, map_ref, frame_sems = refs
        f, low_bit, x, y, core = place()
        slot = low_bit * 2 + x
        copies = []
        for i, ref in enumerate(frame_refs):
            at = pl.multiple_of((slot ^ i) * rows, 16)
            copies.append(
                pltpu.make_async_copy(ref.at[pl.ds(0, rows)], packed.at[pl.ds(at, rows)], frame_sems.at[i])
            )
        flat = []
        for ref in swap_refs:
            flat += [ref.at[j] for j in range(ref.shape[0])] if len(ref.shape) == 3 else [ref]
        for side, group in enumerate((piece_refs, flat)):
            for i, ref in enumerate(group):
                at = pl.multiple_of((f ^ codes[i]) * depth, 16)
                for k in range(4):
                    copies.append(
                        pltpu.make_async_copy(
                            ref.at[:, pl.ds(k * part, part)],
                            (w_in, w_out)[k // 2].at[
                                pl.ds(at + (k % 2) * (depth // 2), depth // 2), pl.ds(side * part, part)
                            ],
                            sems.at[len(copies) - 4],
                        )
                    )
        for copy in copies:
            copy.start()
        if own:
            for dc in range(2):
                start = (y * 2 + (core ^ dc)) * (4 * part) + (x * 2 + low_bit) * part
                map_ref[:, dc * part : (dc + 1) * part] = up_ref[0, :, lanes(start, part)]
        else:
            for i in range(rank // 16):
                map_ref[16 * i : 16 * (i + 1), :] = up_ref[rows:, i * hidden : (i + 1) * hidden]
        for copy in copies:
            copy.wait()
        step = 256 if hidden % 256 == 0 else part
        back = jnp.zeros((rank, count), F32)
        low = packed[:, 2 * width :][:, :rank]
        for at in range(0, hidden, step):
            now = slice(at, at + step)
            pre = dot(packed[:, :width], w_in[:, now]) + dot(low, map_ref[:, now])
            dhid = 0.5 * dot(packed[:, width : 2 * width], w_out[:, now])
            dpre = swish_gradient(pre, dhid)
            sums = dot(low, dpre, ((0,), (0,))).astype(BF)
            if own:
                up_out[:, now] = sums
            else:
                out_ref[:, now] = sums
            back = back + dot(map_ref[:, now], dpre, ((1,), (1,)))
        if own:
            back_out[...] = back
        else:
            out_ref[:, hidden:] = back.astype(BF)

    anywhere = pl.BlockSpec(memory_space=pl.ANY)
    scratch = [pltpu.VMEM((count, lined), BF), pltpu.VMEM((rank, hidden), BF)]
    whole_weights = jax.ShapeDtypeStruct((8 * depth, hidden), BF)
    if own:
        args = (*pieces, *swapped, *frames, up)
        ins = [anywhere] * (len(args) - 1) + [whole(up.shape)]
        outs = [
            jax.ShapeDtypeStruct((rank, hidden), BF),
            jax.ShapeDtypeStruct((rank, count), F32),
            whole_weights,
            whole_weights,
        ]
        scratch.append(pltpu.SemaphoreType.DMA((64,)))
    else:
        args = (*weights, *frames, up)
        ins = [whole(w.shape) for w in weights] + [anywhere] * 4 + [whole(up.shape)]
        outs = [jax.ShapeDtypeStruct((rank, hidden + count), BF)]
    scratch.append(pltpu.SemaphoreType.DMA((4,)))
    return call(body, ins, outs, args, scratch)


def down_quarter(backs, frames, width):
    rank, count = backs[0].shape
    rows, quarter = count // 4, width // 4

    def body(*refs):
        back_refs, frame_refs, (out_ref, normed, sems) = refs[:4], refs[4:8], refs[8:]
        _, low_bit, x, _, _ = place()
        slot = low_bit * 2 + x
        copies = []
        for i, ref in enumerate(frame_refs):
            copies.append(
                pltpu.make_async_copy(
                    ref.at[pl.ds(0, rows), lanes(slot * quarter, quarter)],
                    normed.at[pl.ds(pl.multiple_of((slot ^ i) * rows, 16), rows)],
                    sems.at[i],
                )
            )
        for copy in copies:
            copy.start()
        b, bx, bz, bzx = [ref[...].astype(F32) for ref in back_refs]
        back = ((b + bx) + (bz + bzx)).astype(BF)
        for copy in copies:
            copy.wait()
        out_ref[...] = dot(back, normed[...]).astype(BF)

    args = (*backs, *frames)
    ins = [whole(b.shape) for b in backs] + [pl.BlockSpec(memory_space=pl.ANY)] * 4
    scratch = [pltpu.VMEM((count, quarter), BF), pltpu.SemaphoreType.DMA((4,))]
    outs = [jax.ShapeDtypeStruct((rank, quarter), BF)]
    return call(body, ins, outs, args, scratch)[0]


def spread(own_parts, cross_parts, block):
    rank, hidden = own_parts[0].shape
    part = hidden // 2
    quarter = cross_parts[0].shape[1] - hidden

    def body(*refs):
        own_refs, cross_refs, (up_out, down_out) = refs[:4], refs[4:8], refs[8:]
        _, low_bit, x, y, core = place()
        for i in range(4):
            at = ((x * 2 + low_bit) ^ ((i & 1) * 2 + (i >> 1))) * part
            for dy, ref in enumerate((own_refs[i], cross_refs[i])):
                for dc in range(2):
                    start = ((y ^ dy) * 2 + (core ^ dc)) * block + at
                    up_out[0, :, lanes(start, part)] = ref[:, dc * part : (dc + 1) * part].astype(F32)
            at = ((low_bit * 2 + x) ^ i) * quarter
            down_out[0, :, lanes(at, quarter)] = cross_refs[i][:, hidden:].astype(F32)

    args = (*own_parts, *cross_parts)
    outs = [
        jax.ShapeDtypeStruct((1, rank, 4 * block), F32),
        jax.ShapeDtypeStruct((1, rank, 4 * quarter), F32),
    ]
    return call(body, [whole(a.shape) for a in args], outs, args)


def after(value, *done):
    return lax.optimization_barrier((value, *done))[0]


def plus(a, b):
    return (a.astype(F32) + b.astype(F32)).astype(BF)


def paired_halves(frames, gain, first, second, down_map, up_map, lengths, cotangent):
    over_x, over_low = flip("fsdp", 8, 1), flip("fsdp", 8, 2)
    over_half, over_both = flip("fsdp", 8, 4), flip("fsdp", 8, 6)
    over_xlow = flip("fsdp", 8, 3)
    over_y, over_core = flip("member", 4, 2), flip("member", 4, 1)

    width, rank = frames.shape[2], down_map.shape[2]
    rows = -(-LMAX // 16) * 16
    block = first.shape[1]
    part = block // 4
    hidden = 2 * part

    own, cross, side, w00, w01 = prepare(
        frames, gain, first, second.T, down_map.transpose(0, 2, 1), up_map, lengths, cotangent, rows
    )
    fx, fy, fz = over_x(side), over_y(cross), over_low(own)
    z2n, z3n = over_half(w00), over_both(w01)
    one = (fx, fy, fz, z2n, z3n)
    wx0, wx1 = fx[rows:, : 4 * part], fx[rows:, 4 * part : 8 * part]
    fzx, fzy = over_x(after(fz, *one)), over_y(after(fz, *one))
    z1n, z2f = over_low(after(w01, *one)), over_half(after(wx0, *one))
    near = over_core(jnp.stack([w00, wx0, z2n, z3n]))
    two = (fzx, fzy, z1n, z2f)
    fzxy, fxy = over_x(after(fzy, *two)), over_y(after(fx[:rows], *two))
    z1f, z3f = over_low(after(wx1, *two)), over_both(after(wx1, *two))
    middle = over_core(jnp.stack([z1n, z2f]))
    far = over_core(jnp.stack([z1f, z3f]))
    weights = ([w00, wx0, z2n, z3n, z1n, z2f, z1f, z3f], [near, middle, far])

    up, back, w_in, w_out = work(weights, [own, fx, fz, fzx], up_map, width, rank, True)
    (theirs,) = work((w_in, w_out), [fy, fxy, fzy, fzxy], fy, width, rank, False)

    up = plus(up, over_half(up))
    got = over_y(theirs)
    back = (back + got[:, hidden:].astype(F32)).astype(BF)
    backs = [back, over_x(back), over_low(back), over_xlow(back)]
    cross_up = got[:, :hidden]
    cross_up = plus(cross_up, over_half(cross_up))
    ups = [up, over_x(up), over_low(up), over_xlow(up)]
    down = down_quarter(backs, [own, fx, fz, fzx], width)
    down = plus(down, over_half(down))
    cross_up = jnp.concatenate([cross_up, down], axis=1)
    crosses = [cross_up, over_x(cross_up), over_low(cross_up), over_xlow(cross_up)]
    up_gradient, down_gradient = spread(ups, crosses, block)
    return (down_gradient.transpose(0, 2, 1), up_gradient)


def gathered(frames, gain, first, second, down_map, up_map, lengths, cotangent):
    members = lax.axis_size("member")
    normed = normalize(frames[0], gain)
    low = dot(normed, down_map[0]).astype(BF)
    positions = jnp.arange(BUCKET, dtype=jnp.int32)
    mask = (positions[None, :] < lengths[0][:, None]).reshape(-1)
    masked = cotangent[0] * mask.astype(BF)[:, None]
    rows = normed.shape[0]
    up_slices = lax.all_to_all(up_map, "member", split_axis=2, concat_axis=0, tiled=True)
    all_normed = lax.all_gather(normed, "member", axis=0, tiled=True)
    all_low = lax.all_gather(low, "member", axis=0, tiled=True).reshape(members, rows, -1)
    all_masked = lax.all_gather(masked, "member", axis=0, tiled=True)
    term = jnp.einsum("dgs,dsb->dgb", all_low, up_slices, preferred_element_type=F32)
    pre = term.reshape(members * rows, -1) + dot(
        all_normed, lax.all_gather(first, "fsdp", axis=0, tiled=True)
    )
    dhid = 0.5 * dot(all_masked, lax.all_gather(second, "fsdp", axis=1, tiled=True), ((1,), (1,)))
    dpre = swish_gradient(pre, dhid).reshape(members, rows, -1)
    up_partial = jnp.einsum("jnz,jnv->jzv", all_low, dpre, preferred_element_type=F32)
    back_partial = jnp.einsum("yha,ywa->yhw", dpre, up_slices, preferred_element_type=F32)
    back = lax.psum_scatter(back_partial, "member", scatter_dimension=0, tiled=True)[0].astype(BF)
    up = lax.all_to_all(lax.psum(up_partial, "fsdp"), "member", split_axis=0, concat_axis=2, tiled=True)
    down = lax.psum(dot(normed, back, ((0,), (0,))), "fsdp")
    return (down[None], up)


def solution(mesh):
    in_specs = (
        P("member", "fsdp", None),
        P(),
        P("fsdp", "member"),
        P("member", "fsdp"),
        P("member", None, None),
        P("member", None, None),
        P("member", "fsdp"),
        P("member", "fsdp", None),
    )
    out_specs = (P("member", None, None), P("member", None, None))
    paired = mesh.shape["fsdp"] == 8 and mesh.shape["member"] == 4
    return jax.shard_map(
        paired_halves if paired else gathered,
        mesh=mesh,
        in_specs=in_specs,
        out_specs=out_specs,
        check_vma=False,
    )
```

time: 155 us -> 124 us (0.80)
  local copies, waits for them, and re-layouts: 17.2 us -> 0.15 us
  starting transfers between devices: 38.3 us -> 30.9 us
  other arithmetic: 6.48 us -> 0.36 us
    ppermute x27 -> x29, starting transfers between devices: 38.3 us -> 30.9 us  [flip(): lax.ppermute(value, axis, [(i, i ^ bits) for i in range(size)])]
    unnamed x53 -> x6, local copies, waits for them, and re-layouts: 7.31 us -> 0.02 us
    another operation x6 -> x1, local copies, waits for them, and re-layouts: 3.95 us -> 0.06 us  [paired_halves(): near = over_core(jnp.stack([w00, wx0, z2n, z3n]))]
    another operation x4 -> x3, other arithmetic: 3.61 us -> 0.26 us  [the longest x1 0.15 us: paired_halves(): near = over_core(jnp.stack([w00, wx0, z2n, z3n]))]
    gather x1 -> x0, local copies, waits for them, and re-layouts: 3.22 us -> none  [paired_halves(): jnp.take(jnp.stack([v[:, :width] for v in (own, fx, fz, fzx)]), slots, ax...]
    slice x3 -> x2, local copies, waits for them, and re-layouts: 2.67 us -> 0.06 us  [the longest x1 0.06 us: paired_halves(): fzxy, fxy = (over_x(after(fzy, *two)), over_y(after(fx[:rows], *two)))]
    select_n x2 -> x0, other arithmetic: 1.62 us -> none  [paired_halves(): jnp.take(jnp.stack([v[:, :width] for v in (own, fx, fz, fzx)]), slots, ax...]
    ppermute x27 -> x29, waiting for transfers between devices: 74.7 us -> 74.8 us  [flip(): lax.ppermute(value, axis, [(i, i ^ bits) for i in range(size)])]
  transfers between devices with their start and end apart: 27 -> 29, of which waited for: 12 -> 18; matrix products, arithmetic and copies ran while one was open for 11% -> 0% of each run, Pallas kernels for 5% -> 5%
where the time goes in v3:
time: 124 us
  waiting for transfers between devices  74.8 us (60%)
  starting transfers between devices  30.9 us (25%)
  Pallas kernels  15.9 us (13%)
  between operations  1.48 us (1%)
    ppermute x29, waiting for transfers between devices, flip(): lax.ppermute(value, axis, [(i, i ^ bits) for i in range(size)])  74.8 us
    ppermute x29, starting transfers between devices, flip(): lax.ppermute(value, axis, [(i, i ^ bits) for i in range(size)])  30.9 us
    pallas_call x5, Pallas kernels, call(): pl.pallas_call(body, in_specs=ins, out_specs=[whole(o.shape) for o in out...  15.9 us
  transfers between devices with their start and end apart: 29, of which 18 were waited for; matrix products, arithmetic and copies ran while one was open for 0% of the time, Pallas kernels for 5%

profile of v3, /device:TPU:0, one launch (start us, length us, event | category | flops | bytes accessed | tf_op | source)
XLA Modules:
  0.0 123.5 jit_solution(14613927033166274116)
XLA Ops:
  1.3 4.5 %shard_map.95 = (bf16[128,3200]{1,0:T(8,128)(2,1)}, bf16[144,3200]{1,0:T(8,128)(2,1)}, bf16[224,3200]{1,0:T(8,128)(2,1)}, bf16[96,1536]{1,0:T(8,128)(2,1)}, bf16[96,1536]{1,0:T(8,128)(2,1)}) custom-call(bf16[1,144,1536]{2,1,0:T(8,128)(2,1)} %frames_ref.1, f32[1536]{0:T(1024)} %gain_ref.1, bf16[192,1536]{1,0:T(8,128)(2,1)} %first_ref.1, ...), custom_call_target="tpu_custom_call" | custom-call | tf_op jit(solution)/shard_map/pallas_call | solution.py:48
  5.8 3.0 %collective-permute-start = (bf16[224,3200]{1,0:T(8,128)(2,1)}, bf16[224,3200]{1,0:T(8,128)(2,1)S(1)}, u32[]{:S(2)}, u32[]{:S(2)}) collective-permute-start(bf16[224,3200]{1,0:T(8,128)(2,1)} %get-tuple-element.20), channel_id=1, source_target_pairs={{0,4},{4,0},{8,12},{12,8},{16,20},{20,16},{24,28},{28,24},{1,5},{5... | collective-permute-start | bytes 4300808 | tf_op jit(solution)/shard_map/ppermute | solution.py:31
  8.8 1.5 %collective-permute-start.3 = (bf16[144,3200]{1,0:T(8,128)(2,1)}, bf16[144,3200]{1,0:T(8,128)(2,1)S(1)}, u32[]{:S(2)}, u32[]{:S(2)}) collective-permute-start(bf16[144,3200]{1,0:T(8,128)(2,1)} %get-tuple-element.22), channel_id=1, source_target_pairs={{0,2},{1,3},{2,0},{3,1},{4,6},{5,7},{6,4},{7,5},{8,10},{9,11},{10,... | collective-permute-start | bytes 2764808 | tf_op jit(solution)/shard_map/ppermute | solution.py:31
  10.3 1.6 %collective-permute-start.4 = (bf16[128,3200]{1,0:T(8,128)(2,1)}, bf16[128,3200]{1,0:T(8,128)(2,1)S(1)}, u32[]{:S(2)}, u32[]{:S(2)}) collective-permute-start(bf16[128,3200]{1,0:T(8,128)(2,1)} %get-tuple-element.23.refs_11_.refs_4_), channel_id=1, source_target_pairs={{0,8},{4,12},{8,0},{12,4},{16,24},{20,28},{24,16},{28,20},{1,9},{5... | collective-permute-start | bytes 2457608 | tf_op jit(solution)/shard_map/ppermute | solution.py:31
  11.9 2.6 %collective-permute-start.1 = (bf16[96,1536]{1,0:T(8,128)(2,1)}, bf16[96,1536]{1,0:T(8,128)(2,1)S(1)}, u32[]{:S(2)}, u32[]{:S(2)}) collective-permute-start(bf16[96,1536]{1,0:T(8,128)(2,1)} %get-tuple-element.19.refs_0_), channel_id=1, source_target_pairs={{0,16},{4,20},{8,24},{12,28},{16,0},{20,4},{24,8},{28,12},{1,17},{... | collective-permute-start | bytes 884744 | tf_op jit(solution)/shard_map/ppermute | solution.py:31
  14.7 22.5 %collective-permute-done.1.refs_2_ = bf16[96,1536]{1,0:T(8,128)(2,1)S(1)} collective-permute-done((bf16[96,1536]{1,0:T(8,128)(2,1)}, bf16[96,1536]{1,0:T(8,128)(2,1)S(1)}, u32[]{:S(2)}, u32[]{:S(2)}) %collective-permute-start.1) | collective-permute-done | bytes 294944 | tf_op jit(solution)/shard_map/ppermute | solution.py:31
  37.3 7.4 %collective-permute-done.2.refs_3_ = bf16[96,1536]{1,0:T(8,128)(2,1)S(1)} collective-permute-done((bf16[96,1536]{1,0:T(8,128)(2,1)}, bf16[96,1536]{1,0:T(8,128)(2,1)S(1)}, u32[]{:S(2)}, u32[]{:S(2)}) %collective-permute-start.2) | collective-permute-done | bytes 294944 | tf_op jit(solution)/shard_map/ppermute | solution.py:31
  45.8 2.2 %collective-permute-start.6 = (bf16[96,1536]{1,0:T(8,128)(2,1)S(1)}, bf16[96,1536]{1,0:T(8,128)(2,1)S(1)}, u32[]{:S(2)}, u32[]{:S(2)}) collective-permute-start(bf16[96,1536]{1,0:T(8,128)(2,1)S(1)} %get-tuple-element.25.refs_1_), channel_id=1, source_target_pairs={{0,16},{4,20},{8,24},{12,28},{16,0},{20,4},{24,8},{28,12},{1,17},{... | collective-permute-start | bytes 884744 | tf_op jit(solution)/shard_map/ppermute | solution.py:31
  48.2 10.6 %collective-permute-done.5.refs_4_ = bf16[96,1536]{1,0:T(8,128)(2,1)S(1)} collective-permute-done((bf16[96,1536]{1,0:T(8,128)(2,1)}, bf16[96,1536]{1,0:T(8,128)(2,1)S(1)}, u32[]{:S(2)}, u32[]{:S(2)}) %collective-permute-start.5) | collective-permute-done | bytes 294944 | tf_op jit(solution)/shard_map/ppermute | solution.py:31
  59.9 3.3 %collective-permute-done.7.refs_14_.refs_7_ = bf16[128,3200]{1,0:T(8,128)(2,1)S(1)} collective-permute-done((bf16[128,3200]{1,0:T(8,128)(2,1)S(1)}, bf16[128,3200]{1,0:T(8,128)(2,1)S(1)}, u32[]{:S(2)}, u32[]{:S(2)}) %collective-permute-start.7) | collective-permute-done | bytes 819232 | tf_op jit(solution)/shard_map/ppermute | solution.py:31
  63.5 1.6 %collective-permute-start.10 = (bf16[96,1536]{1,0:T(8,128)(2,1)S(1)}, bf16[96,1536]{1,0:T(8,128)(2,1)S(1)}, u32[]{:S(2)}, u32[]{:S(2)}) collective-permute-start(bf16[96,1536]{1,0:T(8,128)(2,1)S(1)} %get-tuple-element.27), channel_id=1, source_target_pairs={{0,24},{4,28},{8,16},{12,20},{16,8},{20,12},{24,0},{28,4},{1,25},{... | collective-permute-start | bytes 884744 | tf_op jit(solution)/shard_map/ppermute | solution.py:31
  65.3 1.6 %collective-permute-start.18 = (bf16[128,3200]{1,0:T(8,128)(2,1)S(1)}, bf16[128,3200]{1,0:T(8,128)(2,1)S(1)}, u32[]{:S(2)}, u32[]{:S(2)}) collective-permute-start(bf16[128,3200]{1,0:T(8,128)(2,1)S(1)} %slice.22), channel_id=1, source_target_pairs={{0,2},{1,3},{2,0},{3,1},{4,6},{5,7},{6,4},{7,5},{8,10},{9,11},{10,... | collective-permute-start | bytes 2457608 | tf_op jit(solution)/shard_map/ppermute | solution.py:31
  66.9 9.3 %collective-permute-done.9.refs_6_ = bf16[96,1536]{1,0:T(8,128)(2,1)S(1)} collective-permute-done((bf16[96,1536]{1,0:T(8,128)(2,1)S(1)}, bf16[96,1536]{1,0:T(8,128)(2,1)S(1)}, u32[]{:S(2)}, u32[]{:S(2)}) %collective-permute-start.9) | collective-permute-done | bytes 294944 | tf_op jit(solution)/shard_map/ppermute | solution.py:31
  76.2 1.1 collective-permute-start.19
  77.5 2.0 %collective-permute-done.13.refs_10_ = bf16[2,96,1536]{2,1,0:T(8,128)(2,1)S(1)} collective-permute-done((bf16[2,96,1536]{2,1,0:T(8,128)(2,1)S(1)}, bf16[2,96,1536]{2,1,0:T(8,128)(2,1)S(1)}, u32[]{:S(2)}, u32[]{:S(2)}) %collective-permute-start.13) | collective-permute-done | bytes 589856 | tf_op jit(solution)/shard_map/ppermute | solution.py:31
  79.5 5.5 %shard_map.96 = (bf16[64,768]{1,0:T(8,128)(2,1)S(1)}, f32[64,512]{1,0:T(8,128)S(1)}, bf16[1536,768]{1,0:T(8,128)(2,1)S(1)}, bf16[1536,768]{1,0:T(8,128)(2,1)S(1)}) custom-call(bf16[96,1536]{1,0:T(8,128)(2,1)S(1)} %copy-done.2, bf16[96,1536]{1,0:T(8,128)(2,1)S(1)} %get-tuple-element.25.refs_1_, bf16[96,1536]{1,0:T(8,128)(2,1)S(1)} %collective-permute-done.1.refs_2_, ...), custom_call_target="tpu_custom_call" | custom-call | tf_op jit(solution)/shard_map/pallas_call | solution.py:48
  86.0 2.6 %collective-permute-done.19.refs_5_ = bf16[128,3200]{1,0:T(8,128)(2,1)S(1)} collective-permute-done((bf16[128,3200]{1,0:T(8,128)(2,1)S(1)}, bf16[128,3200]{1,0:T(8,128)(2,1)S(1)}, u32[]{:S(2)}, u32[]{:S(2)}) %collective-permute-start.19) | collective-permute-done | bytes 819232 | tf_op jit(solution)/shard_map/ppermute | solution.py:31
  88.6 4.1 %shard_map.97 = bf16[64,1280]{1,0:T(8,128)(2,1)S(1)} custom-call(bf16[1536,768]{1,0:T(8,128)(2,1)S(1)} %get-tuple-element.29.refs_0_, bf16[1536,768]{1,0:T(8,128)(2,1)S(1)} %get-tuple-element.30.refs_1_, bf16[144,3200]{1,0:T(8,128)(2,1)S(1)} %collective-permute-done.3.refs_2_.refs_6_, bf16[128,3200]{1,0:T(8,128)(2,1)S(1)} %collective-permute-done.18.refs_3_, ...), custom_call_target="tpu_custom_call" | custom-call | tf_op jit(solution)/shard_map/pallas_call | solution.py:48
  93.7 4.3 %collective-permute-done.20 = bf16[64,1280]{1,0:T(8,128)(2,1)S(1)} collective-permute-done((bf16[64,1280]{1,0:T(8,128)(2,1)S(1)}, bf16[64,1280]{1,0:T(8,128)(2,1)S(1)}, u32[]{:S(2)}, u32[]{:S(2)}) %collective-permute-start.20) | collective-permute-done | bytes 163872 | tf_op jit(solution)/shard_map/ppermute | solution.py:31
  98.0 1.2 collective-permute-start.22
  99.2 2.4 %collective-permute-start.24 = (bf16[64,512]{1,0:T(8,128)(2,1)S(1)}, bf16[64,512]{1,0:T(8,128)(2,1)S(1)}, u32[]{:S(2)}, u32[]{:S(2)}) collective-permute-start(bf16[64,512]{1,0:T(8,128)(2,1)S(1)} %add_convert_fusion.2.refs_0_), channel_id=1, source_target_pairs={{0,12},{4,8},{8,4},{12,0},{16,28},{20,24},{24,20},{28,16},{1,13},{... | collective-permute-start | bytes 196616 | tf_op jit(solution)/shard_map/ppermute | solution.py:31
  101.7 1.3 %collective-permute-start.15 = (bf16[64,768]{1,0:T(8,128)(2,1)S(1)}, bf16[64,768]{1,0:T(8,128)(2,1)S(1)}, u32[]{:S(2)}, u32[]{:S(2)}) collective-permute-start(bf16[64,768]{1,0:T(8,128)(2,1)S(1)} %add_convert_fusion.1.refs_0_), channel_id=1, source_target_pairs={{0,4},{4,0},{8,12},{12,8},{16,20},{20,16},{24,28},{28,24},{1,5},{5... | collective-permute-start | bytes 294920 | tf_op jit(solution)/shard_map/ppermute | solution.py:31
  104.9 1.4 %collective-permute-start.25 = (bf16[64,384]{1,0:T(8,128)(2,1)S(1)}, bf16[64,384]{1,0:T(8,128)(2,1)S(1)}, u32[]{:S(2)}, u32[]{:S(2)}) collective-permute-start(bf16[64,384]{1,0:T(8,128)(2,1)S(1)} %shard_map.98), channel_id=1, source_target_pairs={{0,16},{4,20},{8,24},{12,28},{16,0},{20,4},{24,8},{28,12},{1,17},{... | collective-permute-start | bytes 147464 | tf_op jit(solution)/shard_map/ppermute | solution.py:31
  106.3 1.4 %collective-permute-done.21 = bf16[64,768]{1,0:T(8,128)(2,1)S(1)} collective-permute-done((bf16[64,768]{1,0:T(8,128)(2,1)S(1)}, bf16[64,768]{1,0:T(8,128)(2,1)S(1)}, u32[]{:S(2)}, u32[]{:S(2)}) %collective-permute-start.21) | collective-permute-done | bytes 98336 | tf_op jit(solution)/shard_map/ppermute | solution.py:31
  107.7 2.3 %collective-permute-done.25 = bf16[64,384]{1,0:T(8,128)(2,1)S(1)} collective-permute-done((bf16[64,384]{1,0:T(8,128)(2,1)S(1)}, bf16[64,384]{1,0:T(8,128)(2,1)S(1)}, u32[]{:S(2)}, u32[]{:S(2)}) %collective-permute-start.25) | collective-permute-done | bytes 49184 | tf_op jit(solution)/shard_map/ppermute | solution.py:31
  110.1 1.2 collective-permute-start.26
  111.3 2.7 %collective-permute-start.27 = (bf16[64,1152]{1,0:T(8,128)(2,1)S(1)}, bf16[64,1152]{1,0:T(8,128)(2,1)S(1)}, u32[]{:S(2)}, u32[]{:S(2)}) collective-permute-start(bf16[64,1152]{1,0:T(8,128)(2,1)S(1)} %pad_maximum_fusion.3.refs_4_), channel_id=1, source_target_pairs={{0,8},{4,12},{8,0},{12,4},{16,24},{20,28},{24,16},{28,20},{1,9},{5... | collective-permute-start | bytes 442376 | tf_op jit(solution)/shard_map/ppermute | solution.py:31
  113.9 1.8 %collective-permute-start.16 = (bf16[64,768]{1,0:T(8,128)(2,1)S(1)}, bf16[64,768]{1,0:T(8,128)(2,1)S(1)}, u32[]{:S(2)}, u32[]{:S(2)}) collective-permute-start(bf16[64,768]{1,0:T(8,128)(2,1)S(1)} %add_convert_fusion.1.refs_0_), channel_id=1, source_target_pairs={{0,8},{4,12},{8,0},{12,4},{16,24},{20,28},{24,16},{28,20},{1,9},{5... | collective-permute-start | bytes 294920 | tf_op jit(solution)/shard_map/ppermute | solution.py:31
  115.8 1.1 collective-permute-start.17
  116.9 3.1 %collective-permute-done.16.refs_2_ = bf16[64,768]{1,0:T(8,128)(2,1)S(1)} collective-permute-done((bf16[64,768]{1,0:T(8,128)(2,1)S(1)}, bf16[64,768]{1,0:T(8,128)(2,1)S(1)}, u32[]{:S(2)}, u32[]{:S(2)}) %collective-permute-start.16) | collective-permute-done | bytes 98336 | tf_op jit(solution)/shard_map/ppermute | solution.py:31
  119.9 2.2 %collective-permute-done.17.refs_3_ = bf16[64,768]{1,0:T(8,128)(2,1)S(1)} collective-permute-done((bf16[64,768]{1,0:T(8,128)(2,1)S(1)}, bf16[64,768]{1,0:T(8,128)(2,1)S(1)}, u32[]{:S(2)}, u32[]{:S(2)}) %collective-permute-start.17) | collective-permute-done | bytes 98336 | tf_op jit(solution)/shard_map/ppermute | solution.py:31
  122.1 1.4 %shard_map.99 = (f32[1,64,6144]{2,1,0:T(8,128)}, f32[1,64,1536]{2,1,0:T(8,128)}) custom-call(bf16[64,768]{1,0:T(8,128)(2,1)S(1)} %add_convert_fusion.1.refs_0_, bf16[64,768]{1,0:T(8,128)(2,1)S(1)} %collective-permute-done.15.refs_1_, bf16[64,768]{1,0:T(8,128)(2,1)S(1)} %collective-permute-done.16.refs_2_, ...), custom_call_target="tpu_custom_call" | custom-call | tf_op jit(solution)/shard_map/pallas_call | solution.py:48
  (48 shorter events, 7.4 us)
Async XLA Ops:
  5.8 42.2 %copy-start.2 = (bf16[96,1536]{1,0:T(8,128)(2,1)S(1)}, bf16[96,1536]{1,0:T(8,128)(2,1)}, u32[]{:S(2)}) copy-start(bf16[96,1536]{1,0:T(8,128)(2,1)} %get-tuple-element.19.refs_0_) | copy-start | bytes 884740
  5.8 38.8 %collective-permute-start = (bf16[224,3200]{1,0:T(8,128)(2,1)}, bf16[224,3200]{1,0:T(8,128)(2,1)S(1)}, u32[]{:S(2)}, u32[]{:S(2)}) collective-permute-start(bf16[224,3200]{1,0:T(8,128)(2,1)} %get-tuple-element.20), channel_id=1, source_target_pairs={{0,4},{4,0},{8,12},{12,8},{16,20},{20,16},{24,28},{28,24},{1,5},{5... | collective-permute-start | bytes 4300808 | tf_op jit(solution)/shard_map/ppermute | solution.py:31
  8.8 35.8 %collective-permute-start.3 = (bf16[144,3200]{1,0:T(8,128)(2,1)}, bf16[144,3200]{1,0:T(8,128)(2,1)S(1)}, u32[]{:S(2)}, u32[]{:S(2)}) collective-permute-start(bf16[144,3200]{1,0:T(8,128)(2,1)} %get-tuple-element.22), channel_id=1, source_target_pairs={{0,2},{1,3},{2,0},{3,1},{4,6},{5,7},{6,4},{7,5},{8,10},{9,11},{10,... | collective-permute-start | bytes 2764808 | tf_op jit(solution)/shard_map/ppermute | solution.py:31
  10.3 34.3 %collective-permute-start.4 = (bf16[128,3200]{1,0:T(8,128)(2,1)}, bf16[128,3200]{1,0:T(8,128)(2,1)S(1)}, u32[]{:S(2)}, u32[]{:S(2)}) collective-permute-start(bf16[128,3200]{1,0:T(8,128)(2,1)} %get-tuple-element.23.refs_11_.refs_4_), channel_id=1, source_target_pairs={{0,8},{4,12},{8,0},{12,4},{16,24},{20,28},{24,16},{28,20},{1,9},{5... | collective-permute-start | bytes 2457608 | tf_op jit(solution)/shard_map/ppermute | solution.py:31
  11.9 25.3 %collective-permute-start.1 = (bf16[96,1536]{1,0:T(8,128)(2,1)}, bf16[96,1536]{1,0:T(8,128)(2,1)S(1)}, u32[]{:S(2)}, u32[]{:S(2)}) collective-permute-start(bf16[96,1536]{1,0:T(8,128)(2,1)} %get-tuple-element.19.refs_0_), channel_id=1, source_target_pairs={{0,16},{4,20},{8,24},{12,28},{16,0},{20,4},{24,8},{28,12},{1,17},{... | collective-permute-start | bytes 884744 | tf_op jit(solution)/shard_map/ppermute | solution.py:31
  14.5 30.1 %collective-permute-start.2 = (bf16[96,1536]{1,0:T(8,128)(2,1)}, bf16[96,1536]{1,0:T(8,128)(2,1)S(1)}, u32[]{:S(2)}, u32[]{:S(2)}) collective-permute-start(bf16[96,1536]{1,0:T(8,128)(2,1)} %get-tuple-element.24), channel_id=1, source_target_pairs={{0,24},{4,28},{8,16},{12,20},{16,8},{20,12},{24,0},{28,4},{1,25},{... | collective-permute-start | bytes 884744 | tf_op jit(solution)/shard_map/ppermute | solution.py:31
  44.7 18.6 %collective-permute-start.7 = (bf16[128,3200]{1,0:T(8,128)(2,1)S(1)}, bf16[128,3200]{1,0:T(8,128)(2,1)S(1)}, u32[]{:S(2)}, u32[]{:S(2)}) collective-permute-start(bf16[128,3200]{1,0:T(8,128)(2,1)S(1)} %collective-permute-done.4.refs_13_.refs_6_), channel_id=1, source_target_pairs={{0,4},{4,0},{8,12},{12,8},{16,20},{20,16},{24,28},{28,24},{1,5},{5... | collective-permute-start | bytes 2457608 | tf_op jit(solution)/shard_map/ppermute | solution.py:31
  45.3 18.2 %collective-permute-start.8 = (bf16[128,3200]{1,0:T(8,128)(2,1)S(1)}, bf16[128,3200]{1,0:T(8,128)(2,1)S(1)}, u32[]{:S(2)}, u32[]{:S(2)}) collective-permute-start(bf16[128,3200]{1,0:T(8,128)(2,1)S(1)} %collective-permute-done.4.refs_13_.refs_6_), channel_id=1, source_target_pairs={{0,2},{1,3},{2,0},{3,1},{4,6},{5,7},{6,4},{7,5},{8,10},{9,11},{10,... | collective-permute-start | bytes 2457608 | tf_op jit(solution)/shard_map/ppermute | solution.py:31
  45.8 13.0 %collective-permute-start.5 = (bf16[96,1536]{1,0:T(8,128)(2,1)}, bf16[96,1536]{1,0:T(8,128)(2,1)S(1)}, u32[]{:S(2)}, u32[]{:S(2)}) collective-permute-start(bf16[96,1536]{1,0:T(8,128)(2,1)} %get-tuple-element.24), channel_id=1, source_target_pairs={{0,8},{4,12},{8,0},{12,4},{16,24},{20,28},{24,16},{28,20},{1,9},{5... | collective-permute-start | bytes 884744 | tf_op jit(solution)/shard_map/ppermute | solution.py:31
  45.8 14.0 %collective-permute-start.6 = (bf16[96,1536]{1,0:T(8,128)(2,1)S(1)}, bf16[96,1536]{1,0:T(8,128)(2,1)S(1)}, u32[]{:S(2)}, u32[]{:S(2)}) collective-permute-start(bf16[96,1536]{1,0:T(8,128)(2,1)S(1)} %get-tuple-element.25.refs_1_), channel_id=1, source_target_pairs={{0,16},{4,20},{8,24},{12,28},{16,0},{20,4},{24,8},{28,12},{1,17},{... | collective-permute-start | bytes 884744 | tf_op jit(solution)/shard_map/ppermute | solution.py:31
  48.2 29.3 %collective-permute-start.11 = (bf16[4,96,1536]{2,1,0:T(8,128)(2,1)S(1)}, bf16[4,96,1536]{2,1,0:T(8,128)(2,1)S(1)}, u32[]{:S(2)}, u32[]{:S(2)}) collective-permute-start(bf16[4,96,1536]{2,1,0:T(8,128)(2,1)S(1)} %pad_maximum_fusion), channel_id=1, source_target_pairs={{0,1},{1,0},{2,3},{3,2},{4,5},{5,4},{6,7},{7,6},{8,9},{9,8},{10,11... | collective-permute-start | bytes 3538952 | tf_op jit(solution)/shard_map/ppermute | solution.py:31
  63.5 12.7 %collective-permute-start.9 = (bf16[96,1536]{1,0:T(8,128)(2,1)S(1)}, bf16[96,1536]{1,0:T(8,128)(2,1)S(1)}, u32[]{:S(2)}, u32[]{:S(2)}) collective-permute-start(bf16[96,1536]{1,0:T(8,128)(2,1)S(1)} %get-tuple-element.27), channel_id=1, source_target_pairs={{0,8},{4,12},{8,0},{12,4},{16,24},{20,28},{24,16},{28,20},{1,9},{5... | collective-permute-start | bytes 884744 | tf_op jit(solution)/shard_map/ppermute | solution.py:31
  63.5 13.9 %collective-permute-start.10 = (bf16[96,1536]{1,0:T(8,128)(2,1)S(1)}, bf16[96,1536]{1,0:T(8,128)(2,1)S(1)}, u32[]{:S(2)}, u32[]{:S(2)}) collective-permute-start(bf16[96,1536]{1,0:T(8,128)(2,1)S(1)} %get-tuple-element.27), channel_id=1, source_target_pairs={{0,24},{4,28},{8,16},{12,20},{16,8},{20,12},{24,0},{28,4},{1,25},{... | collective-permute-start | bytes 884744 | tf_op jit(solution)/shard_map/ppermute | solution.py:31
  65.1 14.4 %copy-start = (bf16[128,3200]{1,0:T(8,128)(2,1)S(1)}, bf16[128,3200]{1,0:T(8,128)(2,1)}, u32[]{:S(2)}) copy-start(bf16[128,3200]{1,0:T(8,128)(2,1)} %get-tuple-element.23.refs_11_.refs_4_) | copy-start | bytes 2457604
  65.1 14.3 %copy-start.1 = (bf16[1,64,6144]{2,1,0:T(8,128)(2,1)S(1)}, bf16[1,64,6144]{2,1,0:T(8,128)(2,1)}, u32[]{:S(2)}) copy-start(bf16[1,64,6144]{2,1,0:T(8,128)(2,1)} %refs_15_.1) | copy-start | bytes 2359300
  65.2 12.3 %collective-permute-start.12 = (bf16[2,96,1536]{2,1,0:T(8,128)(2,1)S(1)}, bf16[2,96,1536]{2,1,0:T(8,128)(2,1)S(1)}, u32[]{:S(2)}, u32[]{:S(2)}) collective-permute-start(bf16[2,96,1536]{2,1,0:T(8,128)(2,1)S(1)} %pad_maximum_fusion.1), channel_id=1, source_target_pairs={{0,1},{1,0},{2,3},{3,2},{4,5},{5,4},{6,7},{7,6},{8,9},{9,8},{10,11... | collective-permute-start | bytes 1769480 | tf_op jit(solution)/shard_map/ppermute | solution.py:31
  65.3 20.7 %collective-permute-start.18 = (bf16[128,3200]{1,0:T(8,128)(2,1)S(1)}, bf16[128,3200]{1,0:T(8,128)(2,1)S(1)}, u32[]{:S(2)}, u32[]{:S(2)}) collective-permute-start(bf16[128,3200]{1,0:T(8,128)(2,1)S(1)} %slice.22), channel_id=1, source_target_pairs={{0,2},{1,3},{2,0},{3,1},{4,6},{5,7},{6,4},{7,5},{8,10},{9,11},{10,... | collective-permute-start | bytes 2457608 | tf_op jit(solution)/shard_map/ppermute | solution.py:31
  76.2 12.3 %collective-permute-start.19 = (bf16[128,3200]{1,0:T(8,128)(2,1)S(1)}, bf16[128,3200]{1,0:T(8,128)(2,1)S(1)}, u32[]{:S(2)}, u32[]{:S(2)}) collective-permute-start(bf16[128,3200]{1,0:T(8,128)(2,1)S(1)} %collective-permute-done.8.refs_4_), channel_id=1, source_target_pairs={{0,4},{4,0},{8,12},{12,8},{16,20},{20,16},{24,28},{28,24},{1,5},{5... | collective-permute-start | bytes 2457608 | tf_op jit(solution)/shard_map/ppermute | solution.py:31
  77.4 2.1 %collective-permute-start.13 = (bf16[2,96,1536]{2,1,0:T(8,128)(2,1)S(1)}, bf16[2,96,1536]{2,1,0:T(8,128)(2,1)S(1)}, u32[]{:S(2)}, u32[]{:S(2)}) collective-permute-start(bf16[2,96,1536]{2,1,0:T(8,128)(2,1)S(1)} %pad_maximum_fusion.2), channel_id=1, source_target_pairs={{0,1},{1,0},{2,3},{3,2},{4,5},{5,4},{6,7},{7,6},{8,9},{9,8},{10,11... | collective-permute-start | bytes 1769480 | tf_op jit(solution)/shard_map/ppermute | solution.py:31
  92.6 5.4 %collective-permute-start.20 = (bf16[64,1280]{1,0:T(8,128)(2,1)S(1)}, bf16[64,1280]{1,0:T(8,128)(2,1)S(1)}, u32[]{:S(2)}, u32[]{:S(2)}) collective-permute-start(bf16[64,1280]{1,0:T(8,128)(2,1)S(1)} %shard_map.97), channel_id=1, source_target_pairs={{0,2},{1,3},{2,0},{3,1},{4,6},{5,7},{6,4},{7,5},{8,10},{9,11},{10,... | collective-permute-start | bytes 491528 | tf_op jit(solution)/shard_map/ppermute | solution.py:31
  92.7 8.9 %collective-permute-start.14 = (bf16[64,768]{1,0:T(8,128)(2,1)S(1)}, bf16[64,768]{1,0:T(8,128)(2,1)S(1)}, u32[]{:S(2)}, u32[]{:S(2)}) collective-permute-start(bf16[64,768]{1,0:T(8,128)(2,1)S(1)} %get-tuple-element.28), channel_id=1, source_target_pairs={{0,16},{4,20},{8,24},{12,28},{16,0},{20,4},{24,8},{28,12},{1,17},{... | collective-permute-start | bytes 294920 | tf_op jit(solution)/shard_map/ppermute | solution.py:31
  98.0 5.0 %collective-permute-start.22 = (bf16[64,512]{1,0:T(8,128)(2,1)S(1)}, bf16[64,512]{1,0:T(8,128)(2,1)S(1)}, u32[]{:S(2)}, u32[]{:S(2)}) collective-permute-start(bf16[64,512]{1,0:T(8,128)(2,1)S(1)} %add_convert_fusion.2.refs_0_), channel_id=1, source_target_pairs={{0,4},{4,0},{8,12},{12,8},{16,20},{20,16},{24,28},{28,24},{1,5},{5... | collective-permute-start | bytes 196616 | tf_op jit(solution)/shard_map/ppermute | solution.py:31
  99.2 4.3 %collective-permute-start.23 = (bf16[64,512]{1,0:T(8,128)(2,1)S(1)}, bf16[64,512]{1,0:T(8,128)(2,1)S(1)}, u32[]{:S(2)}, u32[]{:S(2)}) collective-permute-start(bf16[64,512]{1,0:T(8,128)(2,1)S(1)} %add_convert_fusion.2.refs_0_), channel_id=1, source_target_pairs={{0,8},{4,12},{8,0},{12,4},{16,24},{20,28},{24,16},{28,20},{1,9},{5... | collective-permute-start | bytes 196616 | tf_op jit(solution)/shard_map/ppermute | solution.py:31
  99.2 5.3 %collective-permute-start.24 = (bf16[64,512]{1,0:T(8,128)(2,1)S(1)}, bf16[64,512]{1,0:T(8,128)(2,1)S(1)}, u32[]{:S(2)}, u32[]{:S(2)}) collective-permute-start(bf16[64,512]{1,0:T(8,128)(2,1)S(1)} %add_convert_fusion.2.refs_0_), channel_id=1, source_target_pairs={{0,12},{4,8},{8,4},{12,0},{16,28},{20,24},{24,20},{28,16},{1,13},{... | collective-permute-start | bytes 196616 | tf_op jit(solution)/shard_map/ppermute | solution.py:31
  101.6 6.1 %collective-permute-start.21 = (bf16[64,768]{1,0:T(8,128)(2,1)S(1)}, bf16[64,768]{1,0:T(8,128)(2,1)S(1)}, u32[]{:S(2)}, u32[]{:S(2)}) collective-permute-start(bf16[64,768]{1,0:T(8,128)(2,1)S(1)} %slice.23), channel_id=1, source_target_pairs={{0,16},{4,20},{8,24},{12,28},{16,0},{20,4},{24,8},{28,12},{1,17},{... | collective-permute-start | bytes 294920 | tf_op jit(solution)/shard_map/ppermute | solution.py:31
  101.7 14.0 %collective-permute-start.15 = (bf16[64,768]{1,0:T(8,128)(2,1)S(1)}, bf16[64,768]{1,0:T(8,128)(2,1)S(1)}, u32[]{:S(2)}, u32[]{:S(2)}) collective-permute-start(bf16[64,768]{1,0:T(8,128)(2,1)S(1)} %add_convert_fusion.1.refs_0_), channel_id=1, source_target_pairs={{0,4},{4,0},{8,12},{12,8},{16,20},{20,16},{24,28},{28,24},{1,5},{5... | collective-permute-start | bytes 294920 | tf_op jit(solution)/shard_map/ppermute | solution.py:31
  104.9 5.2 %collective-permute-start.25 = (bf16[64,384]{1,0:T(8,128)(2,1)S(1)}, bf16[64,384]{1,0:T(8,128)(2,1)S(1)}, u32[]{:S(2)}, u32[]{:S(2)}) collective-permute-start(bf16[64,384]{1,0:T(8,128)(2,1)S(1)} %shard_map.98), channel_id=1, source_target_pairs={{0,16},{4,20},{8,24},{12,28},{16,0},{20,4},{24,8},{28,12},{1,17},{... | collective-permute-start | bytes 147464 | tf_op jit(solution)/shard_map/ppermute | solution.py:31
  110.1 12.0 %collective-permute-start.26 = (bf16[64,1152]{1,0:T(8,128)(2,1)S(1)}, bf16[64,1152]{1,0:T(8,128)(2,1)S(1)}, u32[]{:S(2)}, u32[]{:S(2)}) collective-permute-start(bf16[64,1152]{1,0:T(8,128)(2,1)S(1)} %pad_maximum_fusion.3.refs_4_), channel_id=1, source_target_pairs={{0,4},{4,0},{8,12},{12,8},{16,20},{20,16},{24,28},{28,24},{1,5},{5... | collective-permute-start | bytes 442376 | tf_op jit(solution)/shard_map/ppermute | solution.py:31
  111.3 10.8 %collective-permute-start.27 = (bf16[64,1152]{1,0:T(8,128)(2,1)S(1)}, bf16[64,1152]{1,0:T(8,128)(2,1)S(1)}, u32[]{:S(2)}, u32[]{:S(2)}) collective-permute-start(bf16[64,1152]{1,0:T(8,128)(2,1)S(1)} %pad_maximum_fusion.3.refs_4_), channel_id=1, source_target_pairs={{0,8},{4,12},{8,0},{12,4},{16,24},{20,28},{24,16},{28,20},{1,9},{5... | collective-permute-start | bytes 442376 | tf_op jit(solution)/shard_map/ppermute | solution.py:31
  113.9 8.2 %collective-permute-start.28 = (bf16[64,1152]{1,0:T(8,128)(2,1)S(1)}, bf16[64,1152]{1,0:T(8,128)(2,1)S(1)}, u32[]{:S(2)}, u32[]{:S(2)}) collective-permute-start(bf16[64,1152]{1,0:T(8,128)(2,1)S(1)} %pad_maximum_fusion.3.refs_4_), channel_id=1, source_target_pairs={{0,12},{4,8},{8,4},{12,0},{16,28},{20,24},{24,20},{28,16},{1,13},{... | collective-permute-start | bytes 442376 | tf_op jit(solution)/shard_map/ppermute | solution.py:31
  113.9 6.0 %collective-permute-start.16 = (bf16[64,768]{1,0:T(8,128)(2,1)S(1)}, bf16[64,768]{1,0:T(8,128)(2,1)S(1)}, u32[]{:S(2)}, u32[]{:S(2)}) collective-permute-start(bf16[64,768]{1,0:T(8,128)(2,1)S(1)} %add_convert_fusion.1.refs_0_), channel_id=1, source_target_pairs={{0,8},{4,12},{8,0},{12,4},{16,24},{20,28},{24,16},{28,20},{1,9},{5... | collective-permute-start | bytes 294920 | tf_op jit(solution)/shard_map/ppermute | solution.py:31
  115.8 6.3 %collective-permute-start.17 = (bf16[64,768]{1,0:T(8,128)(2,1)S(1)}, bf16[64,768]{1,0:T(8,128)(2,1)S(1)}, u32[]{:S(2)}, u32[]{:S(2)}) collective-permute-start(bf16[64,768]{1,0:T(8,128)(2,1)S(1)} %add_convert_fusion.1.refs_0_), channel_id=1, source_target_pairs={{0,12},{4,8},{8,4},{12,0},{16,28},{20,24},{24,20},{28,16},{1,13},{... | collective-permute-start | bytes 294920 | tf_op jit(solution)/shard_map/ppermute | solution.py:31

commit v4 on v3

--- a/solution.py
+++ b/solution.py
@@ -138,6 +138,7 @@
     n_pieces, n_swapped = len(pieces), len(swapped)
     hidden = 2 * part
     count = 4 * rows
+    kind = F32 if own else BF
 
     def body(*refs):
         piece_refs, refs = refs[:n_pieces], refs[n_pieces:]
@@ -145,7 +146,7 @@
         if own:
             *frame_refs, up_ref, up_out, back_out, w_in, w_out, packed, map_ref, sems, frame_sems = refs
         else:
-            w_in, w_out, *frame_refs, up_ref, out_ref, packed, map_ref, frame_sems = refs
+            w_in, w_out, *frame_refs, up_ref, up_out, back_out, packed, map_ref, frame_sems = refs
         f, low_bit, x, y, core = place()
         slot = low_bit * 2 + x
         copies = []
@@ -189,16 +190,9 @@
             pre = dot(packed[:, :width], w_in[:, now]) + dot(low, map_ref[:, now])
             dhid = 0.5 * dot(packed[:, width : 2 * width], w_out[:, now])
             dpre = swish_gradient(pre, dhid)
-            sums = dot(low, dpre, ((0,), (0,))).astype(BF)
-            if own:
-                up_out[:, now] = sums
-            else:
-                out_ref[:, now] = sums
+            up_out[:, now] = dot(low, dpre, ((0,), (0,))).astype(BF)
             back = back + dot(map_ref[:, now], dpre, ((1,), (1,)))
-        if own:
-            back_out[...] = back
-        else:
-            out_ref[:, hidden:] = back.astype(BF)
+        back_out[...] = back.astype(kind)
 
     anywhere = pl.BlockSpec(memory_space=pl.ANY)
     scratch = [pltpu.VMEM((count, lined), BF), pltpu.VMEM((rank, hidden), BF)]
@@ -206,74 +200,74 @@
     if own:
         args = (*pieces, *swapped, *frames, up)
         ins = [anywhere] * (len(args) - 1) + [whole(up.shape)]
-        outs = [
-            jax.ShapeDtypeStruct((rank, hidden), BF),
-            jax.ShapeDtypeStruct((rank, count), F32),
-            whole_weights,
-            whole_weights,
-        ]
+        outs = [whole_weights, whole_weights]
         scratch.append(pltpu.SemaphoreType.DMA((64,)))
     else:
         args = (*weights, *frames, up)
         ins = [whole(w.shape) for w in weights] + [anywhere] * 4 + [whole(up.shape)]
-        outs = [jax.ShapeDtypeStruct((rank, hidden + count), BF)]
+        outs = []
+    sums = [jax.ShapeDtypeStruct((rank, hidden), BF), jax.ShapeDtypeStruct((rank, count), kind)]
     scratch.append(pltpu.SemaphoreType.DMA((4,)))
-    return call(body, ins, outs, args, scratch)
-
-
-def down_quarter(backs, frames, width):
+    return call(body, ins, sums + outs, args, scratch)
+
+
+def down_half(backs, frames, width):
     rank, count = backs[0].shape
-    rows, quarter = count // 4, width // 4
+    rows, half = count // 4, width // 2
+    n_backs = len(backs)
 
     def body(*refs):
-        back_refs, frame_refs, (out_ref, normed, sems) = refs[:4], refs[4:8], refs[8:]
+        back_refs, frame_refs, (out_ref, normed, sems) = refs[:n_backs], refs[n_backs:-3], refs[-3:]
         _, low_bit, x, _, _ = place()
         slot = low_bit * 2 + x
         copies = []
         for i, ref in enumerate(frame_refs):
             copies.append(
                 pltpu.make_async_copy(
-                    ref.at[pl.ds(0, rows), lanes(slot * quarter, quarter)],
+                    ref.at[pl.ds(0, rows), lanes(x * half, half)],
                     normed.at[pl.ds(pl.multiple_of((slot ^ i) * rows, 16), rows)],
                     sems.at[i],
                 )
             )
         for copy in copies:
             copy.start()
-        b, bx, bz, bzx = [ref[...].astype(F32) for ref in back_refs]
-        back = ((b + bx) + (bz + bzx)).astype(BF)
+        parts = [ref[...].astype(F32) for ref in back_refs]
+        while len(parts) > 1:
+            parts = [parts[i] + parts[i + 1] for i in range(0, len(parts), 2)]
+        back = parts[0].astype(BF)
         for copy in copies:
             copy.wait()
         out_ref[...] = dot(back, normed[...]).astype(BF)
 
     args = (*backs, *frames)
     ins = [whole(b.shape) for b in backs] + [pl.BlockSpec(memory_space=pl.ANY)] * 4
-    scratch = [pltpu.VMEM((count, quarter), BF), pltpu.SemaphoreType.DMA((4,))]
-    outs = [jax.ShapeDtypeStruct((rank, quarter), BF)]
+    scratch = [pltpu.VMEM((count, half), BF), pltpu.SemaphoreType.DMA((4,))]
+    outs = [jax.ShapeDtypeStruct((rank, half), BF)]
     return call(body, ins, outs, args, scratch)[0]
 
 
-def spread(own_parts, cross_parts, block):
-    rank, hidden = own_parts[0].shape
-    part = hidden // 2
-    quarter = cross_parts[0].shape[1] - hidden
+def spread(ups, downs, block):
+    rank, both = ups[0].shape
+    part = both // 4
+    half = downs[0].shape[1]
 
     def body(*refs):
-        own_refs, cross_refs, (up_out, down_out) = refs[:4], refs[4:8], refs[8:]
+        up_refs, down_refs, (up_out, down_out) = refs[:4], refs[4:6], refs[6:]
         _, low_bit, x, y, core = place()
         for i in range(4):
             at = ((x * 2 + low_bit) ^ ((i & 1) * 2 + (i >> 1))) * part
-            for dy, ref in enumerate((own_refs[i], cross_refs[i])):
+            for dy in range(2):
                 for dc in range(2):
                     start = ((y ^ dy) * 2 + (core ^ dc)) * block + at
-                    up_out[0, :, lanes(start, part)] = ref[:, dc * part : (dc + 1) * part].astype(F32)
-            at = ((low_bit * 2 + x) ^ i) * quarter
-            down_out[0, :, lanes(at, quarter)] = cross_refs[i][:, hidden:].astype(F32)
-
-    args = (*own_parts, *cross_parts)
+                    now = (2 * dy + dc) * part
+                    up_out[0, :, lanes(start, part)] = up_refs[i][:, now : now + part].astype(F32)
+        for i in range(2):
+            down_out[0, :, lanes((x ^ i) * half, half)] = down_refs[i][...].astype(F32)
+
+    args = (*ups, *downs)
     outs = [
         jax.ShapeDtypeStruct((1, rank, 4 * block), F32),
-        jax.ShapeDtypeStruct((1, rank, 4 * quarter), F32),
+        jax.ShapeDtypeStruct((1, rank, 2 * half), F32),
     ]
     return call(body, [whole(a.shape) for a in args], outs, args)
 
@@ -291,6 +285,7 @@
     over_half, over_both = flip("fsdp", 8, 4), flip("fsdp", 8, 6)
     over_xlow = flip("fsdp", 8, 3)
     over_y, over_core = flip("member", 4, 2), flip("member", 4, 1)
+    over_yhalf = flip(("fsdp", "member"), 32, 18)
 
     width, rank = frames.shape[2], down_map.shape[2]
     rows = -(-LMAX // 16) * 16
@@ -308,28 +303,25 @@
     fzx, fzy = over_x(after(fz, *one)), over_y(after(fz, *one))
     z1n, z2f = over_low(after(w01, *one)), over_half(after(wx0, *one))
     near = over_core(jnp.stack([w00, wx0, z2n, z3n]))
-    two = (fzx, fzy, z1n, z2f)
+    two = (fzx, fzy)
     fzxy, fxy = over_x(after(fzy, *two)), over_y(after(fx[:rows], *two))
-    z1f, z3f = over_low(after(wx1, *two)), over_both(after(wx1, *two))
+    z1f, z3f = over_low(after(wx1, *one, z1n)), over_both(after(wx1, *one, z2f))
     middle = over_core(jnp.stack([z1n, z2f]))
-    far = over_core(jnp.stack([z1f, z3f]))
-    weights = ([w00, wx0, z2n, z3n, z1n, z2f, z1f, z3f], [near, middle, far])
+    far = [over_core(z1f), over_core(z3f)]
+    weights = ([w00, wx0, z2n, z3n, z1n, z2f, z1f, z3f], [near, middle, *far])
 
     up, back, w_in, w_out = work(weights, [own, fx, fz, fzx], up_map, width, rank, True)
-    (theirs,) = work((w_in, w_out), [fy, fxy, fzy, fzxy], fy, width, rank, False)
-
-    up = plus(up, over_half(up))
-    got = over_y(theirs)
-    back = (back + got[:, hidden:].astype(F32)).astype(BF)
+    cross_up, cross_back = work((w_in, w_out), [fy, fxy, fzy, fzxy], fy, width, rank, False)
+
+    back = (back + over_y(cross_back).astype(F32)).astype(BF)
     backs = [back, over_x(back), over_low(back), over_xlow(back)]
-    cross_up = got[:, :hidden]
-    cross_up = plus(cross_up, over_half(cross_up))
+    cross_up = plus(over_y(cross_up), over_yhalf(cross_up))
+    up = jnp.concatenate([plus(up, over_half(up)), cross_up], axis=1)
+    down = down_half(backs, [own, fx, fz, fzx], width)
+    down = plus(down, over_half(down))
     ups = [up, over_x(up), over_low(up), over_xlow(up)]
-    down = down_quarter(backs, [own, fx, fz, fzx], width)
-    down = plus(down, over_half(down))
-    cross_up = jnp.concatenate([cross_up, down], axis=1)
-    crosses = [cross_up, over_x(cross_up), over_low(cross_up), over_xlow(cross_up)]
-    up_gradient, down_gradient = spread(ups, crosses, block)
+    downs = [down, over_x(down)]
+    up_gradient, down_gradient = spread(ups, downs, block)
     return (down_gradient.transpose(0, 2, 1), up_gradient)
 
 

time: 124 us -> 116 us (0.935)
  waiting for transfers between devices: 74.8 us -> 67.8 us
    ppermute x29, waiting for transfers between devices: 74.8 us -> 67.8 us  [flip(): lax.ppermute(value, axis, [(i, i ^ bits) for i in range(size)])]
  transfers between devices with their start and end apart: 29 -> 29, of which waited for: 18 -> 18; matrix products, arithmetic and copies ran while one was open for 0% -> 0% of each run, Pallas kernels for 5% -> 8%
where the time goes in v4:
time: 116 us
  waiting for transfers between devices  67.8 us (58%)
  starting transfers between devices  30.3 us (26%)
  Pallas kernels  16 us (14%)
  between operations  1.41 us (1%)
    ppermute x29, waiting for transfers between devices, flip(): lax.ppermute(value, axis, [(i, i ^ bits) for i in range(size)])  67.8 us
    ppermute x29, starting transfers between devices, flip(): lax.ppermute(value, axis, [(i, i ^ bits) for i in range(size)])  30.3 us
    pallas_call x5, Pallas kernels, call(): pl.pallas_call(body, in_specs=ins, out_specs=[whole(o.shape) for o in out...  16 us
  transfers between devices with their start and end apart: 29, of which 18 were waited for; matrix products, arithmetic and copies ran while one was open for 0% of the time, Pallas kernels for 8%

profile of v4, /device:TPU:0, one launch (start us, length us, event | category | flops | bytes accessed | tf_op | source)
XLA Modules:
  0.0 116.0 jit_solution(10560237640298693148)
XLA Ops:
  1.3 4.5 %shard_map.95 = (bf16[128,3200]{1,0:T(8,128)(2,1)}, bf16[144,3200]{1,0:T(8,128)(2,1)}, bf16[224,3200]{1,0:T(8,128)(2,1)}, bf16[96,1536]{1,0:T(8,128)(2,1)}, bf16[96,1536]{1,0:T(8,128)(2,1)}) custom-call(bf16[1,144,1536]{2,1,0:T(8,128)(2,1)} %frames_ref.1, f32[1536]{0:T(1024)} %gain_ref.1, bf16[192,1536]{1,0:T(8,128)(2,1)} %first_ref.1, ...), custom_call_target="tpu_custom_call" | custom-call | tf_op jit(solution)/shard_map/pallas_call | solution.py:48
  5.8 3.0 %collective-permute-start = (bf16[224,3200]{1,0:T(8,128)(2,1)}, bf16[224,3200]{1,0:T(8,128)(2,1)S(1)}, u32[]{:S(2)}, u32[]{:S(2)}) collective-permute-start(bf16[224,3200]{1,0:T(8,128)(2,1)} %get-tuple-element.23), channel_id=1, source_target_pairs={{0,4},{4,0},{8,12},{12,8},{16,20},{20,16},{24,28},{28,24},{1,5},{5... | collective-permute-start | bytes 4300808 | tf_op jit(solution)/shard_map/ppermute | solution.py:31
  8.8 1.5 %collective-permute-start.3 = (bf16[144,3200]{1,0:T(8,128)(2,1)}, bf16[144,3200]{1,0:T(8,128)(2,1)S(1)}, u32[]{:S(2)}, u32[]{:S(2)}) collective-permute-start(bf16[144,3200]{1,0:T(8,128)(2,1)} %get-tuple-element.25), channel_id=1, source_target_pairs={{0,2},{1,3},{2,0},{3,1},{4,6},{5,7},{6,4},{7,5},{8,10},{9,11},{10,... | collective-permute-start | bytes 2764808 | tf_op jit(solution)/shard_map/ppermute | solution.py:31
  10.3 1.6 %collective-permute-start.4 = (bf16[128,3200]{1,0:T(8,128)(2,1)}, bf16[128,3200]{1,0:T(8,128)(2,1)S(1)}, u32[]{:S(2)}, u32[]{:S(2)}) collective-permute-start(bf16[128,3200]{1,0:T(8,128)(2,1)} %get-tuple-element.26.refs_12_.refs_4_), channel_id=1, source_target_pairs={{0,8},{4,12},{8,0},{12,4},{16,24},{20,28},{24,16},{28,20},{1,9},{5... | collective-permute-start | bytes 2457608 | tf_op jit(solution)/shard_map/ppermute | solution.py:31
  11.9 2.6 %collective-permute-start.1 = (bf16[96,1536]{1,0:T(8,128)(2,1)}, bf16[96,1536]{1,0:T(8,128)(2,1)S(1)}, u32[]{:S(2)}, u32[]{:S(2)}) collective-permute-start(bf16[96,1536]{1,0:T(8,128)(2,1)} %get-tuple-element.22.refs_0_), channel_id=1, source_target_pairs={{0,16},{4,20},{8,24},{12,28},{16,0},{20,4},{24,8},{28,12},{1,17},{... | collective-permute-start | bytes 884744 | tf_op jit(solution)/shard_map/ppermute | solution.py:31
  14.7 22.5 %collective-permute-done.1.refs_2_ = bf16[96,1536]{1,0:T(8,128)(2,1)S(1)} collective-permute-done((bf16[96,1536]{1,0:T(8,128)(2,1)}, bf16[96,1536]{1,0:T(8,128)(2,1)S(1)}, u32[]{:S(2)}, u32[]{:S(2)}) %collective-permute-start.1) | collective-permute-done | bytes 294944 | tf_op jit(solution)/shard_map/ppermute | solution.py:31
  37.3 7.4 %collective-permute-done.2.refs_3_ = bf16[96,1536]{1,0:T(8,128)(2,1)S(1)} collective-permute-done((bf16[96,1536]{1,0:T(8,128)(2,1)}, bf16[96,1536]{1,0:T(8,128)(2,1)S(1)}, u32[]{:S(2)}, u32[]{:S(2)}) %collective-permute-start.2) | collective-permute-done | bytes 294944 | tf_op jit(solution)/shard_map/ppermute | solution.py:31
  45.8 2.2 %collective-permute-start.6 = (bf16[96,1536]{1,0:T(8,128)(2,1)S(1)}, bf16[96,1536]{1,0:T(8,128)(2,1)S(1)}, u32[]{:S(2)}, u32[]{:S(2)}) collective-permute-start(bf16[96,1536]{1,0:T(8,128)(2,1)S(1)} %get-tuple-element.28.refs_1_), channel_id=1, source_target_pairs={{0,16},{4,20},{8,24},{12,28},{16,0},{20,4},{24,8},{28,12},{1,17},{... | collective-permute-start | bytes 884744 | tf_op jit(solution)/shard_map/ppermute | solution.py:31
  48.2 10.6 %collective-permute-done.5.refs_4_ = bf16[96,1536]{1,0:T(8,128)(2,1)S(1)} collective-permute-done((bf16[96,1536]{1,0:T(8,128)(2,1)}, bf16[96,1536]{1,0:T(8,128)(2,1)S(1)}, u32[]{:S(2)}, u32[]{:S(2)}) %collective-permute-start.5) | collective-permute-done | bytes 294944 | tf_op jit(solution)/shard_map/ppermute | solution.py:31
  58.8 1.0 collective-permute-done.6.refs_5_
  59.9 2.4 %collective-permute-start.8 = (bf16[96,1536]{1,0:T(8,128)(2,1)S(1)}, bf16[96,1536]{1,0:T(8,128)(2,1)S(1)}, u32[]{:S(2)}, u32[]{:S(2)}) collective-permute-start(bf16[96,1536]{1,0:T(8,128)(2,1)S(1)} %get-tuple-element.30), channel_id=1, source_target_pairs={{0,24},{4,28},{8,16},{12,20},{16,8},{20,12},{24,0},{28,4},{1,25},{... | collective-permute-start | bytes 884744 | tf_op jit(solution)/shard_map/ppermute | solution.py:31
  62.3 0.9 collective-permute-done.13.refs_15_.refs_7_
  64.1 1.5 %collective-permute-start.17 = (bf16[128,3200]{1,0:T(8,128)(2,1)S(1)}, bf16[128,3200]{1,0:T(8,128)(2,1)S(1)}, u32[]{:S(2)}, u32[]{:S(2)}) collective-permute-start(bf16[128,3200]{1,0:T(8,128)(2,1)S(1)} %collective-permute-done.15.refs_4_), channel_id=1, source_target_pairs={{0,4},{4,0},{8,12},{12,8},{16,20},{20,16},{24,28},{28,24},{1,5},{5... | collective-permute-start | bytes 2457608 | tf_op jit(solution)/shard_map/ppermute | solution.py:31
  65.7 7.5 %collective-permute-done.7.refs_6_ = bf16[96,1536]{1,0:T(8,128)(2,1)S(1)} collective-permute-done((bf16[96,1536]{1,0:T(8,128)(2,1)S(1)}, bf16[96,1536]{1,0:T(8,128)(2,1)S(1)}, u32[]{:S(2)}, u32[]{:S(2)}) %collective-permute-start.7) | collective-permute-done | bytes 294944 | tf_op jit(solution)/shard_map/ppermute | solution.py:31
  73.7 1.1 collective-permute-done.11.refs_10_
  74.9 1.4 %collective-permute-done.12.refs_11_ = bf16[96,1536]{1,0:T(8,128)(2,1)S(1)} collective-permute-done((bf16[96,1536]{1,0:T(8,128)(2,1)S(1)}, bf16[96,1536]{1,0:T(8,128)(2,1)S(1)}, u32[]{:S(2)}, u32[]{:S(2)}) %collective-permute-start.12) | collective-permute-done | bytes 294944 | tf_op jit(solution)/shard_map/ppermute | solution.py:31
  76.4 5.6 %shard_map.96 = (bf16[64,768]{1,0:T(8,128)(2,1)S(1)}, f32[64,512]{1,0:T(8,128)S(1)}, bf16[1536,768]{1,0:T(8,128)(2,1)S(1)}, bf16[1536,768]{1,0:T(8,128)(2,1)S(1)}) custom-call(bf16[96,1536]{1,0:T(8,128)(2,1)S(1)} %copy-done.2, bf16[96,1536]{1,0:T(8,128)(2,1)S(1)} %get-tuple-element.28.refs_1_, bf16[96,1536]{1,0:T(8,128)(2,1)S(1)} %collective-permute-done.1.refs_2_, ...), custom_call_target="tpu_custom_call" | custom-call | tf_op jit(solution)/shard_map/pallas_call | solution.py:48
  82.8 4.1 %shard_map.97 = (bf16[64,768]{1,0:T(8,128)(2,1)S(1)}, bf16[64,512]{1,0:T(8,128)(2,1)S(1)}) custom-call(bf16[1536,768]{1,0:T(8,128)(2,1)S(1)} %get-tuple-element.33.refs_0_, bf16[1536,768]{1,0:T(8,128)(2,1)S(1)} %get-tuple-element.34.refs_1_, bf16[144,3200]{1,0:T(8,128)(2,1)S(1)} %collective-permute-done.3.refs_2_.refs_6_, ...), custom_call_target="tpu_custom_call" | custom-call | tf_op jit(solution)/shard_map/pallas_call | solution.py:48
  86.8 1.7 %collective-permute-start.23 = (bf16[64,512]{1,0:T(8,128)(2,1)S(1)}, bf16[64,512]{1,0:T(8,128)(2,1)S(1)}, u32[]{:S(2)}, u32[]{:S(2)}) collective-permute-start(bf16[64,512]{1,0:T(8,128)(2,1)S(1)} %get-tuple-element.39), channel_id=1, source_target_pairs={{0,2},{1,3},{2,0},{3,1},{4,6},{5,7},{6,4},{7,5},{8,10},{9,11},{10,... | collective-permute-start | bytes 196616 | tf_op jit(solution)/shard_map/ppermute | solution.py:31
  88.5 1.3 %collective-permute-done.14 = bf16[64,768]{1,0:T(8,128)(2,1)S(1)} collective-permute-done((bf16[64,768]{1,0:T(8,128)(2,1)S(1)}, bf16[64,768]{1,0:T(8,128)(2,1)S(1)}, u32[]{:S(2)}, u32[]{:S(2)}) %collective-permute-start.14) | collective-permute-done | bytes 98336 | tf_op jit(solution)/shard_map/ppermute | solution.py:31
  91.2 1.6 %collective-permute-start.24 = (bf16[64,512]{1,0:T(8,128)(2,1)S(1)}, bf16[64,512]{1,0:T(8,128)(2,1)S(1)}, u32[]{:S(2)}, u32[]{:S(2)}) collective-permute-start(bf16[64,512]{1,0:T(8,128)(2,1)S(1)} %add_convert_fusion.3.refs_0_), channel_id=1, source_target_pairs={{0,4},{4,0},{8,12},{12,8},{16,20},{20,16},{24,28},{28,24},{1,5},{5... | collective-permute-start | bytes 196616 | tf_op jit(solution)/shard_map/ppermute | solution.py:31
  92.8 2.0 %collective-permute-start.25 = (bf16[64,512]{1,0:T(8,128)(2,1)S(1)}, bf16[64,512]{1,0:T(8,128)(2,1)S(1)}, u32[]{:S(2)}, u32[]{:S(2)}) collective-permute-start(bf16[64,512]{1,0:T(8,128)(2,1)S(1)} %add_convert_fusion.3.refs_0_), channel_id=1, source_target_pairs={{0,8},{4,12},{8,0},{12,4},{16,24},{20,28},{24,16},{28,20},{1,9},{5... | collective-permute-start | bytes 196616 | tf_op jit(solution)/shard_map/ppermute | solution.py:31
  95.0 2.3 %collective-permute-done.19 = bf16[64,768]{1,0:T(8,128)(2,1)S(1)} collective-permute-done((bf16[64,768]{1,0:T(8,128)(2,1)S(1)}, bf16[64,768]{1,0:T(8,128)(2,1)S(1)}, u32[]{:S(2)}, u32[]{:S(2)}) %collective-permute-start.19) | collective-permute-done | bytes 98336 | tf_op jit(solution)/shard_map/ppermute | solution.py:31
  97.9 2.1 %collective-permute-done.26.refs_3_ = bf16[64,512]{1,0:T(8,128)(2,1)S(1)} collective-permute-done((bf16[64,512]{1,0:T(8,128)(2,1)S(1)}, bf16[64,512]{1,0:T(8,128)(2,1)S(1)}, u32[]{:S(2)}, u32[]{:S(2)}) %collective-permute-start.26) | collective-permute-done | bytes 65568 | tf_op jit(solution)/shard_map/ppermute | solution.py:31
  100.4 0.9 collective-permute-start.27
  101.4 0.8 collective-permute-start.20
  102.2 2.0 %collective-permute-start.21 = (bf16[64,1536]{1,0:T(8,128)(2,1)S(1)}, bf16[64,1536]{1,0:T(8,128)(2,1)S(1)}, u32[]{:S(2)}, u32[]{:S(2)}) collective-permute-start(bf16[64,1536]{1,0:T(8,128)(2,1)S(1)} %pad_maximum_fusion.2.refs_0_), channel_id=1, source_target_pairs={{0,8},{4,12},{8,0},{12,4},{16,24},{20,28},{24,16},{28,20},{1,9},{5... | collective-permute-start | bytes 589832 | tf_op jit(solution)/shard_map/ppermute | solution.py:31
  104.9 1.8 %collective-permute-done.27 = bf16[64,768]{1,0:T(8,128)(2,1)S(1)} collective-permute-done((bf16[64,768]{1,0:T(8,128)(2,1)S(1)}, bf16[64,768]{1,0:T(8,128)(2,1)S(1)}, u32[]{:S(2)}, u32[]{:S(2)}) %collective-permute-start.27) | collective-permute-done | bytes 98336 | tf_op jit(solution)/shard_map/ppermute | solution.py:31
  106.8 1.1 collective-permute-start.28
  107.9 2.8 %collective-permute-done.21.refs_2_ = bf16[64,1536]{1,0:T(8,128)(2,1)S(1)} collective-permute-done((bf16[64,1536]{1,0:T(8,128)(2,1)S(1)}, bf16[64,1536]{1,0:T(8,128)(2,1)S(1)}, u32[]{:S(2)}, u32[]{:S(2)}) %collective-permute-start.21) | collective-permute-done | bytes 196640 | tf_op jit(solution)/shard_map/ppermute | solution.py:31
  110.7 3.3 %collective-permute-done.22.refs_3_ = bf16[64,1536]{1,0:T(8,128)(2,1)S(1)} collective-permute-done((bf16[64,1536]{1,0:T(8,128)(2,1)S(1)}, bf16[64,1536]{1,0:T(8,128)(2,1)S(1)}, u32[]{:S(2)}, u32[]{:S(2)}) %collective-permute-start.22) | collective-permute-done | bytes 196640 | tf_op jit(solution)/shard_map/ppermute | solution.py:31
  114.6 1.4 %shard_map.99 = (f32[1,64,6144]{2,1,0:T(8,128)}, f32[1,64,1536]{2,1,0:T(8,128)}) custom-call(bf16[64,1536]{1,0:T(8,128)(2,1)S(1)} %pad_maximum_fusion.2.refs_0_, bf16[64,1536]{1,0:T(8,128)(2,1)S(1)} %collective-permute-done.20.refs_1_, bf16[64,1536]{1,0:T(8,128)(2,1)S(1)} %collective-permute-done.21.refs_2_, ...), custom_call_target="tpu_custom_call" | custom-call | tf_op jit(solution)/shard_map/pallas_call | solution.py:48
  (46 shorter events, 7.9 us)
Async XLA Ops:
  5.8 42.2 %copy-start.2 = (bf16[96,1536]{1,0:T(8,128)(2,1)S(1)}, bf16[96,1536]{1,0:T(8,128)(2,1)}, u32[]{:S(2)}) copy-start(bf16[96,1536]{1,0:T(8,128)(2,1)} %get-tuple-element.22.refs_0_) | copy-start | bytes 884740
  5.8 38.8 %collective-permute-start = (bf16[224,3200]{1,0:T(8,128)(2,1)}, bf16[224,3200]{1,0:T(8,128)(2,1)S(1)}, u32[]{:S(2)}, u32[]{:S(2)}) collective-permute-start(bf16[224,3200]{1,0:T(8,128)(2,1)} %get-tuple-element.23), channel_id=1, source_target_pairs={{0,4},{4,0},{8,12},{12,8},{16,20},{20,16},{24,28},{28,24},{1,5},{5... | collective-permute-start | bytes 4300808 | tf_op jit(solution)/shard_map/ppermute | solution.py:31
  8.8 35.8 %collective-permute-start.3 = (bf16[144,3200]{1,0:T(8,128)(2,1)}, bf16[144,3200]{1,0:T(8,128)(2,1)S(1)}, u32[]{:S(2)}, u32[]{:S(2)}) collective-permute-start(bf16[144,3200]{1,0:T(8,128)(2,1)} %get-tuple-element.25), channel_id=1, source_target_pairs={{0,2},{1,3},{2,0},{3,1},{4,6},{5,7},{6,4},{7,5},{8,10},{9,11},{10,... | collective-permute-start | bytes 2764808 | tf_op jit(solution)/shard_map/ppermute | solution.py:31
  10.3 34.3 %collective-permute-start.4 = (bf16[128,3200]{1,0:T(8,128)(2,1)}, bf16[128,3200]{1,0:T(8,128)(2,1)S(1)}, u32[]{:S(2)}, u32[]{:S(2)}) collective-permute-start(bf16[128,3200]{1,0:T(8,128)(2,1)} %get-tuple-element.26.refs_12_.refs_4_), channel_id=1, source_target_pairs={{0,8},{4,12},{8,0},{12,4},{16,24},{20,28},{24,16},{28,20},{1,9},{5... | collective-permute-start | bytes 2457608 | tf_op jit(solution)/shard_map/ppermute | solution.py:31
  11.9 25.3 %collective-permute-start.1 = (bf16[96,1536]{1,0:T(8,128)(2,1)}, bf16[96,1536]{1,0:T(8,128)(2,1)S(1)}, u32[]{:S(2)}, u32[]{:S(2)}) collective-permute-start(bf16[96,1536]{1,0:T(8,128)(2,1)} %get-tuple-element.22.refs_0_), channel_id=1, source_target_pairs={{0,16},{4,20},{8,24},{12,28},{16,0},{20,4},{24,8},{28,12},{1,17},{... | collective-permute-start | bytes 884744 | tf_op jit(solution)/shard_map/ppermute | solution.py:31
  14.5 30.1 %collective-permute-start.2 = (bf16[96,1536]{1,0:T(8,128)(2,1)}, bf16[96,1536]{1,0:T(8,128)(2,1)S(1)}, u32[]{:S(2)}, u32[]{:S(2)}) collective-permute-start(bf16[96,1536]{1,0:T(8,128)(2,1)} %get-tuple-element.27), channel_id=1, source_target_pairs={{0,24},{4,28},{8,16},{12,20},{16,8},{20,12},{24,0},{28,4},{1,25},{... | collective-permute-start | bytes 884744 | tf_op jit(solution)/shard_map/ppermute | solution.py:31
  44.6 18.6 %collective-permute-start.13 = (bf16[128,3200]{1,0:T(8,128)(2,1)S(1)}, bf16[128,3200]{1,0:T(8,128)(2,1)S(1)}, u32[]{:S(2)}, u32[]{:S(2)}) collective-permute-start(bf16[128,3200]{1,0:T(8,128)(2,1)S(1)} %collective-permute-done.4.refs_14_.refs_6_), channel_id=1, source_target_pairs={{0,4},{4,0},{8,12},{12,8},{16,20},{20,16},{24,28},{28,24},{1,5},{5... | collective-permute-start | bytes 2457608 | tf_op jit(solution)/shard_map/ppermute | solution.py:31
  45.2 18.4 %collective-permute-start.15 = (bf16[128,3200]{1,0:T(8,128)(2,1)S(1)}, bf16[128,3200]{1,0:T(8,128)(2,1)S(1)}, u32[]{:S(2)}, u32[]{:S(2)}) collective-permute-start(bf16[128,3200]{1,0:T(8,128)(2,1)S(1)} %collective-permute-done.4.refs_14_.refs_6_), channel_id=1, source_target_pairs={{0,2},{1,3},{2,0},{3,1},{4,6},{5,7},{6,4},{7,5},{8,10},{9,11},{10,... | collective-permute-start | bytes 2457608 | tf_op jit(solution)/shard_map/ppermute | solution.py:31
  45.8 13.0 %collective-permute-start.5 = (bf16[96,1536]{1,0:T(8,128)(2,1)}, bf16[96,1536]{1,0:T(8,128)(2,1)S(1)}, u32[]{:S(2)}, u32[]{:S(2)}) collective-permute-start(bf16[96,1536]{1,0:T(8,128)(2,1)} %get-tuple-element.27), channel_id=1, source_target_pairs={{0,8},{4,12},{8,0},{12,4},{16,24},{20,28},{24,16},{28,20},{1,9},{5... | collective-permute-start | bytes 884744 | tf_op jit(solution)/shard_map/ppermute | solution.py:31
  45.8 14.0 %collective-permute-start.6 = (bf16[96,1536]{1,0:T(8,128)(2,1)S(1)}, bf16[96,1536]{1,0:T(8,128)(2,1)S(1)}, u32[]{:S(2)}, u32[]{:S(2)}) collective-permute-start(bf16[96,1536]{1,0:T(8,128)(2,1)S(1)} %get-tuple-element.28.refs_1_), channel_id=1, source_target_pairs={{0,16},{4,20},{8,24},{12,28},{16,0},{20,4},{24,8},{28,12},{1,17},{... | collective-permute-start | bytes 884744 | tf_op jit(solution)/shard_map/ppermute | solution.py:31
  48.1 28.2 %collective-permute-start.9 = (bf16[4,96,1536]{2,1,0:T(8,128)(2,1)S(1)}, bf16[4,96,1536]{2,1,0:T(8,128)(2,1)S(1)}, u32[]{:S(2)}, u32[]{:S(2)}) collective-permute-start(bf16[4,96,1536]{2,1,0:T(8,128)(2,1)S(1)} %pad_maximum_fusion), channel_id=1, source_target_pairs={{0,1},{1,0},{2,3},{3,2},{4,5},{5,4},{6,7},{7,6},{8,9},{9,8},{10,11... | collective-permute-start | bytes 3538952 | tf_op jit(solution)/shard_map/ppermute | solution.py:31
  58.8 17.5 %copy-start = (bf16[128,3200]{1,0:T(8,128)(2,1)S(1)}, bf16[128,3200]{1,0:T(8,128)(2,1)}, u32[]{:S(2)}) copy-start(bf16[128,3200]{1,0:T(8,128)(2,1)} %get-tuple-element.26.refs_12_.refs_4_) | copy-start | bytes 2457604
  58.8 17.5 %copy-start.1 = (bf16[1,64,6144]{2,1,0:T(8,128)(2,1)S(1)}, bf16[1,64,6144]{2,1,0:T(8,128)(2,1)}, u32[]{:S(2)}) copy-start(bf16[1,64,6144]{2,1,0:T(8,128)(2,1)} %refs_16_.1) | copy-start | bytes 2359300
  58.8 14.4 %collective-permute-start.7 = (bf16[96,1536]{1,0:T(8,128)(2,1)S(1)}, bf16[96,1536]{1,0:T(8,128)(2,1)S(1)}, u32[]{:S(2)}, u32[]{:S(2)}) collective-permute-start(bf16[96,1536]{1,0:T(8,128)(2,1)S(1)} %get-tuple-element.30), channel_id=1, source_target_pairs={{0,8},{4,12},{8,0},{12,4},{16,24},{20,28},{24,16},{28,20},{1,9},{5... | collective-permute-start | bytes 884744 | tf_op jit(solution)/shard_map/ppermute | solution.py:31
  59.9 13.3 %collective-permute-start.8 = (bf16[96,1536]{1,0:T(8,128)(2,1)S(1)}, bf16[96,1536]{1,0:T(8,128)(2,1)S(1)}, u32[]{:S(2)}, u32[]{:S(2)}) collective-permute-start(bf16[96,1536]{1,0:T(8,128)(2,1)S(1)} %get-tuple-element.30), channel_id=1, source_target_pairs={{0,24},{4,28},{8,16},{12,20},{16,8},{20,12},{24,0},{28,4},{1,25},{... | collective-permute-start | bytes 884744 | tf_op jit(solution)/shard_map/ppermute | solution.py:31
  63.6 19.1 %collective-permute-start.16 = (bf16[128,3200]{1,0:T(8,128)(2,1)S(1)}, bf16[128,3200]{1,0:T(8,128)(2,1)S(1)}, u32[]{:S(2)}, u32[]{:S(2)}) collective-permute-start(bf16[128,3200]{1,0:T(8,128)(2,1)S(1)} %slice.14), channel_id=1, source_target_pairs={{0,2},{1,3},{2,0},{3,1},{4,6},{5,7},{6,4},{7,5},{8,10},{9,11},{10,... | collective-permute-start | bytes 2457608 | tf_op jit(solution)/shard_map/ppermute | solution.py:31
  64.1 18.6 %collective-permute-start.17 = (bf16[128,3200]{1,0:T(8,128)(2,1)S(1)}, bf16[128,3200]{1,0:T(8,128)(2,1)S(1)}, u32[]{:S(2)}, u32[]{:S(2)}) collective-permute-start(bf16[128,3200]{1,0:T(8,128)(2,1)S(1)} %collective-permute-done.15.refs_4_), channel_id=1, source_target_pairs={{0,4},{4,0},{8,12},{12,8},{16,20},{20,16},{24,28},{28,24},{1,5},{5... | collective-permute-start | bytes 2457608 | tf_op jit(solution)/shard_map/ppermute | solution.py:31
  73.2 1.6 %collective-permute-start.11 = (bf16[96,1536]{1,0:T(8,128)(2,1)S(1)}, bf16[96,1536]{1,0:T(8,128)(2,1)S(1)}, u32[]{:S(2)}, u32[]{:S(2)}) collective-permute-start(bf16[96,1536]{1,0:T(8,128)(2,1)S(1)} %collective-permute-done.7.refs_6_), channel_id=1, source_target_pairs={{0,1},{1,0},{2,3},{3,2},{4,5},{5,4},{6,7},{7,6},{8,9},{9,8},{10,11... | collective-permute-start | bytes 884744 | tf_op jit(solution)/shard_map/ppermute | solution.py:31
  73.2 3.2 %collective-permute-start.10 = (bf16[2,96,1536]{2,1,0:T(8,128)(2,1)S(1)}, bf16[2,96,1536]{2,1,0:T(8,128)(2,1)S(1)}, u32[]{:S(2)}, u32[]{:S(2)}) collective-permute-start(bf16[2,96,1536]{2,1,0:T(8,128)(2,1)S(1)} %pad_maximum_fusion.1), channel_id=1, source_target_pairs={{0,1},{1,0},{2,3},{3,2},{4,5},{5,4},{6,7},{7,6},{8,9},{9,8},{10,11... | collective-permute-start | bytes 1769480 | tf_op jit(solution)/shard_map/ppermute | solution.py:31
  74.8 1.6 %collective-permute-start.12 = (bf16[96,1536]{1,0:T(8,128)(2,1)S(1)}, bf16[96,1536]{1,0:T(8,128)(2,1)S(1)}, u32[]{:S(2)}, u32[]{:S(2)}) collective-permute-start(bf16[96,1536]{1,0:T(8,128)(2,1)S(1)} %collective-permute-done.8.refs_7_), channel_id=1, source_target_pairs={{0,1},{1,0},{2,3},{3,2},{4,5},{5,4},{6,7},{7,6},{8,9},{9,8},{10,11... | collective-permute-start | bytes 884744 | tf_op jit(solution)/shard_map/ppermute | solution.py:31
  82.0 7.9 %collective-permute-start.14 = (bf16[64,768]{1,0:T(8,128)(2,1)S(1)}, bf16[64,768]{1,0:T(8,128)(2,1)S(1)}, u32[]{:S(2)}, u32[]{:S(2)}) collective-permute-start(bf16[64,768]{1,0:T(8,128)(2,1)S(1)} %get-tuple-element.32), channel_id=1, source_target_pairs={{0,16},{4,20},{8,24},{12,28},{16,0},{20,4},{24,8},{28,12},{1,17},{... | collective-permute-start | bytes 294920 | tf_op jit(solution)/shard_map/ppermute | solution.py:31
  86.8 4.3 %collective-permute-start.23 = (bf16[64,512]{1,0:T(8,128)(2,1)S(1)}, bf16[64,512]{1,0:T(8,128)(2,1)S(1)}, u32[]{:S(2)}, u32[]{:S(2)}) collective-permute-start(bf16[64,512]{1,0:T(8,128)(2,1)S(1)} %get-tuple-element.39), channel_id=1, source_target_pairs={{0,2},{1,3},{2,0},{3,1},{4,6},{5,7},{6,4},{7,5},{8,10},{9,11},{10,... | collective-permute-start | bytes 196616 | tf_op jit(solution)/shard_map/ppermute | solution.py:31
  89.9 7.4 %collective-permute-start.19 = (bf16[64,768]{1,0:T(8,128)(2,1)S(1)}, bf16[64,768]{1,0:T(8,128)(2,1)S(1)}, u32[]{:S(2)}, u32[]{:S(2)}) collective-permute-start(bf16[64,768]{1,0:T(8,128)(2,1)S(1)} %get-tuple-element.37), channel_id=1, source_target_pairs={{0,18},{1,19},{2,16},{3,17},{4,22},{5,23},{6,20},{7,21},{8,26},{9,... | collective-permute-start | bytes 294920 | tf_op jit(solution)/shard_map/ppermute | solution.py:31
  90.7 6.7 %collective-permute-start.18 = (bf16[64,768]{1,0:T(8,128)(2,1)S(1)}, bf16[64,768]{1,0:T(8,128)(2,1)S(1)}, u32[]{:S(2)}, u32[]{:S(2)}) collective-permute-start(bf16[64,768]{1,0:T(8,128)(2,1)S(1)} %get-tuple-element.37), channel_id=1, source_target_pairs={{0,2},{1,3},{2,0},{3,1},{4,6},{5,7},{6,4},{7,5},{8,10},{9,11},{10,... | collective-permute-start | bytes 294920 | tf_op jit(solution)/shard_map/ppermute | solution.py:31
  91.2 6.2 %collective-permute-start.24 = (bf16[64,512]{1,0:T(8,128)(2,1)S(1)}, bf16[64,512]{1,0:T(8,128)(2,1)S(1)}, u32[]{:S(2)}, u32[]{:S(2)}) collective-permute-start(bf16[64,512]{1,0:T(8,128)(2,1)S(1)} %add_convert_fusion.3.refs_0_), channel_id=1, source_target_pairs={{0,4},{4,0},{8,12},{12,8},{16,20},{20,16},{24,28},{28,24},{1,5},{5... | collective-permute-start | bytes 196616 | tf_op jit(solution)/shard_map/ppermute | solution.py:31
  92.8 5.1 %collective-permute-start.25 = (bf16[64,512]{1,0:T(8,128)(2,1)S(1)}, bf16[64,512]{1,0:T(8,128)(2,1)S(1)}, u32[]{:S(2)}, u32[]{:S(2)}) collective-permute-start(bf16[64,512]{1,0:T(8,128)(2,1)S(1)} %add_convert_fusion.3.refs_0_), channel_id=1, source_target_pairs={{0,8},{4,12},{8,0},{12,4},{16,24},{20,28},{24,16},{28,20},{1,9},{5... | collective-permute-start | bytes 196616 | tf_op jit(solution)/shard_map/ppermute | solution.py:31
  94.8 5.2 %collective-permute-start.26 = (bf16[64,512]{1,0:T(8,128)(2,1)S(1)}, bf16[64,512]{1,0:T(8,128)(2,1)S(1)}, u32[]{:S(2)}, u32[]{:S(2)}) collective-permute-start(bf16[64,512]{1,0:T(8,128)(2,1)S(1)} %add_convert_fusion.3.refs_0_), channel_id=1, source_target_pairs={{0,12},{4,8},{8,4},{12,0},{16,28},{20,24},{24,20},{28,16},{1,13},{... | collective-permute-start | bytes 196616 | tf_op jit(solution)/shard_map/ppermute | solution.py:31
  100.4 6.3 %collective-permute-start.27 = (bf16[64,768]{1,0:T(8,128)(2,1)S(1)}, bf16[64,768]{1,0:T(8,128)(2,1)S(1)}, u32[]{:S(2)}, u32[]{:S(2)}) collective-permute-start(bf16[64,768]{1,0:T(8,128)(2,1)S(1)} %shard_map.98), channel_id=1, source_target_pairs={{0,16},{4,20},{8,24},{12,28},{16,0},{20,4},{24,8},{28,12},{1,17},{... | collective-permute-start | bytes 294920 | tf_op jit(solution)/shard_map/ppermute | solution.py:31
  101.4 6.5 %collective-permute-start.20 = (bf16[64,1536]{1,0:T(8,128)(2,1)S(1)}, bf16[64,1536]{1,0:T(8,128)(2,1)S(1)}, u32[]{:S(2)}, u32[]{:S(2)}) collective-permute-start(bf16[64,1536]{1,0:T(8,128)(2,1)S(1)} %pad_maximum_fusion.2.refs_0_), channel_id=1, source_target_pairs={{0,4},{4,0},{8,12},{12,8},{16,20},{20,16},{24,28},{28,24},{1,5},{5... | collective-permute-start | bytes 589832 | tf_op jit(solution)/shard_map/ppermute | solution.py:31
  102.2 8.5 %collective-permute-start.21 = (bf16[64,1536]{1,0:T(8,128)(2,1)S(1)}, bf16[64,1536]{1,0:T(8,128)(2,1)S(1)}, u32[]{:S(2)}, u32[]{:S(2)}) collective-permute-start(bf16[64,1536]{1,0:T(8,128)(2,1)S(1)} %pad_maximum_fusion.2.refs_0_), channel_id=1, source_target_pairs={{0,8},{4,12},{8,0},{12,4},{16,24},{20,28},{24,16},{28,20},{1,9},{5... | collective-permute-start | bytes 589832 | tf_op jit(solution)/shard_map/ppermute | solution.py:31
  104.2 9.8 %collective-permute-start.22 = (bf16[64,1536]{1,0:T(8,128)(2,1)S(1)}, bf16[64,1536]{1,0:T(8,128)(2,1)S(1)}, u32[]{:S(2)}, u32[]{:S(2)}) collective-permute-start(bf16[64,1536]{1,0:T(8,128)(2,1)S(1)} %pad_maximum_fusion.2.refs_0_), channel_id=1, source_target_pairs={{0,12},{4,8},{8,4},{12,0},{16,28},{20,24},{24,20},{28,16},{1,13},{... | collective-permute-start | bytes 589832 | tf_op jit(solution)/shard_map/ppermute | solution.py:31
  106.8 7.8 %collective-permute-start.28 = (bf16[64,768]{1,0:T(8,128)(2,1)S(1)}, bf16[64,768]{1,0:T(8,128)(2,1)S(1)}, u32[]{:S(2)}, u32[]{:S(2)}) collective-permute-start(bf16[64,768]{1,0:T(8,128)(2,1)S(1)} %add_convert_fusion.refs_4_), channel_id=1, source_target_pairs={{0,4},{4,0},{8,12},{12,8},{16,20},{20,16},{24,28},{28,24},{1,5},{5... | collective-permute-start | bytes 294920 | tf_op jit(solution)/shard_map/ppermute | solution.py:31

commit v5 on v4

--- a/solution.py
+++ b/solution.py
@@ -15,7 +15,7 @@
     values = frames.astype(F32)
     mean = jnp.mean(values, axis=1, keepdims=True)
     var = jnp.mean((values - mean) ** 2, axis=1, keepdims=True)
-    return (gain * (values - mean) / jnp.sqrt(var + 1e-05)).astype(BF)
+    return (gain * ((values - mean) * (1.0 / jnp.sqrt(var + 1e-05)))).astype(BF)
 
 
 def swish_gradient(pre, dhid):
@@ -44,15 +44,14 @@
     return pl.ds(pl.multiple_of(start, 128), size)
 
 
-def call(body, ins, outs, args, scratch=(), flops=0, size=0, vmem=40):
+def call(body, ins, outs, args, scratch=(), vmem=40, space=None):
     return pl.pallas_call(
         body,
         in_specs=ins,
-        out_specs=[whole(o.shape) for o in outs],
+        out_specs=[whole(o.shape) if space is None else pl.BlockSpec(memory_space=space) for o in outs],
         out_shape=outs,
         scratch_shapes=list(scratch),
         compiler_params=pltpu.CompilerParams(vmem_limit_bytes=vmem * 1024 * 1024),
-        cost_estimate=pl.CostEstimate(flops=flops, bytes_accessed=size, transcendentals=0),
     )(*args)
 
 
@@ -61,53 +60,60 @@
     part, half = block // 4, depth // 2
     width, rank = frames.shape[2], down_turned.shape[1]
     fold = rank // 16
-    lined = 2 * width + 2 * rank
+    lined = 2 * width
+    below = (rows + 16, rows + 16 + rank // 2)
 
     def body(frames_ref, gain_ref, first_ref, turned_ref, down_ref, up_ref, lengths_ref, cot_ref, *refs):
-        own_ref, cross_ref, side_ref, same_ref, flip_ref, block_ref, masked_ref, map_ref, sems = refs
+        outs, (block_ref, masked_ref, pieces_ref, maps_ref, in_sems, out_sems) = refs[:5], refs[5:]
+        own_ref, cross_ref, side_ref, same_ref, flip_ref = outs
         _, low_bit, x, y, core = place()
-        copies = []
+        loads, stores = [], []
 
         def load(src, dst):
-            copy = pltpu.make_async_copy(src, dst, sems.at[len(copies)])
-            copies.append(copy)
-            copy.start()
+            loads.append(pltpu.make_async_copy(src, dst, in_sems.at[len(loads)]))
+            loads[-1].start()
+
+        def store(src, dst):
+            stores.append(pltpu.make_async_copy(src, dst, out_sems.at[len(stores)]))
+            stores[-1].start()
 
         load(frames_ref.at[0, pl.ds(0, rows)], block_ref)
-        load(down_ref.at[0], map_ref)
         load(cot_ref.at[0, pl.ds(0, rows)], masked_ref)
-        for dl in (0, 1):
-            for dx in (0, 1):
+        for dx in (0, 1):
+            for dl in (0, 1):
                 start = ((x ^ dx) * 2 + (low_bit ^ dl)) * part
                 for k in range(4):
                     src = (first_ref, turned_ref)[k // 2].at[pl.ds((k % 2) * half, half), lanes(start, part)]
-                    if dx:
-                        load(src, side_ref.at[pl.ds(rows, half), pl.ds((4 * dl + k) * part, part)])
-                    else:
-                        load(src, (same_ref, flip_ref)[dl].at[:, pl.ds(k * part, part)])
+                    load(src, pieces_ref.at[2 * dx + dl, :, pl.ds(k * part, part)])
         for dc in range(2):
             start = ((1 - y) * 2 + (core ^ dc)) * block + (x * 2 + low_bit) * part
             for i in range(fold):
                 load(
                     up_ref.at[0, pl.ds(16 * i, 16), lanes(start, part)],
-                    cross_ref.at[pl.ds(rows, 16), pl.ds((2 * i + dc) * part, part)],
+                    maps_ref.at[pl.ds(0, 16), pl.ds((2 * i + dc) * part, part)],
                 )
-        cross_ref[rows:, 2 * fold * part :] = jnp.zeros((16, lined - 2 * fold * part), BF)
-        side_ref[rows:, 8 * part :] = jnp.zeros((half, lined - 8 * part), BF)
-        copies[0].wait()
-        normed = normalize(block_ref[...], gain_ref[...])
+        for i in range(2):
+            load(
+                down_ref.at[0, pl.ds(i * (rank // 2), rank // 2)],
+                maps_ref.at[pl.ds(16, rank // 2), pl.ds(i * width, width)],
+            )
+        loads[1].wait()
+        keep = lax.broadcasted_iota(jnp.int32, (rows, width), 0) < lengths_ref[0, 0]
+        masked_ref[...] = jnp.where(keep, masked_ref[...].astype(F32), 0.0).astype(BF)
         for ref in (own_ref, cross_ref, side_ref):
-            ref[:rows, :width] = normed
-        copies[1].wait()
-        low = dot(normed, map_ref[...], ((1,), (1,)))
-        low = jnp.concatenate([low, jnp.zeros_like(low)], axis=1).astype(BF)
-        copies[2].wait()
-        keep = lax.broadcasted_iota(jnp.int32, (rows, width), 0) < lengths_ref[0, 0]
-        masked = jnp.where(keep, masked_ref[...].astype(F32), 0.0).astype(BF)
+            store(masked_ref, ref.at[pl.ds(0, rows), pl.ds(width, width)])
+        for copy in loads[2:]:
+            copy.wait()
+        store(pieces_ref.at[0], same_ref)
+        store(pieces_ref.at[1], flip_ref)
+        for dl in range(2):
+            store(pieces_ref.at[2 + dl], side_ref.at[pl.ds(rows, half), pl.ds(4 * dl * part, 4 * part)])
+        store(maps_ref, cross_ref.at[pl.ds(rows, 16 + rank // 2)])
+        loads[0].wait()
+        block_ref[...] = normalize(block_ref[...], gain_ref[...])
         for ref in (own_ref, cross_ref, side_ref):
-            ref[:rows, width : 2 * width] = masked
-            ref[:rows, 2 * width :] = low
-        for copy in copies[3:]:
+            store(block_ref, ref.at[pl.ds(0, rows), pl.ds(0, width)])
+        for copy in stores:
             copy.wait()
 
     args = (frames, gain, first, turned, down_turned, up_map, lengths, cotangent)
@@ -115,25 +121,27 @@
     ins[1] = whole((width,))
     ins[6] = pl.BlockSpec(memory_space=pltpu.SMEM)
     piece = (half, 4 * part)
-    shapes = [(rows, lined), (rows + 16, lined), (rows + half, lined), piece, piece]
+    shapes = [(rows, lined), (below[1], lined), (rows + half, lined), piece, piece]
     outs = [jax.ShapeDtypeStruct(shape, BF) for shape in shapes]
     scratch = [
         pltpu.VMEM((rows, width), BF),
         pltpu.VMEM((rows, width), BF),
-        pltpu.VMEM((rank, width), BF),
-        pltpu.SemaphoreType.DMA((19 + 2 * fold,)),
+        pltpu.VMEM((4, *piece), BF),
+        pltpu.VMEM((16 + rank // 2, lined), BF),
+        pltpu.SemaphoreType.DMA((20 + 2 * fold,)),
+        pltpu.SemaphoreType.DMA((11,)),
     ]
-    return call(body, ins, outs, args, scratch, vmem=62)
-
-
-def work(weights, frames, up, width, rank, own):
+    return call(body, ins, outs, args, scratch, vmem=62, space=pltpu.HBM)
+
+
+def work(weights, frames, maps, width, rank, own):
     if own:
         pieces, swapped = weights
         depth, part = pieces[0].shape[0] * 2, pieces[0].shape[1] // 4
     else:
         pieces, swapped = [], []
         depth, part = weights[0].shape[0] // 8, weights[0].shape[1] // 2
-    rows, lined = frames[2].shape
+    rows = frames[2].shape[0]
     codes = (0, 1, 4, 6, 2, 5, 3, 7)
     n_pieces, n_swapped = len(pieces), len(swapped)
     hidden = 2 * part
@@ -144,71 +152,73 @@
         piece_refs, refs = refs[:n_pieces], refs[n_pieces:]
         swap_refs, refs = refs[:n_swapped], refs[n_swapped:]
         if own:
-            *frame_refs, up_ref, up_out, back_out, w_in, w_out, packed, map_ref, sems, frame_sems = refs
+            *frame_refs, down_ref, up_ref, up_out, back_out, w_in, w_out = refs[:10]
         else:
-            w_in, w_out, *frame_refs, up_ref, up_out, back_out, packed, map_ref, frame_sems = refs
+            w_in, w_out, *frame_refs, maps_ref, up_out, back_out = refs[:9]
+        normed, masked, down_map, up_map, sems = refs[-5:]
         f, low_bit, x, y, core = place()
         slot = low_bit * 2 + x
-        copies = []
-        for i, ref in enumerate(frame_refs):
-            at = pl.multiple_of((slot ^ i) * rows, 16)
-            copies.append(
-                pltpu.make_async_copy(ref.at[pl.ds(0, rows)], packed.at[pl.ds(at, rows)], frame_sems.at[i])
-            )
         flat = []
         for ref in swap_refs:
             flat += [ref.at[j] for j in range(ref.shape[0])] if len(ref.shape) == 3 else [ref]
-        for side, group in enumerate((piece_refs, flat)):
-            for i, ref in enumerate(group):
-                at = pl.multiple_of((f ^ codes[i]) * depth, 16)
-                for k in range(4):
-                    copies.append(
-                        pltpu.make_async_copy(
-                            ref.at[:, pl.ds(k * part, part)],
-                            (w_in, w_out)[k // 2].at[
-                                pl.ds(at + (k % 2) * (depth // 2), depth // 2), pl.ds(side * part, part)
-                            ],
-                            sems.at[len(copies) - 4],
+        copies = []
+        for k, (w, kept) in enumerate(((w_out, masked), (w_in, normed))):
+            for i, ref in enumerate(frame_refs):
+                at = pl.multiple_of((slot ^ i) * rows, 16)
+                copies.append((ref.at[pl.ds(0, rows), pl.ds((1 - k) * width, width)], kept.at[pl.ds(at, rows)]))
+            for side, group in enumerate((piece_refs, flat)):
+                for i, ref in enumerate(group):
+                    for lower in range(2):
+                        at = pl.multiple_of((f ^ codes[i]) * depth + lower * (depth // 2), 16)
+                        copies.append(
+                            (
+                                ref.at[:, pl.ds((2 * (1 - k) + lower) * part, part)],
+                                w.at[pl.ds(at, depth // 2), pl.ds(side * part, part)],
+                            )
                         )
-                    )
+        copies = [pltpu.make_async_copy(src, dst, sems.at[i]) for i, (src, dst) in enumerate(copies)]
         for copy in copies:
             copy.start()
         if own:
             for dc in range(2):
                 start = (y * 2 + (core ^ dc)) * (4 * part) + (x * 2 + low_bit) * part
-                map_ref[:, dc * part : (dc + 1) * part] = up_ref[0, :, lanes(start, part)]
+                up_map[:, dc * part : (dc + 1) * part] = up_ref[0, :, lanes(start, part)]
+            down_map[...] = down_ref[0]
         else:
             for i in range(rank // 16):
-                map_ref[16 * i : 16 * (i + 1), :] = up_ref[rows:, i * hidden : (i + 1) * hidden]
+                up_map[16 * i : 16 * (i + 1), :] = maps_ref[rows : rows + 16, i * hidden : (i + 1) * hidden]
+            for i in range(2):
+                at = i * (rank // 2)
+                down_map[at : at + rank // 2, :] = maps_ref[rows + 16 :, i * width : (i + 1) * width]
         for copy in copies:
             copy.wait()
-        step = 256 if hidden % 256 == 0 else part
-        back = jnp.zeros((rank, count), F32)
-        low = packed[:, 2 * width :][:, :rank]
-        for at in range(0, hidden, step):
-            now = slice(at, at + step)
-            pre = dot(packed[:, :width], w_in[:, now]) + dot(low, map_ref[:, now])
-            dhid = 0.5 * dot(packed[:, width : 2 * width], w_out[:, now])
-            dpre = swish_gradient(pre, dhid)
-            up_out[:, now] = dot(low, dpre, ((0,), (0,))).astype(BF)
-            back = back + dot(map_ref[:, now], dpre, ((1,), (1,)))
+        low = dot(down_map[...], normed[...], ((1,), (1,))).astype(BF)
+        pre = dot(normed[...], w_in[...]) + dot(low.T, up_map[...])
+        dhid = 0.5 * dot(masked[...], w_out[...])
+        dpre = swish_gradient(pre, dhid)
+        up_out[...] = dot(low, dpre).astype(BF)
+        back = dot(up_map[...], dpre, ((1,), (1,)))
         back_out[...] = back.astype(kind)
 
     anywhere = pl.BlockSpec(memory_space=pl.ANY)
-    scratch = [pltpu.VMEM((count, lined), BF), pltpu.VMEM((rank, hidden), BF)]
     whole_weights = jax.ShapeDtypeStruct((8 * depth, hidden), BF)
+    outs = [jax.ShapeDtypeStruct((rank, hidden), BF), jax.ShapeDtypeStruct((rank, count), kind)]
     if own:
-        args = (*pieces, *swapped, *frames, up)
-        ins = [anywhere] * (len(args) - 1) + [whole(up.shape)]
-        outs = [whole_weights, whole_weights]
-        scratch.append(pltpu.SemaphoreType.DMA((64,)))
+        args = (*pieces, *swapped, *frames, *maps)
+        ins = [anywhere] * (len(args) - 2)
+        outs += [whole_weights, whole_weights]
     else:
-        args = (*weights, *frames, up)
-        ins = [whole(w.shape) for w in weights] + [anywhere] * 4 + [whole(up.shape)]
-        outs = []
-    sums = [jax.ShapeDtypeStruct((rank, hidden), BF), jax.ShapeDtypeStruct((rank, count), kind)]
-    scratch.append(pltpu.SemaphoreType.DMA((4,)))
-    return call(body, ins, sums + outs, args, scratch)
+        args = (*weights, *frames, *maps)
+        ins = [whole(w.shape) for w in weights] + [anywhere] * 4
+    ins += [whole(a.shape) for a in maps]
+    scratch = [
+        pltpu.VMEM((count, width), BF),
+        pltpu.VMEM((count, width), BF),
+        pltpu.VMEM((rank, width), BF),
+        pltpu.VMEM((rank, hidden), BF),
+        pltpu.SemaphoreType.DMA((72 if own else 8,)),
+    ]
+    return call(body, ins, outs, args, scratch)
 
 
 def down_half(backs, frames, width):
@@ -293,15 +303,16 @@
     part = block // 4
     hidden = 2 * part
 
+    down_turned = down_map.transpose(0, 2, 1)
     own, cross, side, w00, w01 = prepare(
-        frames, gain, first, second.T, down_map.transpose(0, 2, 1), up_map, lengths, cotangent, rows
+        frames, gain, first, second.T, down_turned, up_map, lengths, cotangent, rows
     )
     fx, fy, fz = over_x(side), over_y(cross), over_low(own)
     z2n, z3n = over_half(w00), over_both(w01)
     one = (fx, fy, fz, z2n, z3n)
     wx0, wx1 = fx[rows:, : 4 * part], fx[rows:, 4 * part : 8 * part]
-    fzx, fzy = over_x(after(fz, *one)), over_y(after(fz, *one))
-    z1n, z2f = over_low(after(w01, *one)), over_half(after(wx0, *one))
+    fzx, fzy = over_x(after(fz, fx, fy)), over_y(after(fz, fx, fy))
+    z1n, z2f = over_low(after(w01, fz)), over_half(after(wx0, z2n))
     near = over_core(jnp.stack([w00, wx0, z2n, z3n]))
     two = (fzx, fzy)
     fzxy, fxy = over_x(after(fzy, *two)), over_y(after(fx[:rows], *two))
@@ -310,8 +321,8 @@
     far = [over_core(z1f), over_core(z3f)]
     weights = ([w00, wx0, z2n, z3n, z1n, z2f, z1f, z3f], [near, middle, *far])
 
-    up, back, w_in, w_out = work(weights, [own, fx, fz, fzx], up_map, width, rank, True)
-    cross_up, cross_back = work((w_in, w_out), [fy, fxy, fzy, fzxy], fy, width, rank, False)
+    up, back, w_in, w_out = work(weights, [own, fx, fz, fzx], (down_turned, up_map), width, rank, True)
+    cross_up, cross_back = work((w_in, w_out), [fy, fxy, fzy, fzxy], (fy,), width, rank, False)
 
     back = (back + over_y(cross_back).astype(F32)).astype(BF)
     backs = [back, over_x(back), over_low(back), over_xlow(back)]

time: 116 us -> 112 us (0.966)
  waiting for transfers between devices: 67.8 us -> 55.3 us
  starting transfers between devices: 30.3 us -> 38.6 us
    ppermute x29, waiting for transfers between devices: 67.8 us -> 55.3 us  [flip(): lax.ppermute(value, axis, [(i, i ^ bits) for i in range(size)])]
    ppermute x29, starting transfers between devices: 30.3 us -> 38.6 us  [flip(): lax.ppermute(value, axis, [(i, i ^ bits) for i in range(size)])]
  transfers between devices with their start and end apart: 29 -> 29, of which waited for: 18 -> 15; matrix products, arithmetic and copies ran while one was open for 0% -> 0% of each run, Pallas kernels for 8% -> 9%
where the time goes in v5:
time: 112 us
  waiting for transfers between devices  55.3 us (49%)
  starting transfers between devices  38.6 us (34%)
  Pallas kernels  16 us (14%)
  between operations  1.44 us (1%)
    ppermute x29, waiting for transfers between devices, flip(): lax.ppermute(value, axis, [(i, i ^ bits) for i in range(size)])  55.3 us
    ppermute x29, starting transfers between devices, flip(): lax.ppermute(value, axis, [(i, i ^ bits) for i in range(size)])  38.6 us
    pallas_call x5, Pallas kernels, call(): pl.pallas_call(body, in_specs=ins, out_specs=[whole(o.shape) if space is...  16 us
  transfers between devices with their start and end apart: 29, of which 15 were waited for; matrix products, arithmetic and copies ran while one was open for 0% of the time, Pallas kernels for 9%

profile of v5, /device:TPU:0, one launch (start us, length us, event | category | flops | bytes accessed | tf_op | source)
XLA Modules:
  0.0 111.8 jit_solution(7381738995444909121)
XLA Ops:
  1.3 4.1 %shard_map.95 = (bf16[128,3072]{1,0:T(8,128)(2,1)}, bf16[176,3072]{1,0:T(8,128)(2,1)}, bf16[224,3072]{1,0:T(8,128)(2,1)}, bf16[96,1536]{1,0:T(8,128)(2,1)}, bf16[96,1536]{1,0:T(8,128)(2,1)}) custom-call(bf16[1,144,1536]{2,1,0:T(8,128)(2,1)} %frames_ref.1, f32[1536]{0:T(1024)} %gain_ref.1, bf16[192,1536]{1,0:T(8,128)(2,1)} %first_ref.1, ...), custom_call_target="tpu_custom_call" | custom-call | tf_op jit(solution)/shard_map/pallas_call | solution.py:48
  5.4 3.0 %collective-permute-start = (bf16[224,3072]{1,0:T(8,128)(2,1)}, bf16[224,3072]{1,0:T(8,128)(2,1)S(1)}, u32[]{:S(2)}, u32[]{:S(2)}) collective-permute-start(bf16[224,3072]{1,0:T(8,128)(2,1)} %get-tuple-element.23), channel_id=1, source_target_pairs={{0,4},{4,0},{8,12},{12,8},{16,20},{20,16},{24,28},{28,24},{1,5},{5... | collective-permute-start | bytes 4128776 | tf_op jit(solution)/shard_map/ppermute | solution.py:31
  8.4 1.5 %collective-permute-start.6 = (bf16[176,3072]{1,0:T(8,128)(2,1)}, bf16[176,3072]{1,0:T(8,128)(2,1)S(1)}, u32[]{:S(2)}, u32[]{:S(2)}) collective-permute-start(bf16[176,3072]{1,0:T(8,128)(2,1)} %get-tuple-element.28), channel_id=1, source_target_pairs={{0,2},{1,3},{2,0},{3,1},{4,6},{5,7},{6,4},{7,5},{8,10},{9,11},{10,... | collective-permute-start | bytes 3244040 | tf_op jit(solution)/shard_map/ppermute | solution.py:31
  9.9 1.6 %collective-permute-start.3 = (bf16[128,3072]{1,0:T(8,128)(2,1)}, bf16[128,3072]{1,0:T(8,128)(2,1)S(1)}, u32[]{:S(2)}, u32[]{:S(2)}) collective-permute-start(bf16[128,3072]{1,0:T(8,128)(2,1)} %get-tuple-element.25.refs_12_.refs_4_), channel_id=1, source_target_pairs={{0,8},{4,12},{8,0},{12,4},{16,24},{20,28},{24,16},{28,20},{1,9},{5... | collective-permute-start | bytes 2359304 | tf_op jit(solution)/shard_map/ppermute | solution.py:31
  11.5 2.6 %collective-permute-start.1 = (bf16[96,1536]{1,0:T(8,128)(2,1)}, bf16[96,1536]{1,0:T(8,128)(2,1)S(1)}, u32[]{:S(2)}, u32[]{:S(2)}) collective-permute-start(bf16[96,1536]{1,0:T(8,128)(2,1)} %get-tuple-element.22.refs_0_), channel_id=1, source_target_pairs={{0,16},{4,20},{8,24},{12,28},{16,0},{20,4},{24,8},{28,12},{1,17},{... | collective-permute-start | bytes 884744 | tf_op jit(solution)/shard_map/ppermute | solution.py:31
  14.3 20.9 %collective-permute-done.3.refs_14_.refs_6_ = bf16[128,3072]{1,0:T(8,128)(2,1)S(1)} collective-permute-done((bf16[128,3072]{1,0:T(8,128)(2,1)}, bf16[128,3072]{1,0:T(8,128)(2,1)S(1)}, u32[]{:S(2)}, u32[]{:S(2)}) %collective-permute-start.3) | collective-permute-done | bytes 786464 | tf_op jit(solution)/shard_map/ppermute | solution.py:31
  35.2 3.6 %collective-permute-done.refs_13_.refs_5_ = bf16[224,3072]{1,0:T(8,128)(2,1)S(1)} collective-permute-done((bf16[224,3072]{1,0:T(8,128)(2,1)}, bf16[224,3072]{1,0:T(8,128)(2,1)S(1)}, u32[]{:S(2)}, u32[]{:S(2)}) %collective-permute-start) | collective-permute-done | bytes 1376288 | tf_op jit(solution)/shard_map/ppermute | solution.py:31
  38.8 1.7 %collective-permute-start.13 = (bf16[128,3072]{1,0:T(8,128)(2,1)S(1)}, bf16[128,3072]{1,0:T(8,128)(2,1)S(1)}, u32[]{:S(2)}, u32[]{:S(2)}) collective-permute-start(bf16[128,3072]{1,0:T(8,128)(2,1)S(1)} %collective-permute-done.3.refs_14_.refs_6_), channel_id=1, source_target_pairs={{0,4},{4,0},{8,12},{12,8},{16,20},{20,16},{24,28},{28,24},{1,5},{5... | collective-permute-start | bytes 2359304 | tf_op jit(solution)/shard_map/ppermute | solution.py:31
  40.5 1.5 %collective-permute-start.15 = (bf16[128,3072]{1,0:T(8,128)(2,1)S(1)}, bf16[128,3072]{1,0:T(8,128)(2,1)S(1)}, u32[]{:S(2)}, u32[]{:S(2)}) collective-permute-start(bf16[128,3072]{1,0:T(8,128)(2,1)S(1)} %collective-permute-done.3.refs_14_.refs_6_), channel_id=1, source_target_pairs={{0,2},{1,3},{2,0},{3,1},{4,6},{5,7},{6,4},{7,5},{8,10},{9,11},{10,... | collective-permute-start | bytes 2359304 | tf_op jit(solution)/shard_map/ppermute | solution.py:31
  42.1 3.3 %collective-permute-start.5 = (bf16[96,1536]{1,0:T(8,128)(2,1)S(1)}, bf16[96,1536]{1,0:T(8,128)(2,1)S(1)}, u32[]{:S(2)}, u32[]{:S(2)}) collective-permute-start(bf16[96,1536]{1,0:T(8,128)(2,1)S(1)} %get-tuple-element.27.refs_1_), channel_id=1, source_target_pairs={{0,16},{4,20},{8,24},{12,28},{16,0},{20,4},{24,8},{28,12},{1,17},{... | collective-permute-start | bytes 884744 | tf_op jit(solution)/shard_map/ppermute | solution.py:31
  45.7 8.1 %collective-permute-done.4.refs_4_ = bf16[96,1536]{1,0:T(8,128)(2,1)S(1)} collective-permute-done((bf16[96,1536]{1,0:T(8,128)(2,1)}, bf16[96,1536]{1,0:T(8,128)(2,1)S(1)}, u32[]{:S(2)}, u32[]{:S(2)}) %collective-permute-start.4) | collective-permute-done | bytes 294944 | tf_op jit(solution)/shard_map/ppermute | solution.py:31
  53.8 2.7 %collective-permute-done.5.refs_5_ = bf16[96,1536]{1,0:T(8,128)(2,1)S(1)} collective-permute-done((bf16[96,1536]{1,0:T(8,128)(2,1)S(1)}, bf16[96,1536]{1,0:T(8,128)(2,1)S(1)}, u32[]{:S(2)}, u32[]{:S(2)}) %collective-permute-start.5) | collective-permute-done | bytes 294944 | tf_op jit(solution)/shard_map/ppermute | solution.py:31
  56.5 5.6 %collective-permute-start.8 = (bf16[96,1536]{1,0:T(8,128)(2,1)S(1)}, bf16[96,1536]{1,0:T(8,128)(2,1)S(1)}, u32[]{:S(2)}, u32[]{:S(2)}) collective-permute-start(bf16[96,1536]{1,0:T(8,128)(2,1)S(1)} %get-tuple-element.30), channel_id=1, source_target_pairs={{0,24},{4,28},{8,16},{12,20},{16,8},{20,12},{24,0},{28,4},{1,25},{... | collective-permute-start | bytes 884744 | tf_op jit(solution)/shard_map/ppermute | solution.py:31
  62.2 0.7 collective-permute-start.16
  63.7 5.3 %collective-permute-done.8.refs_7_ = bf16[96,1536]{1,0:T(8,128)(2,1)S(1)} collective-permute-done((bf16[96,1536]{1,0:T(8,128)(2,1)S(1)}, bf16[96,1536]{1,0:T(8,128)(2,1)S(1)}, u32[]{:S(2)}, u32[]{:S(2)}) %collective-permute-start.8) | collective-permute-done | bytes 294944 | tf_op jit(solution)/shard_map/ppermute | solution.py:31
  69.5 1.9 %collective-permute-done.12.refs_11_ = bf16[96,1536]{1,0:T(8,128)(2,1)S(1)} collective-permute-done((bf16[96,1536]{1,0:T(8,128)(2,1)S(1)}, bf16[96,1536]{1,0:T(8,128)(2,1)S(1)}, u32[]{:S(2)}, u32[]{:S(2)}) %collective-permute-start.12) | collective-permute-done | bytes 294944 | tf_op jit(solution)/shard_map/ppermute | solution.py:31
  71.4 5.8 %shard_map.96 = (bf16[64,768]{1,0:T(8,128)(2,1)S(1)}, f32[64,512]{1,0:T(8,128)S(1)}, bf16[1536,768]{1,0:T(8,128)(2,1)S(1)}, bf16[1536,768]{1,0:T(8,128)(2,1)S(1)}) custom-call(bf16[96,1536]{1,0:T(8,128)(2,1)S(1)} %copy-done.2, bf16[96,1536]{1,0:T(8,128)(2,1)S(1)} %get-tuple-element.27.refs_1_, bf16[96,1536]{1,0:T(8,128)(2,1)S(1)} %collective-permute-done.1.refs_2_, ...), custom_call_target="tpu_custom_call" | custom-call | tf_op jit(solution)/shard_map/pallas_call | solution.py:48
  77.2 3.2 %collective-permute-start.14 = (bf16[64,768]{1,0:T(8,128)(2,1)S(1)}, bf16[64,768]{1,0:T(8,128)(2,1)S(1)}, u32[]{:S(2)}, u32[]{:S(2)}) collective-permute-start(bf16[64,768]{1,0:T(8,128)(2,1)S(1)} %get-tuple-element.32), channel_id=1, source_target_pairs={{0,16},{4,20},{8,24},{12,28},{16,0},{20,4},{24,8},{28,12},{1,17},{... | collective-permute-start | bytes 294920 | tf_op jit(solution)/shard_map/ppermute | solution.py:31
  80.5 4.3 %shard_map.97 = (bf16[64,768]{1,0:T(8,128)(2,1)S(1)}, bf16[64,512]{1,0:T(8,128)(2,1)S(1)}) custom-call(bf16[1536,768]{1,0:T(8,128)(2,1)S(1)} %get-tuple-element.33.refs_0_, bf16[1536,768]{1,0:T(8,128)(2,1)S(1)} %get-tuple-element.34.refs_1_, bf16[176,3072]{1,0:T(8,128)(2,1)S(1)} %collective-permute-done.6.refs_2_.refs_6_, ...), custom_call_target="tpu_custom_call" | custom-call | tf_op jit(solution)/shard_map/pallas_call | solution.py:48
  85.7 1.2 %collective-permute-start.18 = (bf16[64,768]{1,0:T(8,128)(2,1)S(1)}, bf16[64,768]{1,0:T(8,128)(2,1)S(1)}, u32[]{:S(2)}, u32[]{:S(2)}) collective-permute-start(bf16[64,768]{1,0:T(8,128)(2,1)S(1)} %get-tuple-element.37), channel_id=1, source_target_pairs={{0,2},{1,3},{2,0},{3,1},{4,6},{5,7},{6,4},{7,5},{8,10},{9,11},{10,... | collective-permute-start | bytes 294920 | tf_op jit(solution)/shard_map/ppermute | solution.py:31
  86.9 0.9 collective-permute-start.19
  87.9 1.8 %collective-permute-done.23 = bf16[64,512]{1,0:T(8,128)(2,1)S(1)} collective-permute-done((bf16[64,512]{1,0:T(8,128)(2,1)S(1)}, bf16[64,512]{1,0:T(8,128)(2,1)S(1)}, u32[]{:S(2)}, u32[]{:S(2)}) %collective-permute-start.23) | collective-permute-done | bytes 65568 | tf_op jit(solution)/shard_map/ppermute | solution.py:31
  90.3 3.0 %collective-permute-start.26 = (bf16[64,512]{1,0:T(8,128)(2,1)S(1)}, bf16[64,512]{1,0:T(8,128)(2,1)S(1)}, u32[]{:S(2)}, u32[]{:S(2)}) collective-permute-start(bf16[64,512]{1,0:T(8,128)(2,1)S(1)} %add_convert_fusion.3.refs_0_), channel_id=1, source_target_pairs={{0,12},{4,8},{8,4},{12,0},{16,28},{20,24},{24,20},{28,16},{1,13},{... | collective-permute-start | bytes 196616 | tf_op jit(solution)/shard_map/ppermute | solution.py:31
  93.3 0.8 collective-permute-done.19
  94.7 1.5 %collective-permute-done.26.refs_3_ = bf16[64,512]{1,0:T(8,128)(2,1)S(1)} collective-permute-done((bf16[64,512]{1,0:T(8,128)(2,1)S(1)}, bf16[64,512]{1,0:T(8,128)(2,1)S(1)}, u32[]{:S(2)}, u32[]{:S(2)}) %collective-permute-start.26) | collective-permute-done | bytes 65568 | tf_op jit(solution)/shard_map/ppermute | solution.py:31
  96.7 1.7 %collective-permute-start.27 = (bf16[64,768]{1,0:T(8,128)(2,1)S(1)}, bf16[64,768]{1,0:T(8,128)(2,1)S(1)}, u32[]{:S(2)}, u32[]{:S(2)}) collective-permute-start(bf16[64,768]{1,0:T(8,128)(2,1)S(1)} %shard_map.98), channel_id=1, source_target_pairs={{0,16},{4,20},{8,24},{12,28},{16,0},{20,4},{24,8},{28,12},{1,17},{... | collective-permute-start | bytes 294920 | tf_op jit(solution)/shard_map/ppermute | solution.py:31
  98.3 1.5 %collective-permute-start.20 = (bf16[64,1536]{1,0:T(8,128)(2,1)S(1)}, bf16[64,1536]{1,0:T(8,128)(2,1)S(1)}, u32[]{:S(2)}, u32[]{:S(2)}) collective-permute-start(bf16[64,1536]{1,0:T(8,128)(2,1)S(1)} %pad_maximum_fusion.2.refs_0_), channel_id=1, source_target_pairs={{0,4},{4,0},{8,12},{12,8},{16,20},{20,16},{24,28},{28,24},{1,5},{5... | collective-permute-start | bytes 589832 | tf_op jit(solution)/shard_map/ppermute | solution.py:31
  100.1 1.8 %collective-permute-start.22 = (bf16[64,1536]{1,0:T(8,128)(2,1)S(1)}, bf16[64,1536]{1,0:T(8,128)(2,1)S(1)}, u32[]{:S(2)}, u32[]{:S(2)}) collective-permute-start(bf16[64,1536]{1,0:T(8,128)(2,1)S(1)} %pad_maximum_fusion.2.refs_0_), channel_id=1, source_target_pairs={{0,12},{4,8},{8,4},{12,0},{16,28},{20,24},{24,20},{28,16},{1,13},{... | collective-permute-start | bytes 589832 | tf_op jit(solution)/shard_map/ppermute | solution.py:31
  102.5 0.9 collective-permute-start.28
  103.4 5.9 %collective-permute-done.20.refs_1_ = bf16[64,1536]{1,0:T(8,128)(2,1)S(1)} collective-permute-done((bf16[64,1536]{1,0:T(8,128)(2,1)S(1)}, bf16[64,1536]{1,0:T(8,128)(2,1)S(1)}, u32[]{:S(2)}, u32[]{:S(2)}) %collective-permute-start.20) | collective-permute-done | bytes 196640 | tf_op jit(solution)/shard_map/ppermute | solution.py:31
  109.4 1.0 collective-permute-done.28.refs_5_
  110.4 1.4 %shard_map.99 = (f32[1,64,6144]{2,1,0:T(8,128)}, f32[1,64,1536]{2,1,0:T(8,128)}) custom-call(bf16[64,1536]{1,0:T(8,128)(2,1)S(1)} %pad_maximum_fusion.2.refs_0_, bf16[64,1536]{1,0:T(8,128)(2,1)S(1)} %collective-permute-done.20.refs_1_, bf16[64,1536]{1,0:T(8,128)(2,1)S(1)} %collective-permute-done.21.refs_2_, ...), custom_call_target="tpu_custom_call" | custom-call | tf_op jit(solution)/shard_map/pallas_call | solution.py:48
  (48 shorter events, 5.5 us)
Async XLA Ops:
  5.4 40.1 %copy-start.2 = (bf16[96,1536]{1,0:T(8,128)(2,1)S(1)}, bf16[96,1536]{1,0:T(8,128)(2,1)}, u32[]{:S(2)}) copy-start(bf16[96,1536]{1,0:T(8,128)(2,1)} %get-tuple-element.22.refs_0_) | copy-start | bytes 884740
  5.4 33.4 %collective-permute-start = (bf16[224,3072]{1,0:T(8,128)(2,1)}, bf16[224,3072]{1,0:T(8,128)(2,1)S(1)}, u32[]{:S(2)}, u32[]{:S(2)}) collective-permute-start(bf16[224,3072]{1,0:T(8,128)(2,1)} %get-tuple-element.23), channel_id=1, source_target_pairs={{0,4},{4,0},{8,12},{12,8},{16,20},{20,16},{24,28},{28,24},{1,5},{5... | collective-permute-start | bytes 4128776 | tf_op jit(solution)/shard_map/ppermute | solution.py:31
  8.4 26.8 %collective-permute-start.6 = (bf16[176,3072]{1,0:T(8,128)(2,1)}, bf16[176,3072]{1,0:T(8,128)(2,1)S(1)}, u32[]{:S(2)}, u32[]{:S(2)}) collective-permute-start(bf16[176,3072]{1,0:T(8,128)(2,1)} %get-tuple-element.28), channel_id=1, source_target_pairs={{0,2},{1,3},{2,0},{3,1},{4,6},{5,7},{6,4},{7,5},{8,10},{9,11},{10,... | collective-permute-start | bytes 3244040 | tf_op jit(solution)/shard_map/ppermute | solution.py:31
  9.9 25.3 %collective-permute-start.3 = (bf16[128,3072]{1,0:T(8,128)(2,1)}, bf16[128,3072]{1,0:T(8,128)(2,1)S(1)}, u32[]{:S(2)}, u32[]{:S(2)}) collective-permute-start(bf16[128,3072]{1,0:T(8,128)(2,1)} %get-tuple-element.25.refs_12_.refs_4_), channel_id=1, source_target_pairs={{0,8},{4,12},{8,0},{12,4},{16,24},{20,28},{24,16},{28,20},{1,9},{5... | collective-permute-start | bytes 2359304 | tf_op jit(solution)/shard_map/ppermute | solution.py:31
  11.5 30.6 %collective-permute-start.1 = (bf16[96,1536]{1,0:T(8,128)(2,1)}, bf16[96,1536]{1,0:T(8,128)(2,1)S(1)}, u32[]{:S(2)}, u32[]{:S(2)}) collective-permute-start(bf16[96,1536]{1,0:T(8,128)(2,1)} %get-tuple-element.22.refs_0_), channel_id=1, source_target_pairs={{0,16},{4,20},{8,24},{12,28},{16,0},{20,4},{24,8},{28,12},{1,17},{... | collective-permute-start | bytes 884744 | tf_op jit(solution)/shard_map/ppermute | solution.py:31
  14.1 31.4 %collective-permute-start.2 = (bf16[96,1536]{1,0:T(8,128)(2,1)}, bf16[96,1536]{1,0:T(8,128)(2,1)S(1)}, u32[]{:S(2)}, u32[]{:S(2)}) collective-permute-start(bf16[96,1536]{1,0:T(8,128)(2,1)} %get-tuple-element.26), channel_id=1, source_target_pairs={{0,24},{4,28},{8,16},{12,20},{16,8},{20,12},{24,0},{28,4},{1,25},{... | collective-permute-start | bytes 884744 | tf_op jit(solution)/shard_map/ppermute | solution.py:31
  35.2 18.6 %collective-permute-start.4 = (bf16[96,1536]{1,0:T(8,128)(2,1)}, bf16[96,1536]{1,0:T(8,128)(2,1)S(1)}, u32[]{:S(2)}, u32[]{:S(2)}) collective-permute-start(bf16[96,1536]{1,0:T(8,128)(2,1)} %get-tuple-element.26), channel_id=1, source_target_pairs={{0,8},{4,12},{8,0},{12,4},{16,24},{20,28},{24,16},{28,20},{1,9},{5... | collective-permute-start | bytes 884744 | tf_op jit(solution)/shard_map/ppermute | solution.py:31
  38.8 23.4 %collective-permute-start.13 = (bf16[128,3072]{1,0:T(8,128)(2,1)S(1)}, bf16[128,3072]{1,0:T(8,128)(2,1)S(1)}, u32[]{:S(2)}, u32[]{:S(2)}) collective-permute-start(bf16[128,3072]{1,0:T(8,128)(2,1)S(1)} %collective-permute-done.3.refs_14_.refs_6_), channel_id=1, source_target_pairs={{0,4},{4,0},{8,12},{12,8},{16,20},{20,16},{24,28},{28,24},{1,5},{5... | collective-permute-start | bytes 2359304 | tf_op jit(solution)/shard_map/ppermute | solution.py:31
  40.5 21.6 %collective-permute-start.15 = (bf16[128,3072]{1,0:T(8,128)(2,1)S(1)}, bf16[128,3072]{1,0:T(8,128)(2,1)S(1)}, u32[]{:S(2)}, u32[]{:S(2)}) collective-permute-start(bf16[128,3072]{1,0:T(8,128)(2,1)S(1)} %collective-permute-done.3.refs_14_.refs_6_), channel_id=1, source_target_pairs={{0,2},{1,3},{2,0},{3,1},{4,6},{5,7},{6,4},{7,5},{8,10},{9,11},{10,... | collective-permute-start | bytes 2359304 | tf_op jit(solution)/shard_map/ppermute | solution.py:31
  42.1 14.3 %collective-permute-start.5 = (bf16[96,1536]{1,0:T(8,128)(2,1)S(1)}, bf16[96,1536]{1,0:T(8,128)(2,1)S(1)}, u32[]{:S(2)}, u32[]{:S(2)}) collective-permute-start(bf16[96,1536]{1,0:T(8,128)(2,1)S(1)} %get-tuple-element.27.refs_1_), channel_id=1, source_target_pairs={{0,16},{4,20},{8,24},{12,28},{16,0},{20,4},{24,8},{28,12},{1,17},{... | collective-permute-start | bytes 884744 | tf_op jit(solution)/shard_map/ppermute | solution.py:31
  45.6 25.8 %collective-permute-start.9 = (bf16[4,96,1536]{2,1,0:T(8,128)(2,1)S(1)}, bf16[4,96,1536]{2,1,0:T(8,128)(2,1)S(1)}, u32[]{:S(2)}, u32[]{:S(2)}) collective-permute-start(bf16[4,96,1536]{2,1,0:T(8,128)(2,1)S(1)} %pad_maximum_fusion), channel_id=1, source_target_pairs={{0,1},{1,0},{2,3},{3,2},{4,5},{5,4},{6,7},{7,6},{8,9},{9,8},{10,11... | collective-permute-start | bytes 3538952 | tf_op jit(solution)/shard_map/ppermute | solution.py:31
  53.8 17.6 %copy-start.1 = (bf16[128,3072]{1,0:T(8,128)(2,1)S(1)}, bf16[128,3072]{1,0:T(8,128)(2,1)}, u32[]{:S(2)}) copy-start(bf16[128,3072]{1,0:T(8,128)(2,1)} %get-tuple-element.25.refs_12_.refs_4_) | copy-start | bytes 2359300
  53.8 17.6 %copy-start.3 = (bf16[1,1536,64]{1,2,0:T(8,128)(2,1)S(1)}, bf16[1,1536,64]{1,2,0:T(8,128)(2,1)}, u32[]{:S(2)}) copy-start(bf16[1,1536,64]{1,2,0:T(8,128)(2,1)} %param.12) | copy-start | bytes 589828
  53.8 9.9 %collective-permute-start.7 = (bf16[96,1536]{1,0:T(8,128)(2,1)S(1)}, bf16[96,1536]{1,0:T(8,128)(2,1)S(1)}, u32[]{:S(2)}, u32[]{:S(2)}) collective-permute-start(bf16[96,1536]{1,0:T(8,128)(2,1)S(1)} %get-tuple-element.30), channel_id=1, source_target_pairs={{0,8},{4,12},{8,0},{12,4},{16,24},{20,28},{24,16},{28,20},{1,9},{5... | collective-permute-start | bytes 884744 | tf_op jit(solution)/shard_map/ppermute | solution.py:31
  56.5 12.5 %collective-permute-start.8 = (bf16[96,1536]{1,0:T(8,128)(2,1)S(1)}, bf16[96,1536]{1,0:T(8,128)(2,1)S(1)}, u32[]{:S(2)}, u32[]{:S(2)}) collective-permute-start(bf16[96,1536]{1,0:T(8,128)(2,1)S(1)} %get-tuple-element.30), channel_id=1, source_target_pairs={{0,24},{4,28},{8,16},{12,20},{16,8},{20,12},{24,0},{28,4},{1,25},{... | collective-permute-start | bytes 884744 | tf_op jit(solution)/shard_map/ppermute | solution.py:31
  62.2 18.3 %collective-permute-start.16 = (bf16[128,3072]{1,0:T(8,128)(2,1)S(1)}, bf16[128,3072]{1,0:T(8,128)(2,1)S(1)}, u32[]{:S(2)}, u32[]{:S(2)}) collective-permute-start(bf16[128,3072]{1,0:T(8,128)(2,1)S(1)} %slice.14), channel_id=1, source_target_pairs={{0,2},{1,3},{2,0},{3,1},{4,6},{5,7},{6,4},{7,5},{8,10},{9,11},{10,... | collective-permute-start | bytes 2359304 | tf_op jit(solution)/shard_map/ppermute | solution.py:31
  62.9 17.6 %collective-permute-start.17 = (bf16[128,3072]{1,0:T(8,128)(2,1)S(1)}, bf16[128,3072]{1,0:T(8,128)(2,1)S(1)}, u32[]{:S(2)}, u32[]{:S(2)}) collective-permute-start(bf16[128,3072]{1,0:T(8,128)(2,1)S(1)} %collective-permute-done.15.refs_4_), channel_id=1, source_target_pairs={{0,4},{4,0},{8,12},{12,8},{16,20},{20,16},{24,28},{28,24},{1,5},{5... | collective-permute-start | bytes 2359304 | tf_op jit(solution)/shard_map/ppermute | solution.py:31
  63.7 5.3 %collective-permute-start.11 = (bf16[96,1536]{1,0:T(8,128)(2,1)S(1)}, bf16[96,1536]{1,0:T(8,128)(2,1)S(1)}, u32[]{:S(2)}, u32[]{:S(2)}) collective-permute-start(bf16[96,1536]{1,0:T(8,128)(2,1)S(1)} %collective-permute-done.7.refs_6_), channel_id=1, source_target_pairs={{0,1},{1,0},{2,3},{3,2},{4,5},{5,4},{6,7},{7,6},{8,9},{9,8},{10,11... | collective-permute-start | bytes 884744 | tf_op jit(solution)/shard_map/ppermute | solution.py:31
  68.9 2.4 %collective-permute-start.10 = (bf16[2,96,1536]{2,1,0:T(8,128)(2,1)S(1)}, bf16[2,96,1536]{2,1,0:T(8,128)(2,1)S(1)}, u32[]{:S(2)}, u32[]{:S(2)}) collective-permute-start(bf16[2,96,1536]{2,1,0:T(8,128)(2,1)S(1)} %pad_maximum_fusion.1), channel_id=1, source_target_pairs={{0,1},{1,0},{2,3},{3,2},{4,5},{5,4},{6,7},{7,6},{8,9},{9,8},{10,11... | collective-permute-start | bytes 1769480 | tf_op jit(solution)/shard_map/ppermute | solution.py:31
  69.0 2.4 %collective-permute-start.12 = (bf16[96,1536]{1,0:T(8,128)(2,1)S(1)}, bf16[96,1536]{1,0:T(8,128)(2,1)S(1)}, u32[]{:S(2)}, u32[]{:S(2)}) collective-permute-start(bf16[96,1536]{1,0:T(8,128)(2,1)S(1)} %collective-permute-done.8.refs_7_), channel_id=1, source_target_pairs={{0,1},{1,0},{2,3},{3,2},{4,5},{5,4},{6,7},{7,6},{8,9},{9,8},{10,11... | collective-permute-start | bytes 884744 | tf_op jit(solution)/shard_map/ppermute | solution.py:31
  77.2 8.4 %collective-permute-start.14 = (bf16[64,768]{1,0:T(8,128)(2,1)S(1)}, bf16[64,768]{1,0:T(8,128)(2,1)S(1)}, u32[]{:S(2)}, u32[]{:S(2)}) collective-permute-start(bf16[64,768]{1,0:T(8,128)(2,1)S(1)} %get-tuple-element.32), channel_id=1, source_target_pairs={{0,16},{4,20},{8,24},{12,28},{16,0},{20,4},{24,8},{28,12},{1,17},{... | collective-permute-start | bytes 294920 | tf_op jit(solution)/shard_map/ppermute | solution.py:31
  84.7 4.9 %collective-permute-start.23 = (bf16[64,512]{1,0:T(8,128)(2,1)S(1)}, bf16[64,512]{1,0:T(8,128)(2,1)S(1)}, u32[]{:S(2)}, u32[]{:S(2)}) collective-permute-start(bf16[64,512]{1,0:T(8,128)(2,1)S(1)} %get-tuple-element.39), channel_id=1, source_target_pairs={{0,2},{1,3},{2,0},{3,1},{4,6},{5,7},{6,4},{7,5},{8,10},{9,11},{10,... | collective-permute-start | bytes 196616 | tf_op jit(solution)/shard_map/ppermute | solution.py:31
  85.7 7.6 %collective-permute-start.18 = (bf16[64,768]{1,0:T(8,128)(2,1)S(1)}, bf16[64,768]{1,0:T(8,128)(2,1)S(1)}, u32[]{:S(2)}, u32[]{:S(2)}) collective-permute-start(bf16[64,768]{1,0:T(8,128)(2,1)S(1)} %get-tuple-element.37), channel_id=1, source_target_pairs={{0,2},{1,3},{2,0},{3,1},{4,6},{5,7},{6,4},{7,5},{8,10},{9,11},{10,... | collective-permute-start | bytes 294920 | tf_op jit(solution)/shard_map/ppermute | solution.py:31
  86.9 7.1 %collective-permute-start.19 = (bf16[64,768]{1,0:T(8,128)(2,1)S(1)}, bf16[64,768]{1,0:T(8,128)(2,1)S(1)}, u32[]{:S(2)}, u32[]{:S(2)}) collective-permute-start(bf16[64,768]{1,0:T(8,128)(2,1)S(1)} %get-tuple-element.37), channel_id=1, source_target_pairs={{0,18},{1,19},{2,16},{3,17},{4,22},{5,23},{6,20},{7,21},{8,26},{9,... | collective-permute-start | bytes 294920 | tf_op jit(solution)/shard_map/ppermute | solution.py:31
  89.7 5.0 %collective-permute-start.24 = (bf16[64,512]{1,0:T(8,128)(2,1)S(1)}, bf16[64,512]{1,0:T(8,128)(2,1)S(1)}, u32[]{:S(2)}, u32[]{:S(2)}) collective-permute-start(bf16[64,512]{1,0:T(8,128)(2,1)S(1)} %add_convert_fusion.3.refs_0_), channel_id=1, source_target_pairs={{0,4},{4,0},{8,12},{12,8},{16,20},{20,16},{24,28},{28,24},{1,5},{5... | collective-permute-start | bytes 196616 | tf_op jit(solution)/shard_map/ppermute | solution.py:31
  90.3 4.4 %collective-permute-start.25 = (bf16[64,512]{1,0:T(8,128)(2,1)S(1)}, bf16[64,512]{1,0:T(8,128)(2,1)S(1)}, u32[]{:S(2)}, u32[]{:S(2)}) collective-permute-start(bf16[64,512]{1,0:T(8,128)(2,1)S(1)} %add_convert_fusion.3.refs_0_), channel_id=1, source_target_pairs={{0,8},{4,12},{8,0},{12,4},{16,24},{20,28},{24,16},{28,20},{1,9},{5... | collective-permute-start | bytes 196616 | tf_op jit(solution)/shard_map/ppermute | solution.py:31
  90.3 5.9 %collective-permute-start.26 = (bf16[64,512]{1,0:T(8,128)(2,1)S(1)}, bf16[64,512]{1,0:T(8,128)(2,1)S(1)}, u32[]{:S(2)}, u32[]{:S(2)}) collective-permute-start(bf16[64,512]{1,0:T(8,128)(2,1)S(1)} %add_convert_fusion.3.refs_0_), channel_id=1, source_target_pairs={{0,12},{4,8},{8,4},{12,0},{16,28},{20,24},{24,20},{28,16},{1,13},{... | collective-permute-start | bytes 196616 | tf_op jit(solution)/shard_map/ppermute | solution.py:31
  96.7 5.8 %collective-permute-start.27 = (bf16[64,768]{1,0:T(8,128)(2,1)S(1)}, bf16[64,768]{1,0:T(8,128)(2,1)S(1)}, u32[]{:S(2)}, u32[]{:S(2)}) collective-permute-start(bf16[64,768]{1,0:T(8,128)(2,1)S(1)} %shard_map.98), channel_id=1, source_target_pairs={{0,16},{4,20},{8,24},{12,28},{16,0},{20,4},{24,8},{28,12},{1,17},{... | collective-permute-start | bytes 294920 | tf_op jit(solution)/shard_map/ppermute | solution.py:31
  98.3 11.0 %collective-permute-start.20 = (bf16[64,1536]{1,0:T(8,128)(2,1)S(1)}, bf16[64,1536]{1,0:T(8,128)(2,1)S(1)}, u32[]{:S(2)}, u32[]{:S(2)}) collective-permute-start(bf16[64,1536]{1,0:T(8,128)(2,1)S(1)} %pad_maximum_fusion.2.refs_0_), channel_id=1, source_target_pairs={{0,4},{4,0},{8,12},{12,8},{16,20},{20,16},{24,28},{28,24},{1,5},{5... | collective-permute-start | bytes 589832 | tf_op jit(solution)/shard_map/ppermute | solution.py:31
  99.9 9.5 %collective-permute-start.21 = (bf16[64,1536]{1,0:T(8,128)(2,1)S(1)}, bf16[64,1536]{1,0:T(8,128)(2,1)S(1)}, u32[]{:S(2)}, u32[]{:S(2)}) collective-permute-start(bf16[64,1536]{1,0:T(8,128)(2,1)S(1)} %pad_maximum_fusion.2.refs_0_), channel_id=1, source_target_pairs={{0,8},{4,12},{8,0},{12,4},{16,24},{20,28},{24,16},{28,20},{1,9},{5... | collective-permute-start | bytes 589832 | tf_op jit(solution)/shard_map/ppermute | solution.py:31
  100.1 9.3 %collective-permute-start.22 = (bf16[64,1536]{1,0:T(8,128)(2,1)S(1)}, bf16[64,1536]{1,0:T(8,128)(2,1)S(1)}, u32[]{:S(2)}, u32[]{:S(2)}) collective-permute-start(bf16[64,1536]{1,0:T(8,128)(2,1)S(1)} %pad_maximum_fusion.2.refs_0_), channel_id=1, source_target_pairs={{0,12},{4,8},{8,4},{12,0},{16,28},{20,24},{24,20},{28,16},{1,13},{... | collective-permute-start | bytes 589832 | tf_op jit(solution)/shard_map/ppermute | solution.py:31
  102.5 7.9 %collective-permute-start.28 = (bf16[64,768]{1,0:T(8,128)(2,1)S(1)}, bf16[64,768]{1,0:T(8,128)(2,1)S(1)}, u32[]{:S(2)}, u32[]{:S(2)}) collective-permute-start(bf16[64,768]{1,0:T(8,128)(2,1)S(1)} %add_convert_fusion.refs_4_), channel_id=1, source_target_pairs={{0,4},{4,0},{8,12},{12,8},{16,20},{20,16},{24,28},{28,24},{1,5},{5... | collective-permute-start | bytes 294920 | tf_op jit(solution)/shard_map/ppermute | solution.py:31
  (1 other events, 17.6 us)

commit v6 on v5

--- a/solution.py
+++ b/solution.py
@@ -155,30 +155,18 @@
             *frame_refs, down_ref, up_ref, up_out, back_out, w_in, w_out = refs[:10]
         else:
             w_in, w_out, *frame_refs, maps_ref, up_out, back_out = refs[:9]
-        normed, masked, down_map, up_map, sems = refs[-5:]
+        down_map, up_map = refs[-2:]
         f, low_bit, x, y, core = place()
         slot = low_bit * 2 + x
         flat = []
         for ref in swap_refs:
             flat += [ref.at[j] for j in range(ref.shape[0])] if len(ref.shape) == 3 else [ref]
-        copies = []
-        for k, (w, kept) in enumerate(((w_out, masked), (w_in, normed))):
-            for i, ref in enumerate(frame_refs):
-                at = pl.multiple_of((slot ^ i) * rows, 16)
-                copies.append((ref.at[pl.ds(0, rows), pl.ds((1 - k) * width, width)], kept.at[pl.ds(at, rows)]))
-            for side, group in enumerate((piece_refs, flat)):
-                for i, ref in enumerate(group):
-                    for lower in range(2):
-                        at = pl.multiple_of((f ^ codes[i]) * depth + lower * (depth // 2), 16)
-                        copies.append(
-                            (
-                                ref.at[:, pl.ds((2 * (1 - k) + lower) * part, part)],
-                                w.at[pl.ds(at, depth // 2), pl.ds(side * part, part)],
-                            )
-                        )
-        copies = [pltpu.make_async_copy(src, dst, sems.at[i]) for i, (src, dst) in enumerate(copies)]
-        for copy in copies:
-            copy.start()
+        for side, group in enumerate((piece_refs, flat)):
+            for i, ref in enumerate(group):
+                for k in range(4):
+                    at = pl.multiple_of((f ^ codes[i]) * depth + (k % 2) * (depth // 2), 16)
+                    w = (w_in, w_out)[k // 2]
+                    w[pl.ds(at, depth // 2), side * part : (side + 1) * part] = ref[:, k * part : (k + 1) * part]
         if own:
             for dc in range(2):
                 start = (y * 2 + (core ^ dc)) * (4 * part) + (x * 2 + low_bit) * part
@@ -190,33 +178,29 @@
             for i in range(2):
                 at = i * (rank // 2)
                 down_map[at : at + rank // 2, :] = maps_ref[rows + 16 :, i * width : (i + 1) * width]
-        for copy in copies:
-            copy.wait()
-        low = dot(down_map[...], normed[...], ((1,), (1,))).astype(BF)
-        pre = dot(normed[...], w_in[...]) + dot(low.T, up_map[...])
-        dhid = 0.5 * dot(masked[...], w_out[...])
+        normed = jnp.concatenate([ref[:rows, :width] for ref in frame_refs], axis=0)
+        masked = jnp.concatenate([ref[:rows, width:] for ref in frame_refs], axis=0)
+        low = dot(down_map[...], normed, ((1,), (1,))).astype(BF)
+        pre = dot(normed, w_in[...]) + dot(low.T, up_map[...])
+        dhid = 0.5 * dot(masked, w_out[...])
         dpre = swish_gradient(pre, dhid)
         up_out[...] = dot(low, dpre).astype(BF)
         back = dot(up_map[...], dpre, ((1,), (1,)))
-        back_out[...] = back.astype(kind)
-
-    anywhere = pl.BlockSpec(memory_space=pl.ANY)
+        for i in range(4):
+            back_out[:, lanes((slot ^ i) * rows, rows)] = back[:, i * rows : (i + 1) * rows].astype(kind)
+
     whole_weights = jax.ShapeDtypeStruct((8 * depth, hidden), BF)
     outs = [jax.ShapeDtypeStruct((rank, hidden), BF), jax.ShapeDtypeStruct((rank, count), kind)]
     if own:
         args = (*pieces, *swapped, *frames, *maps)
-        ins = [anywhere] * (len(args) - 2)
+        ins = [whole(a.shape) for a in args]
         outs += [whole_weights, whole_weights]
     else:
         args = (*weights, *frames, *maps)
-        ins = [whole(w.shape) for w in weights] + [anywhere] * 4
-    ins += [whole(a.shape) for a in maps]
+        ins = [whole(a.shape) for a in args]
     scratch = [
-        pltpu.VMEM((count, width), BF),
-        pltpu.VMEM((count, width), BF),
         pltpu.VMEM((rank, width), BF),
         pltpu.VMEM((rank, hidden), BF),
-        pltpu.SemaphoreType.DMA((72 if own else 8,)),
     ]
     return call(body, ins, outs, args, scratch)
 

time: 112 us -> 110 us (0.982)
  Pallas kernels: 16 us -> 14 us
    pallas_call x5, Pallas kernels: 16 us -> 14 us  [call(): pl.pallas_call(body, in_specs=ins, out_specs=[whole(o.shape) if space is...]
  transfers between devices with their start and end apart: 29 -> 29, of which waited for: 15 -> 17; matrix products, arithmetic and copies ran while one was open for 0% -> 0% of each run, Pallas kernels for 9% -> 7%
where the time goes in v6:
time: 110 us
  waiting for transfers between devices  55.4 us (50%)
  starting transfers between devices  38.5 us (35%)
  Pallas kernels  14 us (13%)
  between operations  1.44 us (1%)
    ppermute x29, waiting for transfers between devices, flip(): lax.ppermute(value, axis, [(i, i ^ bits) for i in range(size)])  55.4 us
    ppermute x29, starting transfers between devices, flip(): lax.ppermute(value, axis, [(i, i ^ bits) for i in range(size)])  38.5 us
    pallas_call x5, Pallas kernels, call(): pl.pallas_call(body, in_specs=ins, out_specs=[whole(o.shape) if space is...  14 us
  transfers between devices with their start and end apart: 29, of which 17 were waited for; matrix products, arithmetic and copies ran while one was open for 0% of the time, Pallas kernels for 7%

profile of v6, /device:TPU:0, one launch (start us, length us, event | category | flops | bytes accessed | tf_op | source)
XLA Modules:
  0.0 109.7 jit_solution(5806466348209807898)
XLA Ops:
  1.3 4.1 %shard_map.95 = (bf16[128,3072]{1,0:T(8,128)(2,1)}, bf16[176,3072]{1,0:T(8,128)(2,1)}, bf16[224,3072]{1,0:T(8,128)(2,1)}, bf16[96,1536]{1,0:T(8,128)(2,1)}, bf16[96,1536]{1,0:T(8,128)(2,1)}) custom-call(bf16[1,144,1536]{2,1,0:T(8,128)(2,1)} %frames_ref.1, f32[1536]{0:T(1024)} %gain_ref.1, bf16[192,1536]{1,0:T(8,128)(2,1)} %first_ref.1, ...), custom_call_target="tpu_custom_call" | custom-call | tf_op jit(solution)/shard_map/pallas_call | solution.py:48
  5.4 3.0 %collective-permute-start = (bf16[224,3072]{1,0:T(8,128)(2,1)}, bf16[224,3072]{1,0:T(8,128)(2,1)S(1)}, u32[]{:S(2)}, u32[]{:S(2)}) collective-permute-start(bf16[224,3072]{1,0:T(8,128)(2,1)} %get-tuple-element.23), channel_id=1, source_target_pairs={{0,4},{4,0},{8,12},{12,8},{16,20},{20,16},{24,28},{28,24},{1,5},{5... | collective-permute-start | bytes 4128776 | tf_op jit(solution)/shard_map/ppermute | solution.py:31
  8.4 1.5 %collective-permute-start.6 = (bf16[176,3072]{1,0:T(8,128)(2,1)}, bf16[176,3072]{1,0:T(8,128)(2,1)S(1)}, u32[]{:S(2)}, u32[]{:S(2)}) collective-permute-start(bf16[176,3072]{1,0:T(8,128)(2,1)} %get-tuple-element.28), channel_id=1, source_target_pairs={{0,2},{1,3},{2,0},{3,1},{4,6},{5,7},{6,4},{7,5},{8,10},{9,11},{10,... | collective-permute-start | bytes 3244040 | tf_op jit(solution)/shard_map/ppermute | solution.py:31
  9.9 1.6 %collective-permute-start.3 = (bf16[128,3072]{1,0:T(8,128)(2,1)}, bf16[128,3072]{1,0:T(8,128)(2,1)S(1)}, u32[]{:S(2)}, u32[]{:S(2)}) collective-permute-start(bf16[128,3072]{1,0:T(8,128)(2,1)} %get-tuple-element.25.refs_12_.refs_4_), channel_id=1, source_target_pairs={{0,8},{4,12},{8,0},{12,4},{16,24},{20,28},{24,16},{28,20},{1,9},{5... | collective-permute-start | bytes 2359304 | tf_op jit(solution)/shard_map/ppermute | solution.py:31
  11.5 2.6 %collective-permute-start.1 = (bf16[96,1536]{1,0:T(8,128)(2,1)}, bf16[96,1536]{1,0:T(8,128)(2,1)S(1)}, u32[]{:S(2)}, u32[]{:S(2)}) collective-permute-start(bf16[96,1536]{1,0:T(8,128)(2,1)} %get-tuple-element.22.refs_0_), channel_id=1, source_target_pairs={{0,16},{4,20},{8,24},{12,28},{16,0},{20,4},{24,8},{28,12},{1,17},{... | collective-permute-start | bytes 884744 | tf_op jit(solution)/shard_map/ppermute | solution.py:31
  14.3 20.9 %collective-permute-done.3.refs_14_.refs_6_ = bf16[128,3072]{1,0:T(8,128)(2,1)S(1)} collective-permute-done((bf16[128,3072]{1,0:T(8,128)(2,1)}, bf16[128,3072]{1,0:T(8,128)(2,1)S(1)}, u32[]{:S(2)}, u32[]{:S(2)}) %collective-permute-start.3) | collective-permute-done | bytes 786464 | tf_op jit(solution)/shard_map/ppermute | solution.py:31
  35.2 3.6 %collective-permute-done.refs_13_.refs_5_ = bf16[224,3072]{1,0:T(8,128)(2,1)S(1)} collective-permute-done((bf16[224,3072]{1,0:T(8,128)(2,1)}, bf16[224,3072]{1,0:T(8,128)(2,1)S(1)}, u32[]{:S(2)}, u32[]{:S(2)}) %collective-permute-start) | collective-permute-done | bytes 1376288 | tf_op jit(solution)/shard_map/ppermute | solution.py:31
  38.8 1.7 %collective-permute-start.13 = (bf16[128,3072]{1,0:T(8,128)(2,1)S(1)}, bf16[128,3072]{1,0:T(8,128)(2,1)S(1)}, u32[]{:S(2)}, u32[]{:S(2)}) collective-permute-start(bf16[128,3072]{1,0:T(8,128)(2,1)S(1)} %collective-permute-done.3.refs_14_.refs_6_), channel_id=1, source_target_pairs={{0,4},{4,0},{8,12},{12,8},{16,20},{20,16},{24,28},{28,24},{1,5},{5... | collective-permute-start | bytes 2359304 | tf_op jit(solution)/shard_map/ppermute | solution.py:31
  40.5 1.5 %collective-permute-start.15 = (bf16[128,3072]{1,0:T(8,128)(2,1)S(1)}, bf16[128,3072]{1,0:T(8,128)(2,1)S(1)}, u32[]{:S(2)}, u32[]{:S(2)}) collective-permute-start(bf16[128,3072]{1,0:T(8,128)(2,1)S(1)} %collective-permute-done.3.refs_14_.refs_6_), channel_id=1, source_target_pairs={{0,2},{1,3},{2,0},{3,1},{4,6},{5,7},{6,4},{7,5},{8,10},{9,11},{10,... | collective-permute-start | bytes 2359304 | tf_op jit(solution)/shard_map/ppermute | solution.py:31
  42.1 3.3 %collective-permute-start.5 = (bf16[96,1536]{1,0:T(8,128)(2,1)S(1)}, bf16[96,1536]{1,0:T(8,128)(2,1)S(1)}, u32[]{:S(2)}, u32[]{:S(2)}) collective-permute-start(bf16[96,1536]{1,0:T(8,128)(2,1)S(1)} %get-tuple-element.27.refs_1_), channel_id=1, source_target_pairs={{0,16},{4,20},{8,24},{12,28},{16,0},{20,4},{24,8},{28,12},{1,17},{... | collective-permute-start | bytes 884744 | tf_op jit(solution)/shard_map/ppermute | solution.py:31
  45.7 8.1 %collective-permute-done.4.refs_4_ = bf16[96,1536]{1,0:T(8,128)(2,1)S(1)} collective-permute-done((bf16[96,1536]{1,0:T(8,128)(2,1)}, bf16[96,1536]{1,0:T(8,128)(2,1)S(1)}, u32[]{:S(2)}, u32[]{:S(2)}) %collective-permute-start.4) | collective-permute-done | bytes 294944 | tf_op jit(solution)/shard_map/ppermute | solution.py:31
  53.8 2.7 %collective-permute-done.5.refs_5_ = bf16[96,1536]{1,0:T(8,128)(2,1)S(1)} collective-permute-done((bf16[96,1536]{1,0:T(8,128)(2,1)S(1)}, bf16[96,1536]{1,0:T(8,128)(2,1)S(1)}, u32[]{:S(2)}, u32[]{:S(2)}) %collective-permute-start.5) | collective-permute-done | bytes 294944 | tf_op jit(solution)/shard_map/ppermute | solution.py:31
  56.5 5.6 %collective-permute-start.8 = (bf16[96,1536]{1,0:T(8,128)(2,1)S(1)}, bf16[96,1536]{1,0:T(8,128)(2,1)S(1)}, u32[]{:S(2)}, u32[]{:S(2)}) collective-permute-start(bf16[96,1536]{1,0:T(8,128)(2,1)S(1)} %get-tuple-element.30), channel_id=1, source_target_pairs={{0,24},{4,28},{8,16},{12,20},{16,8},{20,12},{24,0},{28,4},{1,25},{... | collective-permute-start | bytes 884744 | tf_op jit(solution)/shard_map/ppermute | solution.py:31
  63.7 5.3 %collective-permute-done.8.refs_7_ = bf16[96,1536]{1,0:T(8,128)(2,1)S(1)} collective-permute-done((bf16[96,1536]{1,0:T(8,128)(2,1)S(1)}, bf16[96,1536]{1,0:T(8,128)(2,1)S(1)}, u32[]{:S(2)}, u32[]{:S(2)}) %collective-permute-start.8) | collective-permute-done | bytes 294944 | tf_op jit(solution)/shard_map/ppermute | solution.py:31
  69.5 1.9 %collective-permute-done.12.refs_11_ = bf16[96,1536]{1,0:T(8,128)(2,1)S(1)} collective-permute-done((bf16[96,1536]{1,0:T(8,128)(2,1)S(1)}, bf16[96,1536]{1,0:T(8,128)(2,1)S(1)}, u32[]{:S(2)}, u32[]{:S(2)}) %collective-permute-start.12) | collective-permute-done | bytes 294944 | tf_op jit(solution)/shard_map/ppermute | solution.py:31
  71.4 4.1 %shard_map.96 = (bf16[64,768]{1,0:T(8,128)(2,1)S(1)}, f32[64,512]{1,0:T(8,128)S(1)}, bf16[1536,768]{1,0:T(8,128)(2,1)S(1)}, bf16[1536,768]{1,0:T(8,128)(2,1)S(1)}) custom-call(bf16[96,1536]{1,0:T(8,128)(2,1)S(1)} %copy-done.2, bf16[96,1536]{1,0:T(8,128)(2,1)S(1)} %get-tuple-element.27.refs_1_, bf16[96,1536]{1,0:T(8,128)(2,1)S(1)} %collective-permute-done.1.refs_2_, ...), custom_call_target="tpu_custom_call" | custom-call | tf_op jit(solution)/shard_map/pallas_call | solution.py:48
  75.6 3.2 %collective-permute-start.14 = (bf16[64,768]{1,0:T(8,128)(2,1)S(1)}, bf16[64,768]{1,0:T(8,128)(2,1)S(1)}, u32[]{:S(2)}, u32[]{:S(2)}) collective-permute-start(bf16[64,768]{1,0:T(8,128)(2,1)S(1)} %get-tuple-element.32), channel_id=1, source_target_pairs={{0,16},{4,20},{8,24},{12,28},{16,0},{20,4},{24,8},{28,12},{1,17},{... | collective-permute-start | bytes 294920 | tf_op jit(solution)/shard_map/ppermute | solution.py:31
  78.8 3.9 %shard_map.97 = (bf16[64,768]{1,0:T(8,128)(2,1)S(1)}, bf16[64,512]{1,0:T(8,128)(2,1)S(1)}) custom-call(bf16[1536,768]{1,0:T(8,128)(2,1)S(1)} %get-tuple-element.33.refs_0_, bf16[1536,768]{1,0:T(8,128)(2,1)S(1)} %get-tuple-element.34.refs_1_, bf16[176,3072]{1,0:T(8,128)(2,1)S(1)} %collective-permute-done.6.refs_2_.refs_6_, ...), custom_call_target="tpu_custom_call" | custom-call | tf_op jit(solution)/shard_map/pallas_call | solution.py:48
  84.0 0.9 collective-permute-start.18
  84.9 1.3 %collective-permute-start.19 = (bf16[64,768]{1,0:T(8,128)(2,1)S(1)}, bf16[64,768]{1,0:T(8,128)(2,1)S(1)}, u32[]{:S(2)}, u32[]{:S(2)}) collective-permute-start(bf16[64,768]{1,0:T(8,128)(2,1)S(1)} %get-tuple-element.37), channel_id=1, source_target_pairs={{0,18},{1,19},{2,16},{3,17},{4,22},{5,23},{6,20},{7,21},{8,26},{9,... | collective-permute-start | bytes 294920 | tf_op jit(solution)/shard_map/ppermute | solution.py:31
  86.2 1.5 %collective-permute-done.23 = bf16[64,512]{1,0:T(8,128)(2,1)S(1)} collective-permute-done((bf16[64,512]{1,0:T(8,128)(2,1)S(1)}, bf16[64,512]{1,0:T(8,128)(2,1)S(1)}, u32[]{:S(2)}, u32[]{:S(2)}) %collective-permute-start.23) | collective-permute-done | bytes 65568 | tf_op jit(solution)/shard_map/ppermute | solution.py:31
  88.5 2.8 %collective-permute-start.26 = (bf16[64,512]{1,0:T(8,128)(2,1)S(1)}, bf16[64,512]{1,0:T(8,128)(2,1)S(1)}, u32[]{:S(2)}, u32[]{:S(2)}) collective-permute-start(bf16[64,512]{1,0:T(8,128)(2,1)S(1)} %add_convert_fusion.3.refs_0_), channel_id=1, source_target_pairs={{0,12},{4,8},{8,4},{12,0},{16,28},{20,24},{24,20},{28,16},{1,13},{... | collective-permute-start | bytes 196616 | tf_op jit(solution)/shard_map/ppermute | solution.py:31
  92.7 1.5 %collective-permute-done.26.refs_3_ = bf16[64,512]{1,0:T(8,128)(2,1)S(1)} collective-permute-done((bf16[64,512]{1,0:T(8,128)(2,1)S(1)}, bf16[64,512]{1,0:T(8,128)(2,1)S(1)}, u32[]{:S(2)}, u32[]{:S(2)}) %collective-permute-start.26) | collective-permute-done | bytes 65568 | tf_op jit(solution)/shard_map/ppermute | solution.py:31
  94.7 1.6 %collective-permute-start.27 = (bf16[64,768]{1,0:T(8,128)(2,1)S(1)}, bf16[64,768]{1,0:T(8,128)(2,1)S(1)}, u32[]{:S(2)}, u32[]{:S(2)}) collective-permute-start(bf16[64,768]{1,0:T(8,128)(2,1)S(1)} %shard_map.98), channel_id=1, source_target_pairs={{0,16},{4,20},{8,24},{12,28},{16,0},{20,4},{24,8},{28,12},{1,17},{... | collective-permute-start | bytes 294920 | tf_op jit(solution)/shard_map/ppermute | solution.py:31
  96.3 1.5 %collective-permute-start.20 = (bf16[64,1536]{1,0:T(8,128)(2,1)S(1)}, bf16[64,1536]{1,0:T(8,128)(2,1)S(1)}, u32[]{:S(2)}, u32[]{:S(2)}) collective-permute-start(bf16[64,1536]{1,0:T(8,128)(2,1)S(1)} %pad_maximum_fusion.2.refs_0_), channel_id=1, source_target_pairs={{0,4},{4,0},{8,12},{12,8},{16,20},{20,16},{24,28},{28,24},{1,5},{5... | collective-permute-start | bytes 589832 | tf_op jit(solution)/shard_map/ppermute | solution.py:31
  98.4 1.5 %collective-permute-start.22 = (bf16[64,1536]{1,0:T(8,128)(2,1)S(1)}, bf16[64,1536]{1,0:T(8,128)(2,1)S(1)}, u32[]{:S(2)}, u32[]{:S(2)}) collective-permute-start(bf16[64,1536]{1,0:T(8,128)(2,1)S(1)} %pad_maximum_fusion.2.refs_0_), channel_id=1, source_target_pairs={{0,12},{4,8},{8,4},{12,0},{16,28},{20,24},{24,20},{28,16},{1,13},{... | collective-permute-start | bytes 589832 | tf_op jit(solution)/shard_map/ppermute | solution.py:31
  99.9 0.7 collective-permute-done.27
  100.6 0.8 collective-permute-start.28
  101.4 3.6 %collective-permute-done.20.refs_1_ = bf16[64,1536]{1,0:T(8,128)(2,1)S(1)} collective-permute-done((bf16[64,1536]{1,0:T(8,128)(2,1)S(1)}, bf16[64,1536]{1,0:T(8,128)(2,1)S(1)}, u32[]{:S(2)}, u32[]{:S(2)}) %collective-permute-start.20) | collective-permute-done | bytes 196640 | tf_op jit(solution)/shard_map/ppermute | solution.py:31
  105.0 2.6 %collective-permute-done.22.refs_3_ = bf16[64,1536]{1,0:T(8,128)(2,1)S(1)} collective-permute-done((bf16[64,1536]{1,0:T(8,128)(2,1)S(1)}, bf16[64,1536]{1,0:T(8,128)(2,1)S(1)}, u32[]{:S(2)}, u32[]{:S(2)}) %collective-permute-start.22) | collective-permute-done | bytes 196640 | tf_op jit(solution)/shard_map/ppermute | solution.py:31
  107.7 0.7 collective-permute-done.28.refs_5_
  108.4 1.4 %shard_map.99 = (f32[1,64,6144]{2,1,0:T(8,128)}, f32[1,64,1536]{2,1,0:T(8,128)}) custom-call(bf16[64,1536]{1,0:T(8,128)(2,1)S(1)} %pad_maximum_fusion.2.refs_0_, bf16[64,1536]{1,0:T(8,128)(2,1)S(1)} %collective-permute-done.20.refs_1_, bf16[64,1536]{1,0:T(8,128)(2,1)S(1)} %collective-permute-done.21.refs_2_, ...), custom_call_target="tpu_custom_call" | custom-call | tf_op jit(solution)/shard_map/pallas_call | solution.py:48
  (48 shorter events, 7.2 us)
Async XLA Ops:
  5.4 40.1 %copy-start.2 = (bf16[96,1536]{1,0:T(8,128)(2,1)S(1)}, bf16[96,1536]{1,0:T(8,128)(2,1)}, u32[]{:S(2)}) copy-start(bf16[96,1536]{1,0:T(8,128)(2,1)} %get-tuple-element.22.refs_0_) | copy-start | bytes 884740
  5.4 33.4 %collective-permute-start = (bf16[224,3072]{1,0:T(8,128)(2,1)}, bf16[224,3072]{1,0:T(8,128)(2,1)S(1)}, u32[]{:S(2)}, u32[]{:S(2)}) collective-permute-start(bf16[224,3072]{1,0:T(8,128)(2,1)} %get-tuple-element.23), channel_id=1, source_target_pairs={{0,4},{4,0},{8,12},{12,8},{16,20},{20,16},{24,28},{28,24},{1,5},{5... | collective-permute-start | bytes 4128776 | tf_op jit(solution)/shard_map/ppermute | solution.py:31
  8.4 26.8 %collective-permute-start.6 = (bf16[176,3072]{1,0:T(8,128)(2,1)}, bf16[176,3072]{1,0:T(8,128)(2,1)S(1)}, u32[]{:S(2)}, u32[]{:S(2)}) collective-permute-start(bf16[176,3072]{1,0:T(8,128)(2,1)} %get-tuple-element.28), channel_id=1, source_target_pairs={{0,2},{1,3},{2,0},{3,1},{4,6},{5,7},{6,4},{7,5},{8,10},{9,11},{10,... | collective-permute-start | bytes 3244040 | tf_op jit(solution)/shard_map/ppermute | solution.py:31
  9.9 25.3 %collective-permute-start.3 = (bf16[128,3072]{1,0:T(8,128)(2,1)}, bf16[128,3072]{1,0:T(8,128)(2,1)S(1)}, u32[]{:S(2)}, u32[]{:S(2)}) collective-permute-start(bf16[128,3072]{1,0:T(8,128)(2,1)} %get-tuple-element.25.refs_12_.refs_4_), channel_id=1, source_target_pairs={{0,8},{4,12},{8,0},{12,4},{16,24},{20,28},{24,16},{28,20},{1,9},{5... | collective-permute-start | bytes 2359304 | tf_op jit(solution)/shard_map/ppermute | solution.py:31
  11.5 30.6 %collective-permute-start.1 = (bf16[96,1536]{1,0:T(8,128)(2,1)}, bf16[96,1536]{1,0:T(8,128)(2,1)S(1)}, u32[]{:S(2)}, u32[]{:S(2)}) collective-permute-start(bf16[96,1536]{1,0:T(8,128)(2,1)} %get-tuple-element.22.refs_0_), channel_id=1, source_target_pairs={{0,16},{4,20},{8,24},{12,28},{16,0},{20,4},{24,8},{28,12},{1,17},{... | collective-permute-start | bytes 884744 | tf_op jit(solution)/shard_map/ppermute | solution.py:31
  14.1 31.4 %collective-permute-start.2 = (bf16[96,1536]{1,0:T(8,128)(2,1)}, bf16[96,1536]{1,0:T(8,128)(2,1)S(1)}, u32[]{:S(2)}, u32[]{:S(2)}) collective-permute-start(bf16[96,1536]{1,0:T(8,128)(2,1)} %get-tuple-element.26), channel_id=1, source_target_pairs={{0,24},{4,28},{8,16},{12,20},{16,8},{20,12},{24,0},{28,4},{1,25},{... | collective-permute-start | bytes 884744 | tf_op jit(solution)/shard_map/ppermute | solution.py:31
  35.2 18.6 %collective-permute-start.4 = (bf16[96,1536]{1,0:T(8,128)(2,1)}, bf16[96,1536]{1,0:T(8,128)(2,1)S(1)}, u32[]{:S(2)}, u32[]{:S(2)}) collective-permute-start(bf16[96,1536]{1,0:T(8,128)(2,1)} %get-tuple-element.26), channel_id=1, source_target_pairs={{0,8},{4,12},{8,0},{12,4},{16,24},{20,28},{24,16},{28,20},{1,9},{5... | collective-permute-start | bytes 884744 | tf_op jit(solution)/shard_map/ppermute | solution.py:31
  38.8 23.4 %collective-permute-start.13 = (bf16[128,3072]{1,0:T(8,128)(2,1)S(1)}, bf16[128,3072]{1,0:T(8,128)(2,1)S(1)}, u32[]{:S(2)}, u32[]{:S(2)}) collective-permute-start(bf16[128,3072]{1,0:T(8,128)(2,1)S(1)} %collective-permute-done.3.refs_14_.refs_6_), channel_id=1, source_target_pairs={{0,4},{4,0},{8,12},{12,8},{16,20},{20,16},{24,28},{28,24},{1,5},{5... | collective-permute-start | bytes 2359304 | tf_op jit(solution)/shard_map/ppermute | solution.py:31
  40.5 21.6 %collective-permute-start.15 = (bf16[128,3072]{1,0:T(8,128)(2,1)S(1)}, bf16[128,3072]{1,0:T(8,128)(2,1)S(1)}, u32[]{:S(2)}, u32[]{:S(2)}) collective-permute-start(bf16[128,3072]{1,0:T(8,128)(2,1)S(1)} %collective-permute-done.3.refs_14_.refs_6_), channel_id=1, source_target_pairs={{0,2},{1,3},{2,0},{3,1},{4,6},{5,7},{6,4},{7,5},{8,10},{9,11},{10,... | collective-permute-start | bytes 2359304 | tf_op jit(solution)/shard_map/ppermute | solution.py:31
  42.1 14.3 %collective-permute-start.5 = (bf16[96,1536]{1,0:T(8,128)(2,1)S(1)}, bf16[96,1536]{1,0:T(8,128)(2,1)S(1)}, u32[]{:S(2)}, u32[]{:S(2)}) collective-permute-start(bf16[96,1536]{1,0:T(8,128)(2,1)S(1)} %get-tuple-element.27.refs_1_), channel_id=1, source_target_pairs={{0,16},{4,20},{8,24},{12,28},{16,0},{20,4},{24,8},{28,12},{1,17},{... | collective-permute-start | bytes 884744 | tf_op jit(solution)/shard_map/ppermute | solution.py:31
  45.6 25.8 %collective-permute-start.9 = (bf16[4,96,1536]{2,1,0:T(8,128)(2,1)S(1)}, bf16[4,96,1536]{2,1,0:T(8,128)(2,1)S(1)}, u32[]{:S(2)}, u32[]{:S(2)}) collective-permute-start(bf16[4,96,1536]{2,1,0:T(8,128)(2,1)S(1)} %pad_maximum_fusion), channel_id=1, source_target_pairs={{0,1},{1,0},{2,3},{3,2},{4,5},{5,4},{6,7},{7,6},{8,9},{9,8},{10,11... | collective-permute-start | bytes 3538952 | tf_op jit(solution)/shard_map/ppermute | solution.py:31
  53.8 17.6 %copy-start.1 = (bf16[128,3072]{1,0:T(8,128)(2,1)S(1)}, bf16[128,3072]{1,0:T(8,128)(2,1)}, u32[]{:S(2)}) copy-start(bf16[128,3072]{1,0:T(8,128)(2,1)} %get-tuple-element.25.refs_12_.refs_4_) | copy-start | bytes 2359300
  53.8 17.6 %copy-start.3 = (bf16[1,1536,64]{1,2,0:T(8,128)(2,1)S(1)}, bf16[1,1536,64]{1,2,0:T(8,128)(2,1)}, u32[]{:S(2)}) copy-start(bf16[1,1536,64]{1,2,0:T(8,128)(2,1)} %param.12) | copy-start | bytes 589828
  53.8 9.9 %collective-permute-start.7 = (bf16[96,1536]{1,0:T(8,128)(2,1)S(1)}, bf16[96,1536]{1,0:T(8,128)(2,1)S(1)}, u32[]{:S(2)}, u32[]{:S(2)}) collective-permute-start(bf16[96,1536]{1,0:T(8,128)(2,1)S(1)} %get-tuple-element.30), channel_id=1, source_target_pairs={{0,8},{4,12},{8,0},{12,4},{16,24},{20,28},{24,16},{28,20},{1,9},{5... | collective-permute-start | bytes 884744 | tf_op jit(solution)/shard_map/ppermute | solution.py:31
  56.5 12.5 %collective-permute-start.8 = (bf16[96,1536]{1,0:T(8,128)(2,1)S(1)}, bf16[96,1536]{1,0:T(8,128)(2,1)S(1)}, u32[]{:S(2)}, u32[]{:S(2)}) collective-permute-start(bf16[96,1536]{1,0:T(8,128)(2,1)S(1)} %get-tuple-element.30), channel_id=1, source_target_pairs={{0,24},{4,28},{8,16},{12,20},{16,8},{20,12},{24,0},{28,4},{1,25},{... | collective-permute-start | bytes 884744 | tf_op jit(solution)/shard_map/ppermute | solution.py:31
  62.2 16.6 %collective-permute-start.16 = (bf16[128,3072]{1,0:T(8,128)(2,1)S(1)}, bf16[128,3072]{1,0:T(8,128)(2,1)S(1)}, u32[]{:S(2)}, u32[]{:S(2)}) collective-permute-start(bf16[128,3072]{1,0:T(8,128)(2,1)S(1)} %slice.14), channel_id=1, source_target_pairs={{0,2},{1,3},{2,0},{3,1},{4,6},{5,7},{6,4},{7,5},{8,10},{9,11},{10,... | collective-permute-start | bytes 2359304 | tf_op jit(solution)/shard_map/ppermute | solution.py:31
  62.9 15.9 %collective-permute-start.17 = (bf16[128,3072]{1,0:T(8,128)(2,1)S(1)}, bf16[128,3072]{1,0:T(8,128)(2,1)S(1)}, u32[]{:S(2)}, u32[]{:S(2)}) collective-permute-start(bf16[128,3072]{1,0:T(8,128)(2,1)S(1)} %collective-permute-done.15.refs_4_), channel_id=1, source_target_pairs={{0,4},{4,0},{8,12},{12,8},{16,20},{20,16},{24,28},{28,24},{1,5},{5... | collective-permute-start | bytes 2359304 | tf_op jit(solution)/shard_map/ppermute | solution.py:31
  63.7 5.3 %collective-permute-start.11 = (bf16[96,1536]{1,0:T(8,128)(2,1)S(1)}, bf16[96,1536]{1,0:T(8,128)(2,1)S(1)}, u32[]{:S(2)}, u32[]{:S(2)}) collective-permute-start(bf16[96,1536]{1,0:T(8,128)(2,1)S(1)} %collective-permute-done.7.refs_6_), channel_id=1, source_target_pairs={{0,1},{1,0},{2,3},{3,2},{4,5},{5,4},{6,7},{7,6},{8,9},{9,8},{10,11... | collective-permute-start | bytes 884744 | tf_op jit(solution)/shard_map/ppermute | solution.py:31
  68.9 2.4 %collective-permute-start.10 = (bf16[2,96,1536]{2,1,0:T(8,128)(2,1)S(1)}, bf16[2,96,1536]{2,1,0:T(8,128)(2,1)S(1)}, u32[]{:S(2)}, u32[]{:S(2)}) collective-permute-start(bf16[2,96,1536]{2,1,0:T(8,128)(2,1)S(1)} %pad_maximum_fusion.1), channel_id=1, source_target_pairs={{0,1},{1,0},{2,3},{3,2},{4,5},{5,4},{6,7},{7,6},{8,9},{9,8},{10,11... | collective-permute-start | bytes 1769480 | tf_op jit(solution)/shard_map/ppermute | solution.py:31
  69.0 2.4 %collective-permute-start.12 = (bf16[96,1536]{1,0:T(8,128)(2,1)S(1)}, bf16[96,1536]{1,0:T(8,128)(2,1)S(1)}, u32[]{:S(2)}, u32[]{:S(2)}) collective-permute-start(bf16[96,1536]{1,0:T(8,128)(2,1)S(1)} %collective-permute-done.8.refs_7_), channel_id=1, source_target_pairs={{0,1},{1,0},{2,3},{3,2},{4,5},{5,4},{6,7},{7,6},{8,9},{9,8},{10,11... | collective-permute-start | bytes 884744 | tf_op jit(solution)/shard_map/ppermute | solution.py:31
  75.6 8.4 %collective-permute-start.14 = (bf16[64,768]{1,0:T(8,128)(2,1)S(1)}, bf16[64,768]{1,0:T(8,128)(2,1)S(1)}, u32[]{:S(2)}, u32[]{:S(2)}) collective-permute-start(bf16[64,768]{1,0:T(8,128)(2,1)S(1)} %get-tuple-element.32), channel_id=1, source_target_pairs={{0,16},{4,20},{8,24},{12,28},{16,0},{20,4},{24,8},{28,12},{1,17},{... | collective-permute-start | bytes 294920 | tf_op jit(solution)/shard_map/ppermute | solution.py:31
  82.7 5.0 %collective-permute-start.23 = (bf16[64,512]{1,0:T(8,128)(2,1)S(1)}, bf16[64,512]{1,0:T(8,128)(2,1)S(1)}, u32[]{:S(2)}, u32[]{:S(2)}) collective-permute-start(bf16[64,512]{1,0:T(8,128)(2,1)S(1)} %get-tuple-element.39), channel_id=1, source_target_pairs={{0,2},{1,3},{2,0},{3,1},{4,6},{5,7},{6,4},{7,5},{8,10},{9,11},{10,... | collective-permute-start | bytes 196616 | tf_op jit(solution)/shard_map/ppermute | solution.py:31
  84.0 7.3 %collective-permute-start.18 = (bf16[64,768]{1,0:T(8,128)(2,1)S(1)}, bf16[64,768]{1,0:T(8,128)(2,1)S(1)}, u32[]{:S(2)}, u32[]{:S(2)}) collective-permute-start(bf16[64,768]{1,0:T(8,128)(2,1)S(1)} %get-tuple-element.37), channel_id=1, source_target_pairs={{0,2},{1,3},{2,0},{3,1},{4,6},{5,7},{6,4},{7,5},{8,10},{9,11},{10,... | collective-permute-start | bytes 294920 | tf_op jit(solution)/shard_map/ppermute | solution.py:31
  84.9 7.1 %collective-permute-start.19 = (bf16[64,768]{1,0:T(8,128)(2,1)S(1)}, bf16[64,768]{1,0:T(8,128)(2,1)S(1)}, u32[]{:S(2)}, u32[]{:S(2)}) collective-permute-start(bf16[64,768]{1,0:T(8,128)(2,1)S(1)} %get-tuple-element.37), channel_id=1, source_target_pairs={{0,18},{1,19},{2,16},{3,17},{4,22},{5,23},{6,20},{7,21},{8,26},{9,... | collective-permute-start | bytes 294920 | tf_op jit(solution)/shard_map/ppermute | solution.py:31
  87.7 4.6 %collective-permute-start.24 = (bf16[64,512]{1,0:T(8,128)(2,1)S(1)}, bf16[64,512]{1,0:T(8,128)(2,1)S(1)}, u32[]{:S(2)}, u32[]{:S(2)}) collective-permute-start(bf16[64,512]{1,0:T(8,128)(2,1)S(1)} %add_convert_fusion.3.refs_0_), channel_id=1, source_target_pairs={{0,4},{4,0},{8,12},{12,8},{16,20},{20,16},{24,28},{28,24},{1,5},{5... | collective-permute-start | bytes 196616 | tf_op jit(solution)/shard_map/ppermute | solution.py:31
  88.3 4.4 %collective-permute-start.25 = (bf16[64,512]{1,0:T(8,128)(2,1)S(1)}, bf16[64,512]{1,0:T(8,128)(2,1)S(1)}, u32[]{:S(2)}, u32[]{:S(2)}) collective-permute-start(bf16[64,512]{1,0:T(8,128)(2,1)S(1)} %add_convert_fusion.3.refs_0_), channel_id=1, source_target_pairs={{0,8},{4,12},{8,0},{12,4},{16,24},{20,28},{24,16},{28,20},{1,9},{5... | collective-permute-start | bytes 196616 | tf_op jit(solution)/shard_map/ppermute | solution.py:31
  88.5 5.7 %collective-permute-start.26 = (bf16[64,512]{1,0:T(8,128)(2,1)S(1)}, bf16[64,512]{1,0:T(8,128)(2,1)S(1)}, u32[]{:S(2)}, u32[]{:S(2)}) collective-permute-start(bf16[64,512]{1,0:T(8,128)(2,1)S(1)} %add_convert_fusion.3.refs_0_), channel_id=1, source_target_pairs={{0,12},{4,8},{8,4},{12,0},{16,28},{20,24},{24,20},{28,16},{1,13},{... | collective-permute-start | bytes 196616 | tf_op jit(solution)/shard_map/ppermute | solution.py:31
  94.7 5.8 %collective-permute-start.27 = (bf16[64,768]{1,0:T(8,128)(2,1)S(1)}, bf16[64,768]{1,0:T(8,128)(2,1)S(1)}, u32[]{:S(2)}, u32[]{:S(2)}) collective-permute-start(bf16[64,768]{1,0:T(8,128)(2,1)S(1)} %shard_map.98), channel_id=1, source_target_pairs={{0,16},{4,20},{8,24},{12,28},{16,0},{20,4},{24,8},{28,12},{1,17},{... | collective-permute-start | bytes 294920 | tf_op jit(solution)/shard_map/ppermute | solution.py:31
  96.3 8.7 %collective-permute-start.20 = (bf16[64,1536]{1,0:T(8,128)(2,1)S(1)}, bf16[64,1536]{1,0:T(8,128)(2,1)S(1)}, u32[]{:S(2)}, u32[]{:S(2)}) collective-permute-start(bf16[64,1536]{1,0:T(8,128)(2,1)S(1)} %pad_maximum_fusion.2.refs_0_), channel_id=1, source_target_pairs={{0,4},{4,0},{8,12},{12,8},{16,20},{20,16},{24,28},{28,24},{1,5},{5... | collective-permute-start | bytes 589832 | tf_op jit(solution)/shard_map/ppermute | solution.py:31
  97.8 7.2 %collective-permute-start.21 = (bf16[64,1536]{1,0:T(8,128)(2,1)S(1)}, bf16[64,1536]{1,0:T(8,128)(2,1)S(1)}, u32[]{:S(2)}, u32[]{:S(2)}) collective-permute-start(bf16[64,1536]{1,0:T(8,128)(2,1)S(1)} %pad_maximum_fusion.2.refs_0_), channel_id=1, source_target_pairs={{0,8},{4,12},{8,0},{12,4},{16,24},{20,28},{24,16},{28,20},{1,9},{5... | collective-permute-start | bytes 589832 | tf_op jit(solution)/shard_map/ppermute | solution.py:31
  98.4 9.3 %collective-permute-start.22 = (bf16[64,1536]{1,0:T(8,128)(2,1)S(1)}, bf16[64,1536]{1,0:T(8,128)(2,1)S(1)}, u32[]{:S(2)}, u32[]{:S(2)}) collective-permute-start(bf16[64,1536]{1,0:T(8,128)(2,1)S(1)} %pad_maximum_fusion.2.refs_0_), channel_id=1, source_target_pairs={{0,12},{4,8},{8,4},{12,0},{16,28},{20,24},{24,20},{28,16},{1,13},{... | collective-permute-start | bytes 589832 | tf_op jit(solution)/shard_map/ppermute | solution.py:31
  100.6 7.8 %collective-permute-start.28 = (bf16[64,768]{1,0:T(8,128)(2,1)S(1)}, bf16[64,768]{1,0:T(8,128)(2,1)S(1)}, u32[]{:S(2)}, u32[]{:S(2)}) collective-permute-start(bf16[64,768]{1,0:T(8,128)(2,1)S(1)} %add_convert_fusion.refs_4_), channel_id=1, source_target_pairs={{0,4},{4,0},{8,12},{12,8},{16,20},{20,16},{24,28},{28,24},{1,5},{5... | collective-permute-start | bytes 294920 | tf_op jit(solution)/shard_map/ppermute | solution.py:31
  (1 other events, 17.6 us)

commit v7 on v6

--- a/solution.py
+++ b/solution.py
@@ -134,6 +134,19 @@
     return call(body, ins, outs, args, scratch, vmem=62, space=pltpu.HBM)
 
 
+def low_of(frames, down_turned):
+    rows, rank, width = frames[0].shape[0], down_turned.shape[1], down_turned.shape[2]
+
+    def body(*refs):
+        frame_refs, (down_ref, out_ref) = refs[:4], refs[4:]
+        normed = jnp.concatenate([ref[:rows, :width] for ref in frame_refs], axis=0)
+        out_ref[...] = dot(down_ref[0], normed, ((1,), (1,))).astype(BF)
+
+    args = (*frames, down_turned)
+    outs = [jax.ShapeDtypeStruct((rank, 4 * rows), BF)]
+    return call(body, [whole(a.shape) for a in args], outs, args)[0]
+
+
 def work(weights, frames, maps, width, rank, own):
     if own:
         pieces, swapped = weights
@@ -152,7 +165,7 @@
         piece_refs, refs = refs[:n_pieces], refs[n_pieces:]
         swap_refs, refs = refs[:n_swapped], refs[n_swapped:]
         if own:
-            *frame_refs, down_ref, up_ref, up_out, back_out, w_in, w_out = refs[:10]
+            *frame_refs, low_ref, up_ref, up_out, back_out, w_in, w_out = refs[:10]
         else:
             w_in, w_out, *frame_refs, maps_ref, up_out, back_out = refs[:9]
         down_map, up_map = refs[-2:]
@@ -171,7 +184,6 @@
             for dc in range(2):
                 start = (y * 2 + (core ^ dc)) * (4 * part) + (x * 2 + low_bit) * part
                 up_map[:, dc * part : (dc + 1) * part] = up_ref[0, :, lanes(start, part)]
-            down_map[...] = down_ref[0]
         else:
             for i in range(rank // 16):
                 up_map[16 * i : 16 * (i + 1), :] = maps_ref[rows : rows + 16, i * hidden : (i + 1) * hidden]
@@ -180,7 +192,7 @@
                 down_map[at : at + rank // 2, :] = maps_ref[rows + 16 :, i * width : (i + 1) * width]
         normed = jnp.concatenate([ref[:rows, :width] for ref in frame_refs], axis=0)
         masked = jnp.concatenate([ref[:rows, width:] for ref in frame_refs], axis=0)
-        low = dot(down_map[...], normed, ((1,), (1,))).astype(BF)
+        low = low_ref[...] if own else dot(down_map[...], normed, ((1,), (1,))).astype(BF)
         pre = dot(normed, w_in[...]) + dot(low.T, up_map[...])
         dhid = 0.5 * dot(masked, w_out[...])
         dpre = swish_gradient(pre, dhid)
@@ -208,36 +220,21 @@
 def down_half(backs, frames, width):
     rank, count = backs[0].shape
     rows, half = count // 4, width // 2
-    n_backs = len(backs)
 
     def body(*refs):
-        back_refs, frame_refs, (out_ref, normed, sems) = refs[:n_backs], refs[n_backs:-3], refs[-3:]
+        back_refs, frame_refs, out_ref, normed = refs[:4], refs[4:8], refs[8], refs[9]
         _, low_bit, x, _, _ = place()
         slot = low_bit * 2 + x
-        copies = []
         for i, ref in enumerate(frame_refs):
-            copies.append(
-                pltpu.make_async_copy(
-                    ref.at[pl.ds(0, rows), lanes(x * half, half)],
-                    normed.at[pl.ds(pl.multiple_of((slot ^ i) * rows, 16), rows)],
-                    sems.at[i],
-                )
-            )
-        for copy in copies:
-            copy.start()
-        parts = [ref[...].astype(F32) for ref in back_refs]
-        while len(parts) > 1:
-            parts = [parts[i] + parts[i + 1] for i in range(0, len(parts), 2)]
-        back = parts[0].astype(BF)
-        for copy in copies:
-            copy.wait()
+            at = pl.multiple_of((slot ^ i) * rows, 16)
+            normed[pl.ds(at, rows), :] = ref[:rows, lanes(x * half, half)]
+        b, bx, bz, bzx = [ref[...].astype(F32) for ref in back_refs]
+        back = ((b + bx) + (bz + bzx)).astype(BF)
         out_ref[...] = dot(back, normed[...]).astype(BF)
 
     args = (*backs, *frames)
-    ins = [whole(b.shape) for b in backs] + [pl.BlockSpec(memory_space=pl.ANY)] * 4
-    scratch = [pltpu.VMEM((count, half), BF), pltpu.SemaphoreType.DMA((4,))]
     outs = [jax.ShapeDtypeStruct((rank, half), BF)]
-    return call(body, ins, outs, args, scratch)[0]
+    return call(body, [whole(a.shape) for a in args], outs, args, [pltpu.VMEM((count, half), BF)])[0]
 
 
 def spread(ups, downs, block):
@@ -302,10 +299,11 @@
     fzxy, fxy = over_x(after(fzy, *two)), over_y(after(fx[:rows], *two))
     z1f, z3f = over_low(after(wx1, *one, z1n)), over_both(after(wx1, *one, z2f))
     middle = over_core(jnp.stack([z1n, z2f]))
+    low = low_of([own, fx, fz, fzx], down_turned)
     far = [over_core(z1f), over_core(z3f)]
     weights = ([w00, wx0, z2n, z3n, z1n, z2f, z1f, z3f], [near, middle, *far])
 
-    up, back, w_in, w_out = work(weights, [own, fx, fz, fzx], (down_turned, up_map), width, rank, True)
+    up, back, w_in, w_out = work(weights, [own, fx, fz, fzx], (low, up_map), width, rank, True)
     cross_up, cross_back = work((w_in, w_out), [fy, fxy, fzy, fzxy], (fy,), width, rank, False)
 
     back = (back + over_y(cross_back).astype(F32)).astype(BF)

time: 110 us -> 109 us (level)
  waiting for transfers between devices: 55.4 us -> 54 us
    ppermute x29, waiting for transfers between devices: 55.4 us -> 54 us  [flip(): lax.ppermute(value, axis, [(i, i ^ bits) for i in range(size)])]
    pallas_call x5 -> x6, Pallas kernels: 14 us -> 13.8 us  [call(): pl.pallas_call(body, in_specs=ins, out_specs=[whole(o.shape) if space is...]
  transfers between devices with their start and end apart: 29 -> 29, of which waited for: 17 -> 16; matrix products, arithmetic and copies ran while one was open for 0% -> 0% of each run, Pallas kernels for 7% -> 7%
where the time goes in v7:
time: 109 us
  waiting for transfers between devices  54 us (50%)
  starting transfers between devices  39.4 us (36%)
  Pallas kernels  13.8 us (13%)
  between operations  1.43 us (1%)
    ppermute x29, waiting for transfers between devices, flip(): lax.ppermute(value, axis, [(i, i ^ bits) for i in range(size)])  54 us
    ppermute x29, starting transfers between devices, flip(): lax.ppermute(value, axis, [(i, i ^ bits) for i in range(size)])  39.4 us
    pallas_call x6, Pallas kernels, call(): pl.pallas_call(body, in_specs=ins, out_specs=[whole(o.shape) if space is...  13.8 us
  transfers between devices with their start and end apart: 29, of which 16 were waited for; matrix products, arithmetic and copies ran while one was open for 0% of the time, Pallas kernels for 7%

profile of v7, /device:TPU:0, one launch (start us, length us, event | category | flops | bytes accessed | tf_op | source)
XLA Modules:
  0.0 109.1 jit_solution(17883193284030467434)
XLA Ops:
  1.3 4.1 %shard_map.95 = (bf16[128,3072]{1,0:T(8,128)(2,1)}, bf16[176,3072]{1,0:T(8,128)(2,1)}, bf16[224,3072]{1,0:T(8,128)(2,1)}, bf16[96,1536]{1,0:T(8,128)(2,1)}, bf16[96,1536]{1,0:T(8,128)(2,1)}) custom-call(bf16[1,144,1536]{2,1,0:T(8,128)(2,1)} %frames_ref.1, f32[1536]{0:T(1024)} %gain_ref.1, bf16[192,1536]{1,0:T(8,128)(2,1)} %first_ref.1, ...), custom_call_target="tpu_custom_call" | custom-call | tf_op jit(solution)/shard_map/pallas_call | solution.py:48
  5.4 3.0 %collective-permute-start = (bf16[224,3072]{1,0:T(8,128)(2,1)}, bf16[224,3072]{1,0:T(8,128)(2,1)S(1)}, u32[]{:S(2)}, u32[]{:S(2)}) collective-permute-start(bf16[224,3072]{1,0:T(8,128)(2,1)} %get-tuple-element.23), channel_id=1, source_target_pairs={{0,4},{4,0},{8,12},{12,8},{16,20},{20,16},{24,28},{28,24},{1,5},{5... | collective-permute-start | bytes 4128776 | tf_op jit(solution)/shard_map/ppermute | solution.py:31
  8.4 1.5 %collective-permute-start.6 = (bf16[176,3072]{1,0:T(8,128)(2,1)}, bf16[176,3072]{1,0:T(8,128)(2,1)S(1)}, u32[]{:S(2)}, u32[]{:S(2)}) collective-permute-start(bf16[176,3072]{1,0:T(8,128)(2,1)} %get-tuple-element.28), channel_id=1, source_target_pairs={{0,2},{1,3},{2,0},{3,1},{4,6},{5,7},{6,4},{7,5},{8,10},{9,11},{10,... | collective-permute-start | bytes 3244040 | tf_op jit(solution)/shard_map/ppermute | solution.py:31
  9.9 1.6 %collective-permute-start.3 = (bf16[128,3072]{1,0:T(8,128)(2,1)}, bf16[128,3072]{1,0:T(8,128)(2,1)S(1)}, u32[]{:S(2)}, u32[]{:S(2)}) collective-permute-start(bf16[128,3072]{1,0:T(8,128)(2,1)} %get-tuple-element.25.refs_0_.refs_12_.refs_4_), channel_id=1, source_target_pairs={{0,8},{4,12},{8,0},{12,4},{16,24},{20,28},{24,16},{28,20},{1,9},{5... | collective-permute-start | bytes 2359304 | tf_op jit(solution)/shard_map/ppermute | solution.py:31
  11.5 2.6 %collective-permute-start.1 = (bf16[96,1536]{1,0:T(8,128)(2,1)}, bf16[96,1536]{1,0:T(8,128)(2,1)S(1)}, u32[]{:S(2)}, u32[]{:S(2)}) collective-permute-start(bf16[96,1536]{1,0:T(8,128)(2,1)} %get-tuple-element.22.refs_0_), channel_id=1, source_target_pairs={{0,16},{4,20},{8,24},{12,28},{16,0},{20,4},{24,8},{28,12},{1,17},{... | collective-permute-start | bytes 884744 | tf_op jit(solution)/shard_map/ppermute | solution.py:31
  14.3 20.9 %collective-permute-done.3.refs_2_.refs_14_.refs_6_ = bf16[128,3072]{1,0:T(8,128)(2,1)S(1)} collective-permute-done((bf16[128,3072]{1,0:T(8,128)(2,1)}, bf16[128,3072]{1,0:T(8,128)(2,1)S(1)}, u32[]{:S(2)}, u32[]{:S(2)}) %collective-permute-start.3) | collective-permute-done | bytes 786464 | tf_op jit(solution)/shard_map/ppermute | solution.py:31
  35.2 3.6 %collective-permute-done.refs_1_.refs_13_.refs_5_ = bf16[224,3072]{1,0:T(8,128)(2,1)S(1)} collective-permute-done((bf16[224,3072]{1,0:T(8,128)(2,1)}, bf16[224,3072]{1,0:T(8,128)(2,1)S(1)}, u32[]{:S(2)}, u32[]{:S(2)}) %collective-permute-start) | collective-permute-done | bytes 1376288 | tf_op jit(solution)/shard_map/ppermute | solution.py:31
  38.8 1.7 %collective-permute-start.13 = (bf16[128,3072]{1,0:T(8,128)(2,1)S(1)}, bf16[128,3072]{1,0:T(8,128)(2,1)S(1)}, u32[]{:S(2)}, u32[]{:S(2)}) collective-permute-start(bf16[128,3072]{1,0:T(8,128)(2,1)S(1)} %collective-permute-done.3.refs_2_.refs_14_.refs_6_), channel_id=1, source_target_pairs={{0,4},{4,0},{8,12},{12,8},{16,20},{20,16},{24,28},{28,24},{1,5},{5... | collective-permute-start | bytes 2359304 | tf_op jit(solution)/shard_map/ppermute | solution.py:31
  40.5 1.5 %collective-permute-start.15 = (bf16[128,3072]{1,0:T(8,128)(2,1)S(1)}, bf16[128,3072]{1,0:T(8,128)(2,1)S(1)}, u32[]{:S(2)}, u32[]{:S(2)}) collective-permute-start(bf16[128,3072]{1,0:T(8,128)(2,1)S(1)} %collective-permute-done.3.refs_2_.refs_14_.refs_6_), channel_id=1, source_target_pairs={{0,2},{1,3},{2,0},{3,1},{4,6},{5,7},{6,4},{7,5},{8,10},{9,11},{10,... | collective-permute-start | bytes 2359304 | tf_op jit(solution)/shard_map/ppermute | solution.py:31
  42.1 3.3 %collective-permute-start.5 = (bf16[96,1536]{1,0:T(8,128)(2,1)S(1)}, bf16[96,1536]{1,0:T(8,128)(2,1)S(1)}, u32[]{:S(2)}, u32[]{:S(2)}) collective-permute-start(bf16[96,1536]{1,0:T(8,128)(2,1)S(1)} %get-tuple-element.27.refs_1_), channel_id=1, source_target_pairs={{0,16},{4,20},{8,24},{12,28},{16,0},{20,4},{24,8},{28,12},{1,17},{... | collective-permute-start | bytes 884744 | tf_op jit(solution)/shard_map/ppermute | solution.py:31
  45.7 8.1 %collective-permute-done.4.refs_4_ = bf16[96,1536]{1,0:T(8,128)(2,1)S(1)} collective-permute-done((bf16[96,1536]{1,0:T(8,128)(2,1)}, bf16[96,1536]{1,0:T(8,128)(2,1)S(1)}, u32[]{:S(2)}, u32[]{:S(2)}) %collective-permute-start.4) | collective-permute-done | bytes 294944 | tf_op jit(solution)/shard_map/ppermute | solution.py:31
  53.8 2.7 %collective-permute-done.5.refs_5_ = bf16[96,1536]{1,0:T(8,128)(2,1)S(1)} collective-permute-done((bf16[96,1536]{1,0:T(8,128)(2,1)S(1)}, bf16[96,1536]{1,0:T(8,128)(2,1)S(1)}, u32[]{:S(2)}, u32[]{:S(2)}) %collective-permute-start.5) | collective-permute-done | bytes 294944 | tf_op jit(solution)/shard_map/ppermute | solution.py:31
  56.5 5.6 %collective-permute-start.8 = (bf16[96,1536]{1,0:T(8,128)(2,1)S(1)}, bf16[96,1536]{1,0:T(8,128)(2,1)S(1)}, u32[]{:S(2)}, u32[]{:S(2)}) collective-permute-start(bf16[96,1536]{1,0:T(8,128)(2,1)S(1)} %get-tuple-element.30), channel_id=1, source_target_pairs={{0,24},{4,28},{8,16},{12,20},{16,8},{20,12},{24,0},{28,4},{1,25},{... | collective-permute-start | bytes 884744 | tf_op jit(solution)/shard_map/ppermute | solution.py:31
  63.7 5.3 %collective-permute-done.8.refs_7_ = bf16[96,1536]{1,0:T(8,128)(2,1)S(1)} collective-permute-done((bf16[96,1536]{1,0:T(8,128)(2,1)S(1)}, bf16[96,1536]{1,0:T(8,128)(2,1)S(1)}, u32[]{:S(2)}, u32[]{:S(2)}) %collective-permute-start.8) | collective-permute-done | bytes 294944 | tf_op jit(solution)/shard_map/ppermute | solution.py:31
  70.1 1.3 %collective-permute-done.12.refs_11_ = bf16[96,1536]{1,0:T(8,128)(2,1)S(1)} collective-permute-done((bf16[96,1536]{1,0:T(8,128)(2,1)S(1)}, bf16[96,1536]{1,0:T(8,128)(2,1)S(1)}, u32[]{:S(2)}, u32[]{:S(2)}) %collective-permute-start.12) | collective-permute-done | bytes 294944 | tf_op jit(solution)/shard_map/ppermute | solution.py:31
  71.4 3.6 %shard_map.97 = (bf16[64,768]{1,0:T(8,128)(2,1)S(1)}, f32[64,512]{1,0:T(8,128)S(1)}, bf16[1536,768]{1,0:T(8,128)(2,1)S(1)}, bf16[1536,768]{1,0:T(8,128)(2,1)S(1)}) custom-call(bf16[96,1536]{1,0:T(8,128)(2,1)S(1)} %copy-done.2, bf16[96,1536]{1,0:T(8,128)(2,1)S(1)} %get-tuple-element.27.refs_1_, bf16[96,1536]{1,0:T(8,128)(2,1)S(1)} %collective-permute-done.1.refs_2_, ...), custom_call_target="tpu_custom_call" | custom-call | tf_op jit(solution)/shard_map/pallas_call | solution.py:48
  75.0 3.2 %collective-permute-start.14 = (bf16[64,768]{1,0:T(8,128)(2,1)S(1)}, bf16[64,768]{1,0:T(8,128)(2,1)S(1)}, u32[]{:S(2)}, u32[]{:S(2)}) collective-permute-start(bf16[64,768]{1,0:T(8,128)(2,1)S(1)} %get-tuple-element.32), channel_id=1, source_target_pairs={{0,16},{4,20},{8,24},{12,28},{16,0},{20,4},{24,8},{28,12},{1,17},{... | collective-permute-start | bytes 294920 | tf_op jit(solution)/shard_map/ppermute | solution.py:31
  78.2 3.9 %shard_map.98 = (bf16[64,768]{1,0:T(8,128)(2,1)S(1)}, bf16[64,512]{1,0:T(8,128)(2,1)S(1)}) custom-call(bf16[1536,768]{1,0:T(8,128)(2,1)S(1)} %get-tuple-element.33.refs_0_, bf16[1536,768]{1,0:T(8,128)(2,1)S(1)} %get-tuple-element.34.refs_1_, bf16[176,3072]{1,0:T(8,128)(2,1)S(1)} %collective-permute-done.6.refs_2_.refs_6_, ...), custom_call_target="tpu_custom_call" | custom-call | tf_op jit(solution)/shard_map/pallas_call | solution.py:48
  82.1 1.2 %collective-permute-start.23 = (bf16[64,512]{1,0:T(8,128)(2,1)S(1)}, bf16[64,512]{1,0:T(8,128)(2,1)S(1)}, u32[]{:S(2)}, u32[]{:S(2)}) collective-permute-start(bf16[64,512]{1,0:T(8,128)(2,1)S(1)} %get-tuple-element.39), channel_id=1, source_target_pairs={{0,2},{1,3},{2,0},{3,1},{4,6},{5,7},{6,4},{7,5},{8,10},{9,11},{10,... | collective-permute-start | bytes 196616 | tf_op jit(solution)/shard_map/ppermute | solution.py:31
  83.4 0.8 collective-permute-start.18
  84.3 1.3 %collective-permute-start.19 = (bf16[64,768]{1,0:T(8,128)(2,1)S(1)}, bf16[64,768]{1,0:T(8,128)(2,1)S(1)}, u32[]{:S(2)}, u32[]{:S(2)}) collective-permute-start(bf16[64,768]{1,0:T(8,128)(2,1)S(1)} %get-tuple-element.37), channel_id=1, source_target_pairs={{0,18},{1,19},{2,16},{3,17},{4,22},{5,23},{6,20},{7,21},{8,26},{9,... | collective-permute-start | bytes 294920 | tf_op jit(solution)/shard_map/ppermute | solution.py:31
  85.6 1.5 %collective-permute-done.23 = bf16[64,512]{1,0:T(8,128)(2,1)S(1)} collective-permute-done((bf16[64,512]{1,0:T(8,128)(2,1)S(1)}, bf16[64,512]{1,0:T(8,128)(2,1)S(1)}, u32[]{:S(2)}, u32[]{:S(2)}) %collective-permute-start.23) | collective-permute-done | bytes 65568 | tf_op jit(solution)/shard_map/ppermute | solution.py:31
  87.9 2.8 %collective-permute-start.26 = (bf16[64,512]{1,0:T(8,128)(2,1)S(1)}, bf16[64,512]{1,0:T(8,128)(2,1)S(1)}, u32[]{:S(2)}, u32[]{:S(2)}) collective-permute-start(bf16[64,512]{1,0:T(8,128)(2,1)S(1)} %add_convert_fusion.3.refs_0_), channel_id=1, source_target_pairs={{0,12},{4,8},{8,4},{12,0},{16,28},{20,24},{24,20},{28,16},{1,13},{... | collective-permute-start | bytes 196616 | tf_op jit(solution)/shard_map/ppermute | solution.py:31
  90.7 1.0 collective-permute-done.19
  92.1 1.5 %collective-permute-done.26.refs_3_ = bf16[64,512]{1,0:T(8,128)(2,1)S(1)} collective-permute-done((bf16[64,512]{1,0:T(8,128)(2,1)S(1)}, bf16[64,512]{1,0:T(8,128)(2,1)S(1)}, u32[]{:S(2)}, u32[]{:S(2)}) %collective-permute-start.26) | collective-permute-done | bytes 65568 | tf_op jit(solution)/shard_map/ppermute | solution.py:31
  93.9 1.8 %collective-permute-start.27 = (bf16[64,768]{1,0:T(8,128)(2,1)S(1)}, bf16[64,768]{1,0:T(8,128)(2,1)S(1)}, u32[]{:S(2)}, u32[]{:S(2)}) collective-permute-start(bf16[64,768]{1,0:T(8,128)(2,1)S(1)} %shard_map.99), channel_id=1, source_target_pairs={{0,16},{4,20},{8,24},{12,28},{16,0},{20,4},{24,8},{28,12},{1,17},{... | collective-permute-start | bytes 294920 | tf_op jit(solution)/shard_map/ppermute | solution.py:31
  95.7 1.5 %collective-permute-start.20 = (bf16[64,1536]{1,0:T(8,128)(2,1)S(1)}, bf16[64,1536]{1,0:T(8,128)(2,1)S(1)}, u32[]{:S(2)}, u32[]{:S(2)}) collective-permute-start(bf16[64,1536]{1,0:T(8,128)(2,1)S(1)} %pad_maximum_fusion.2.refs_0_), channel_id=1, source_target_pairs={{0,4},{4,0},{8,12},{12,8},{16,20},{20,16},{24,28},{28,24},{1,5},{5... | collective-permute-start | bytes 589832 | tf_op jit(solution)/shard_map/ppermute | solution.py:31
  97.6 1.6 %collective-permute-start.22 = (bf16[64,1536]{1,0:T(8,128)(2,1)S(1)}, bf16[64,1536]{1,0:T(8,128)(2,1)S(1)}, u32[]{:S(2)}, u32[]{:S(2)}) collective-permute-start(bf16[64,1536]{1,0:T(8,128)(2,1)S(1)} %pad_maximum_fusion.2.refs_0_), channel_id=1, source_target_pairs={{0,12},{4,8},{8,4},{12,0},{16,28},{20,24},{24,20},{28,16},{1,13},{... | collective-permute-start | bytes 589832 | tf_op jit(solution)/shard_map/ppermute | solution.py:31
  99.8 1.0 collective-permute-start.28
  100.8 3.8 %collective-permute-done.20.refs_1_ = bf16[64,1536]{1,0:T(8,128)(2,1)S(1)} collective-permute-done((bf16[64,1536]{1,0:T(8,128)(2,1)S(1)}, bf16[64,1536]{1,0:T(8,128)(2,1)S(1)}, u32[]{:S(2)}, u32[]{:S(2)}) %collective-permute-start.20) | collective-permute-done | bytes 196640 | tf_op jit(solution)/shard_map/ppermute | solution.py:31
  104.6 2.4 %collective-permute-done.22.refs_3_ = bf16[64,1536]{1,0:T(8,128)(2,1)S(1)} collective-permute-done((bf16[64,1536]{1,0:T(8,128)(2,1)S(1)}, bf16[64,1536]{1,0:T(8,128)(2,1)S(1)}, u32[]{:S(2)}, u32[]{:S(2)}) %collective-permute-start.22) | collective-permute-done | bytes 196640 | tf_op jit(solution)/shard_map/ppermute | solution.py:31
  107.7 1.4 %shard_map.100 = (f32[1,64,6144]{2,1,0:T(8,128)}, f32[1,64,1536]{2,1,0:T(8,128)}) custom-call(bf16[64,1536]{1,0:T(8,128)(2,1)S(1)} %pad_maximum_fusion.2.refs_0_, bf16[64,1536]{1,0:T(8,128)(2,1)S(1)} %collective-permute-done.20.refs_1_, bf16[64,1536]{1,0:T(8,128)(2,1)S(1)} %collective-permute-done.21.refs_2_, ...), custom_call_target="tpu_custom_call" | custom-call | tf_op jit(solution)/shard_map/pallas_call | solution.py:48
  (49 shorter events, 6.5 us)
Async XLA Ops:
  5.4 40.1 %copy-start.2 = (bf16[96,1536]{1,0:T(8,128)(2,1)S(1)}, bf16[96,1536]{1,0:T(8,128)(2,1)}, u32[]{:S(2)}) copy-start(bf16[96,1536]{1,0:T(8,128)(2,1)} %get-tuple-element.22.refs_0_) | copy-start | bytes 884740
  5.4 33.4 %collective-permute-start = (bf16[224,3072]{1,0:T(8,128)(2,1)}, bf16[224,3072]{1,0:T(8,128)(2,1)S(1)}, u32[]{:S(2)}, u32[]{:S(2)}) collective-permute-start(bf16[224,3072]{1,0:T(8,128)(2,1)} %get-tuple-element.23), channel_id=1, source_target_pairs={{0,4},{4,0},{8,12},{12,8},{16,20},{20,16},{24,28},{28,24},{1,5},{5... | collective-permute-start | bytes 4128776 | tf_op jit(solution)/shard_map/ppermute | solution.py:31
  8.4 26.8 %collective-permute-start.6 = (bf16[176,3072]{1,0:T(8,128)(2,1)}, bf16[176,3072]{1,0:T(8,128)(2,1)S(1)}, u32[]{:S(2)}, u32[]{:S(2)}) collective-permute-start(bf16[176,3072]{1,0:T(8,128)(2,1)} %get-tuple-element.28), channel_id=1, source_target_pairs={{0,2},{1,3},{2,0},{3,1},{4,6},{5,7},{6,4},{7,5},{8,10},{9,11},{10,... | collective-permute-start | bytes 3244040 | tf_op jit(solution)/shard_map/ppermute | solution.py:31
  9.9 25.3 %collective-permute-start.3 = (bf16[128,3072]{1,0:T(8,128)(2,1)}, bf16[128,3072]{1,0:T(8,128)(2,1)S(1)}, u32[]{:S(2)}, u32[]{:S(2)}) collective-permute-start(bf16[128,3072]{1,0:T(8,128)(2,1)} %get-tuple-element.25.refs_0_.refs_12_.refs_4_), channel_id=1, source_target_pairs={{0,8},{4,12},{8,0},{12,4},{16,24},{20,28},{24,16},{28,20},{1,9},{5... | collective-permute-start | bytes 2359304 | tf_op jit(solution)/shard_map/ppermute | solution.py:31
  11.5 30.6 %collective-permute-start.1 = (bf16[96,1536]{1,0:T(8,128)(2,1)}, bf16[96,1536]{1,0:T(8,128)(2,1)S(1)}, u32[]{:S(2)}, u32[]{:S(2)}) collective-permute-start(bf16[96,1536]{1,0:T(8,128)(2,1)} %get-tuple-element.22.refs_0_), channel_id=1, source_target_pairs={{0,16},{4,20},{8,24},{12,28},{16,0},{20,4},{24,8},{28,12},{1,17},{... | collective-permute-start | bytes 884744 | tf_op jit(solution)/shard_map/ppermute | solution.py:31
  14.1 31.4 %collective-permute-start.2 = (bf16[96,1536]{1,0:T(8,128)(2,1)}, bf16[96,1536]{1,0:T(8,128)(2,1)S(1)}, u32[]{:S(2)}, u32[]{:S(2)}) collective-permute-start(bf16[96,1536]{1,0:T(8,128)(2,1)} %get-tuple-element.26), channel_id=1, source_target_pairs={{0,24},{4,28},{8,16},{12,20},{16,8},{20,12},{24,0},{28,4},{1,25},{... | collective-permute-start | bytes 884744 | tf_op jit(solution)/shard_map/ppermute | solution.py:31
  35.2 18.6 %collective-permute-start.4 = (bf16[96,1536]{1,0:T(8,128)(2,1)}, bf16[96,1536]{1,0:T(8,128)(2,1)S(1)}, u32[]{:S(2)}, u32[]{:S(2)}) collective-permute-start(bf16[96,1536]{1,0:T(8,128)(2,1)} %get-tuple-element.26), channel_id=1, source_target_pairs={{0,8},{4,12},{8,0},{12,4},{16,24},{20,28},{24,16},{28,20},{1,9},{5... | collective-permute-start | bytes 884744 | tf_op jit(solution)/shard_map/ppermute | solution.py:31
  38.8 23.4 %collective-permute-start.13 = (bf16[128,3072]{1,0:T(8,128)(2,1)S(1)}, bf16[128,3072]{1,0:T(8,128)(2,1)S(1)}, u32[]{:S(2)}, u32[]{:S(2)}) collective-permute-start(bf16[128,3072]{1,0:T(8,128)(2,1)S(1)} %collective-permute-done.3.refs_2_.refs_14_.refs_6_), channel_id=1, source_target_pairs={{0,4},{4,0},{8,12},{12,8},{16,20},{20,16},{24,28},{28,24},{1,5},{5... | collective-permute-start | bytes 2359304 | tf_op jit(solution)/shard_map/ppermute | solution.py:31
  40.5 21.6 %collective-permute-start.15 = (bf16[128,3072]{1,0:T(8,128)(2,1)S(1)}, bf16[128,3072]{1,0:T(8,128)(2,1)S(1)}, u32[]{:S(2)}, u32[]{:S(2)}) collective-permute-start(bf16[128,3072]{1,0:T(8,128)(2,1)S(1)} %collective-permute-done.3.refs_2_.refs_14_.refs_6_), channel_id=1, source_target_pairs={{0,2},{1,3},{2,0},{3,1},{4,6},{5,7},{6,4},{7,5},{8,10},{9,11},{10,... | collective-permute-start | bytes 2359304 | tf_op jit(solution)/shard_map/ppermute | solution.py:31
  42.1 14.3 %collective-permute-start.5 = (bf16[96,1536]{1,0:T(8,128)(2,1)S(1)}, bf16[96,1536]{1,0:T(8,128)(2,1)S(1)}, u32[]{:S(2)}, u32[]{:S(2)}) collective-permute-start(bf16[96,1536]{1,0:T(8,128)(2,1)S(1)} %get-tuple-element.27.refs_1_), channel_id=1, source_target_pairs={{0,16},{4,20},{8,24},{12,28},{16,0},{20,4},{24,8},{28,12},{1,17},{... | collective-permute-start | bytes 884744 | tf_op jit(solution)/shard_map/ppermute | solution.py:31
  45.6 25.8 %collective-permute-start.9 = (bf16[4,96,1536]{2,1,0:T(8,128)(2,1)S(1)}, bf16[4,96,1536]{2,1,0:T(8,128)(2,1)S(1)}, u32[]{:S(2)}, u32[]{:S(2)}) collective-permute-start(bf16[4,96,1536]{2,1,0:T(8,128)(2,1)S(1)} %pad_maximum_fusion), channel_id=1, source_target_pairs={{0,1},{1,0},{2,3},{3,2},{4,5},{5,4},{6,7},{7,6},{8,9},{9,8},{10,11... | collective-permute-start | bytes 3538952 | tf_op jit(solution)/shard_map/ppermute | solution.py:31
  53.8 15.7 %copy-start = (bf16[128,3072]{1,0:T(8,128)(2,1)S(1)}, bf16[128,3072]{1,0:T(8,128)(2,1)}, u32[]{:S(2)}) copy-start(bf16[128,3072]{1,0:T(8,128)(2,1)} %get-tuple-element.25.refs_0_.refs_12_.refs_4_) | copy-start | bytes 2359300
  53.8 15.7 %copy-start.3 = (bf16[1,1536,64]{1,2,0:T(8,128)(2,1)S(1)}, bf16[1,1536,64]{1,2,0:T(8,128)(2,1)}, u32[]{:S(2)}) copy-start(bf16[1,1536,64]{1,2,0:T(8,128)(2,1)} %param.12) | copy-start | bytes 589828
  53.8 9.9 %collective-permute-start.7 = (bf16[96,1536]{1,0:T(8,128)(2,1)S(1)}, bf16[96,1536]{1,0:T(8,128)(2,1)S(1)}, u32[]{:S(2)}, u32[]{:S(2)}) collective-permute-start(bf16[96,1536]{1,0:T(8,128)(2,1)S(1)} %get-tuple-element.30), channel_id=1, source_target_pairs={{0,8},{4,12},{8,0},{12,4},{16,24},{20,28},{24,16},{28,20},{1,9},{5... | collective-permute-start | bytes 884744 | tf_op jit(solution)/shard_map/ppermute | solution.py:31
  56.5 12.5 %collective-permute-start.8 = (bf16[96,1536]{1,0:T(8,128)(2,1)S(1)}, bf16[96,1536]{1,0:T(8,128)(2,1)S(1)}, u32[]{:S(2)}, u32[]{:S(2)}) collective-permute-start(bf16[96,1536]{1,0:T(8,128)(2,1)S(1)} %get-tuple-element.30), channel_id=1, source_target_pairs={{0,24},{4,28},{8,16},{12,20},{16,8},{20,12},{24,0},{28,4},{1,25},{... | collective-permute-start | bytes 884744 | tf_op jit(solution)/shard_map/ppermute | solution.py:31
  62.2 16.0 %collective-permute-start.16 = (bf16[128,3072]{1,0:T(8,128)(2,1)S(1)}, bf16[128,3072]{1,0:T(8,128)(2,1)S(1)}, u32[]{:S(2)}, u32[]{:S(2)}) collective-permute-start(bf16[128,3072]{1,0:T(8,128)(2,1)S(1)} %slice.14), channel_id=1, source_target_pairs={{0,2},{1,3},{2,0},{3,1},{4,6},{5,7},{6,4},{7,5},{8,10},{9,11},{10,... | collective-permute-start | bytes 2359304 | tf_op jit(solution)/shard_map/ppermute | solution.py:31
  62.9 15.3 %collective-permute-start.17 = (bf16[128,3072]{1,0:T(8,128)(2,1)S(1)}, bf16[128,3072]{1,0:T(8,128)(2,1)S(1)}, u32[]{:S(2)}, u32[]{:S(2)}) collective-permute-start(bf16[128,3072]{1,0:T(8,128)(2,1)S(1)} %collective-permute-done.15.refs_4_), channel_id=1, source_target_pairs={{0,4},{4,0},{8,12},{12,8},{16,20},{20,16},{24,28},{28,24},{1,5},{5... | collective-permute-start | bytes 2359304 | tf_op jit(solution)/shard_map/ppermute | solution.py:31
  63.7 5.3 %collective-permute-start.11 = (bf16[96,1536]{1,0:T(8,128)(2,1)S(1)}, bf16[96,1536]{1,0:T(8,128)(2,1)S(1)}, u32[]{:S(2)}, u32[]{:S(2)}) collective-permute-start(bf16[96,1536]{1,0:T(8,128)(2,1)S(1)} %collective-permute-done.7.refs_6_), channel_id=1, source_target_pairs={{0,1},{1,0},{2,3},{3,2},{4,5},{5,4},{6,7},{7,6},{8,9},{9,8},{10,11... | collective-permute-start | bytes 884744 | tf_op jit(solution)/shard_map/ppermute | solution.py:31
  68.9 2.4 %collective-permute-start.10 = (bf16[2,96,1536]{2,1,0:T(8,128)(2,1)S(1)}, bf16[2,96,1536]{2,1,0:T(8,128)(2,1)S(1)}, u32[]{:S(2)}, u32[]{:S(2)}) collective-permute-start(bf16[2,96,1536]{2,1,0:T(8,128)(2,1)S(1)} %pad_maximum_fusion.1), channel_id=1, source_target_pairs={{0,1},{1,0},{2,3},{3,2},{4,5},{5,4},{6,7},{7,6},{8,9},{9,8},{10,11... | collective-permute-start | bytes 1769480 | tf_op jit(solution)/shard_map/ppermute | solution.py:31
  69.0 2.4 %collective-permute-start.12 = (bf16[96,1536]{1,0:T(8,128)(2,1)S(1)}, bf16[96,1536]{1,0:T(8,128)(2,1)S(1)}, u32[]{:S(2)}, u32[]{:S(2)}) collective-permute-start(bf16[96,1536]{1,0:T(8,128)(2,1)S(1)} %collective-permute-done.8.refs_7_), channel_id=1, source_target_pairs={{0,1},{1,0},{2,3},{3,2},{4,5},{5,4},{6,7},{7,6},{8,9},{9,8},{10,11... | collective-permute-start | bytes 884744 | tf_op jit(solution)/shard_map/ppermute | solution.py:31
  75.0 8.4 %collective-permute-start.14 = (bf16[64,768]{1,0:T(8,128)(2,1)S(1)}, bf16[64,768]{1,0:T(8,128)(2,1)S(1)}, u32[]{:S(2)}, u32[]{:S(2)}) collective-permute-start(bf16[64,768]{1,0:T(8,128)(2,1)S(1)} %get-tuple-element.32), channel_id=1, source_target_pairs={{0,16},{4,20},{8,24},{12,28},{16,0},{20,4},{24,8},{28,12},{1,17},{... | collective-permute-start | bytes 294920 | tf_op jit(solution)/shard_map/ppermute | solution.py:31
  82.1 5.0 %collective-permute-start.23 = (bf16[64,512]{1,0:T(8,128)(2,1)S(1)}, bf16[64,512]{1,0:T(8,128)(2,1)S(1)}, u32[]{:S(2)}, u32[]{:S(2)}) collective-permute-start(bf16[64,512]{1,0:T(8,128)(2,1)S(1)} %get-tuple-element.39), channel_id=1, source_target_pairs={{0,2},{1,3},{2,0},{3,1},{4,6},{5,7},{6,4},{7,5},{8,10},{9,11},{10,... | collective-permute-start | bytes 196616 | tf_op jit(solution)/shard_map/ppermute | solution.py:31
  83.4 7.2 %collective-permute-start.18 = (bf16[64,768]{1,0:T(8,128)(2,1)S(1)}, bf16[64,768]{1,0:T(8,128)(2,1)S(1)}, u32[]{:S(2)}, u32[]{:S(2)}) collective-permute-start(bf16[64,768]{1,0:T(8,128)(2,1)S(1)} %get-tuple-element.37), channel_id=1, source_target_pairs={{0,2},{1,3},{2,0},{3,1},{4,6},{5,7},{6,4},{7,5},{8,10},{9,11},{10,... | collective-permute-start | bytes 294920 | tf_op jit(solution)/shard_map/ppermute | solution.py:31
  84.3 7.4 %collective-permute-start.19 = (bf16[64,768]{1,0:T(8,128)(2,1)S(1)}, bf16[64,768]{1,0:T(8,128)(2,1)S(1)}, u32[]{:S(2)}, u32[]{:S(2)}) collective-permute-start(bf16[64,768]{1,0:T(8,128)(2,1)S(1)} %get-tuple-element.37), channel_id=1, source_target_pairs={{0,18},{1,19},{2,16},{3,17},{4,22},{5,23},{6,20},{7,21},{8,26},{9,... | collective-permute-start | bytes 294920 | tf_op jit(solution)/shard_map/ppermute | solution.py:31
  87.1 4.6 %collective-permute-start.24 = (bf16[64,512]{1,0:T(8,128)(2,1)S(1)}, bf16[64,512]{1,0:T(8,128)(2,1)S(1)}, u32[]{:S(2)}, u32[]{:S(2)}) collective-permute-start(bf16[64,512]{1,0:T(8,128)(2,1)S(1)} %add_convert_fusion.3.refs_0_), channel_id=1, source_target_pairs={{0,4},{4,0},{8,12},{12,8},{16,20},{20,16},{24,28},{28,24},{1,5},{5... | collective-permute-start | bytes 196616 | tf_op jit(solution)/shard_map/ppermute | solution.py:31
  87.7 4.4 %collective-permute-start.25 = (bf16[64,512]{1,0:T(8,128)(2,1)S(1)}, bf16[64,512]{1,0:T(8,128)(2,1)S(1)}, u32[]{:S(2)}, u32[]{:S(2)}) collective-permute-start(bf16[64,512]{1,0:T(8,128)(2,1)S(1)} %add_convert_fusion.3.refs_0_), channel_id=1, source_target_pairs={{0,8},{4,12},{8,0},{12,4},{16,24},{20,28},{24,16},{28,20},{1,9},{5... | collective-permute-start | bytes 196616 | tf_op jit(solution)/shard_map/ppermute | solution.py:31
  87.9 5.7 %collective-permute-start.26 = (bf16[64,512]{1,0:T(8,128)(2,1)S(1)}, bf16[64,512]{1,0:T(8,128)(2,1)S(1)}, u32[]{:S(2)}, u32[]{:S(2)}) collective-permute-start(bf16[64,512]{1,0:T(8,128)(2,1)S(1)} %add_convert_fusion.3.refs_0_), channel_id=1, source_target_pairs={{0,12},{4,8},{8,4},{12,0},{16,28},{20,24},{24,20},{28,16},{1,13},{... | collective-permute-start | bytes 196616 | tf_op jit(solution)/shard_map/ppermute | solution.py:31
  93.9 5.8 %collective-permute-start.27 = (bf16[64,768]{1,0:T(8,128)(2,1)S(1)}, bf16[64,768]{1,0:T(8,128)(2,1)S(1)}, u32[]{:S(2)}, u32[]{:S(2)}) collective-permute-start(bf16[64,768]{1,0:T(8,128)(2,1)S(1)} %shard_map.99), channel_id=1, source_target_pairs={{0,16},{4,20},{8,24},{12,28},{16,0},{20,4},{24,8},{28,12},{1,17},{... | collective-permute-start | bytes 294920 | tf_op jit(solution)/shard_map/ppermute | solution.py:31
  95.7 8.9 %collective-permute-start.20 = (bf16[64,1536]{1,0:T(8,128)(2,1)S(1)}, bf16[64,1536]{1,0:T(8,128)(2,1)S(1)}, u32[]{:S(2)}, u32[]{:S(2)}) collective-permute-start(bf16[64,1536]{1,0:T(8,128)(2,1)S(1)} %pad_maximum_fusion.2.refs_0_), channel_id=1, source_target_pairs={{0,4},{4,0},{8,12},{12,8},{16,20},{20,16},{24,28},{28,24},{1,5},{5... | collective-permute-start | bytes 589832 | tf_op jit(solution)/shard_map/ppermute | solution.py:31
  97.2 7.4 %collective-permute-start.21 = (bf16[64,1536]{1,0:T(8,128)(2,1)S(1)}, bf16[64,1536]{1,0:T(8,128)(2,1)S(1)}, u32[]{:S(2)}, u32[]{:S(2)}) collective-permute-start(bf16[64,1536]{1,0:T(8,128)(2,1)S(1)} %pad_maximum_fusion.2.refs_0_), channel_id=1, source_target_pairs={{0,8},{4,12},{8,0},{12,4},{16,24},{20,28},{24,16},{28,20},{1,9},{5... | collective-permute-start | bytes 589832 | tf_op jit(solution)/shard_map/ppermute | solution.py:31
  97.6 9.3 %collective-permute-start.22 = (bf16[64,1536]{1,0:T(8,128)(2,1)S(1)}, bf16[64,1536]{1,0:T(8,128)(2,1)S(1)}, u32[]{:S(2)}, u32[]{:S(2)}) collective-permute-start(bf16[64,1536]{1,0:T(8,128)(2,1)S(1)} %pad_maximum_fusion.2.refs_0_), channel_id=1, source_target_pairs={{0,12},{4,8},{8,4},{12,0},{16,28},{20,24},{24,20},{28,16},{1,13},{... | collective-permute-start | bytes 589832 | tf_op jit(solution)/shard_map/ppermute | solution.py:31
  99.8 8.0 %collective-permute-start.28 = (bf16[64,768]{1,0:T(8,128)(2,1)S(1)}, bf16[64,768]{1,0:T(8,128)(2,1)S(1)}, u32[]{:S(2)}, u32[]{:S(2)}) collective-permute-start(bf16[64,768]{1,0:T(8,128)(2,1)S(1)} %add_convert_fusion.refs_4_), channel_id=1, source_target_pairs={{0,4},{4,0},{8,12},{12,8},{16,20},{20,16},{24,28},{28,24},{1,5},{5... | collective-permute-start | bytes 294920 | tf_op jit(solution)/shard_map/ppermute | solution.py:31
  (1 other events, 7.9 us)

commit v8 on v7

--- a/solution.py
+++ b/solution.py
@@ -292,7 +292,7 @@
     z2n, z3n = over_half(w00), over_both(w01)
     one = (fx, fy, fz, z2n, z3n)
     wx0, wx1 = fx[rows:, : 4 * part], fx[rows:, 4 * part : 8 * part]
-    fzx, fzy = over_x(after(fz, fx, fy)), over_y(after(fz, fx, fy))
+    fzx, fzy = over_x(after(fz, fx)), over_y(after(fz, fx, fy))
     z1n, z2f = over_low(after(w01, fz)), over_half(after(wx0, z2n))
     near = over_core(jnp.stack([w00, wx0, z2n, z3n]))
     two = (fzx, fzy)

time: 109 us -> 109 us (level)
  no operation moved by 1% of the time
where the time goes in v8:
time: 109 us
  waiting for transfers between devices  54.1 us (50%)
  starting transfers between devices  39.4 us (36%)
  Pallas kernels  13.8 us (13%)
  between operations  1.43 us (1%)
    ppermute x29, waiting for transfers between devices, flip(): lax.ppermute(value, axis, [(i, i ^ bits) for i in range(size)])  54.1 us
    ppermute x29, starting transfers between devices, flip(): lax.ppermute(value, axis, [(i, i ^ bits) for i in range(size)])  39.4 us
    pallas_call x6, Pallas kernels, call(): pl.pallas_call(body, in_specs=ins, out_specs=[whole(o.shape) if space is...  13.8 us
  transfers between devices with their start and end apart: 29, of which 16 were waited for; matrix products, arithmetic and copies ran while one was open for 0% of the time, Pallas kernels for 7%

profile of v8, /device:TPU:0, one launch (start us, length us, event | category | flops | bytes accessed | tf_op | source)
XLA Modules:
  0.0 109.1 jit_solution(10394141182190621743)
XLA Ops:
  1.3 4.1 %shard_map.95 = (bf16[128,3072]{1,0:T(8,128)(2,1)}, bf16[176,3072]{1,0:T(8,128)(2,1)}, bf16[224,3072]{1,0:T(8,128)(2,1)}, bf16[96,1536]{1,0:T(8,128)(2,1)}, bf16[96,1536]{1,0:T(8,128)(2,1)}) custom-call(bf16[1,144,1536]{2,1,0:T(8,128)(2,1)} %frames_ref.1, f32[1536]{0:T(1024)} %gain_ref.1, bf16[192,1536]{1,0:T(8,128)(2,1)} %first_ref.1, ...), custom_call_target="tpu_custom_call" | custom-call | tf_op jit(solution)/shard_map/pallas_call | solution.py:48
  5.4 3.0 %collective-permute-start = (bf16[224,3072]{1,0:T(8,128)(2,1)}, bf16[224,3072]{1,0:T(8,128)(2,1)S(1)}, u32[]{:S(2)}, u32[]{:S(2)}) collective-permute-start(bf16[224,3072]{1,0:T(8,128)(2,1)} %get-tuple-element.24), channel_id=1, source_target_pairs={{0,4},{4,0},{8,12},{12,8},{16,20},{20,16},{24,28},{28,24},{1,5},{5... | collective-permute-start | bytes 4128776 | tf_op jit(solution)/shard_map/ppermute | solution.py:31
  8.4 1.5 %collective-permute-start.6 = (bf16[176,3072]{1,0:T(8,128)(2,1)}, bf16[176,3072]{1,0:T(8,128)(2,1)S(1)}, u32[]{:S(2)}, u32[]{:S(2)}) collective-permute-start(bf16[176,3072]{1,0:T(8,128)(2,1)} %get-tuple-element.29), channel_id=1, source_target_pairs={{0,2},{1,3},{2,0},{3,1},{4,6},{5,7},{6,4},{7,5},{8,10},{9,11},{10,... | collective-permute-start | bytes 3244040 | tf_op jit(solution)/shard_map/ppermute | solution.py:31
  9.9 1.6 %collective-permute-start.3 = (bf16[128,3072]{1,0:T(8,128)(2,1)}, bf16[128,3072]{1,0:T(8,128)(2,1)S(1)}, u32[]{:S(2)}, u32[]{:S(2)}) collective-permute-start(bf16[128,3072]{1,0:T(8,128)(2,1)} %get-tuple-element.26.refs_0_.refs_12_.refs_4_), channel_id=1, source_target_pairs={{0,8},{4,12},{8,0},{12,4},{16,24},{20,28},{24,16},{28,20},{1,9},{5... | collective-permute-start | bytes 2359304 | tf_op jit(solution)/shard_map/ppermute | solution.py:31
  11.5 2.6 %collective-permute-start.1 = (bf16[96,1536]{1,0:T(8,128)(2,1)}, bf16[96,1536]{1,0:T(8,128)(2,1)S(1)}, u32[]{:S(2)}, u32[]{:S(2)}) collective-permute-start(bf16[96,1536]{1,0:T(8,128)(2,1)} %get-tuple-element.23.refs_0_), channel_id=1, source_target_pairs={{0,16},{4,20},{8,24},{12,28},{16,0},{20,4},{24,8},{28,12},{1,17},{... | collective-permute-start | bytes 884744 | tf_op jit(solution)/shard_map/ppermute | solution.py:31
  14.3 20.9 %collective-permute-done.3.refs_2_.refs_14_.refs_6_ = bf16[128,3072]{1,0:T(8,128)(2,1)S(1)} collective-permute-done((bf16[128,3072]{1,0:T(8,128)(2,1)}, bf16[128,3072]{1,0:T(8,128)(2,1)S(1)}, u32[]{:S(2)}, u32[]{:S(2)}) %collective-permute-start.3) | collective-permute-done | bytes 786464 | tf_op jit(solution)/shard_map/ppermute | solution.py:31
  35.2 3.6 %collective-permute-done.refs_1_.refs_13_.refs_5_ = bf16[224,3072]{1,0:T(8,128)(2,1)S(1)} collective-permute-done((bf16[224,3072]{1,0:T(8,128)(2,1)}, bf16[224,3072]{1,0:T(8,128)(2,1)S(1)}, u32[]{:S(2)}, u32[]{:S(2)}) %collective-permute-start) | collective-permute-done | bytes 1376288 | tf_op jit(solution)/shard_map/ppermute | solution.py:31
  38.8 1.7 %collective-permute-start.13 = (bf16[128,3072]{1,0:T(8,128)(2,1)S(1)}, bf16[128,3072]{1,0:T(8,128)(2,1)S(1)}, u32[]{:S(2)}, u32[]{:S(2)}) collective-permute-start(bf16[128,3072]{1,0:T(8,128)(2,1)S(1)} %collective-permute-done.3.refs_2_.refs_14_.refs_6_), channel_id=1, source_target_pairs={{0,4},{4,0},{8,12},{12,8},{16,20},{20,16},{24,28},{28,24},{1,5},{5... | collective-permute-start | bytes 2359304 | tf_op jit(solution)/shard_map/ppermute | solution.py:31
  40.5 1.5 %collective-permute-start.15 = (bf16[128,3072]{1,0:T(8,128)(2,1)S(1)}, bf16[128,3072]{1,0:T(8,128)(2,1)S(1)}, u32[]{:S(2)}, u32[]{:S(2)}) collective-permute-start(bf16[128,3072]{1,0:T(8,128)(2,1)S(1)} %collective-permute-done.3.refs_2_.refs_14_.refs_6_), channel_id=1, source_target_pairs={{0,2},{1,3},{2,0},{3,1},{4,6},{5,7},{6,4},{7,5},{8,10},{9,11},{10,... | collective-permute-start | bytes 2359304 | tf_op jit(solution)/shard_map/ppermute | solution.py:31
  42.1 3.3 %collective-permute-start.5 = (bf16[96,1536]{1,0:T(8,128)(2,1)S(1)}, bf16[96,1536]{1,0:T(8,128)(2,1)S(1)}, u32[]{:S(2)}, u32[]{:S(2)}) collective-permute-start(bf16[96,1536]{1,0:T(8,128)(2,1)S(1)} %get-tuple-element.28.refs_1_), channel_id=1, source_target_pairs={{0,16},{4,20},{8,24},{12,28},{16,0},{20,4},{24,8},{28,12},{1,17},{... | collective-permute-start | bytes 884744 | tf_op jit(solution)/shard_map/ppermute | solution.py:31
  45.7 8.1 %collective-permute-done.4.refs_4_ = bf16[96,1536]{1,0:T(8,128)(2,1)S(1)} collective-permute-done((bf16[96,1536]{1,0:T(8,128)(2,1)}, bf16[96,1536]{1,0:T(8,128)(2,1)S(1)}, u32[]{:S(2)}, u32[]{:S(2)}) %collective-permute-start.4) | collective-permute-done | bytes 294944 | tf_op jit(solution)/shard_map/ppermute | solution.py:31
  53.8 2.7 %collective-permute-done.5.refs_5_ = bf16[96,1536]{1,0:T(8,128)(2,1)S(1)} collective-permute-done((bf16[96,1536]{1,0:T(8,128)(2,1)S(1)}, bf16[96,1536]{1,0:T(8,128)(2,1)S(1)}, u32[]{:S(2)}, u32[]{:S(2)}) %collective-permute-start.5) | collective-permute-done | bytes 294944 | tf_op jit(solution)/shard_map/ppermute | solution.py:31
  56.5 5.6 %collective-permute-start.8 = (bf16[96,1536]{1,0:T(8,128)(2,1)S(1)}, bf16[96,1536]{1,0:T(8,128)(2,1)S(1)}, u32[]{:S(2)}, u32[]{:S(2)}) collective-permute-start(bf16[96,1536]{1,0:T(8,128)(2,1)S(1)} %get-tuple-element.31), channel_id=1, source_target_pairs={{0,24},{4,28},{8,16},{12,20},{16,8},{20,12},{24,0},{28,4},{1,25},{... | collective-permute-start | bytes 884744 | tf_op jit(solution)/shard_map/ppermute | solution.py:31
  63.7 5.3 %collective-permute-done.8.refs_7_ = bf16[96,1536]{1,0:T(8,128)(2,1)S(1)} collective-permute-done((bf16[96,1536]{1,0:T(8,128)(2,1)S(1)}, bf16[96,1536]{1,0:T(8,128)(2,1)S(1)}, u32[]{:S(2)}, u32[]{:S(2)}) %collective-permute-start.8) | collective-permute-done | bytes 294944 | tf_op jit(solution)/shard_map/ppermute | solution.py:31
  70.1 1.3 %collective-permute-done.12.refs_11_ = bf16[96,1536]{1,0:T(8,128)(2,1)S(1)} collective-permute-done((bf16[96,1536]{1,0:T(8,128)(2,1)S(1)}, bf16[96,1536]{1,0:T(8,128)(2,1)S(1)}, u32[]{:S(2)}, u32[]{:S(2)}) %collective-permute-start.12) | collective-permute-done | bytes 294944 | tf_op jit(solution)/shard_map/ppermute | solution.py:31
  71.4 3.6 %shard_map.97 = (bf16[64,768]{1,0:T(8,128)(2,1)S(1)}, f32[64,512]{1,0:T(8,128)S(1)}, bf16[1536,768]{1,0:T(8,128)(2,1)S(1)}, bf16[1536,768]{1,0:T(8,128)(2,1)S(1)}) custom-call(bf16[96,1536]{1,0:T(8,128)(2,1)S(1)} %copy-done.2, bf16[96,1536]{1,0:T(8,128)(2,1)S(1)} %get-tuple-element.28.refs_1_, bf16[96,1536]{1,0:T(8,128)(2,1)S(1)} %collective-permute-done.1.refs_2_, ...), custom_call_target="tpu_custom_call" | custom-call | tf_op jit(solution)/shard_map/pallas_call | solution.py:48
  74.9 3.3 %collective-permute-start.14 = (bf16[64,768]{1,0:T(8,128)(2,1)S(1)}, bf16[64,768]{1,0:T(8,128)(2,1)S(1)}, u32[]{:S(2)}, u32[]{:S(2)}) collective-permute-start(bf16[64,768]{1,0:T(8,128)(2,1)S(1)} %get-tuple-element.33), channel_id=1, source_target_pairs={{0,16},{4,20},{8,24},{12,28},{16,0},{20,4},{24,8},{28,12},{1,17},{... | collective-permute-start | bytes 294920 | tf_op jit(solution)/shard_map/ppermute | solution.py:31
  78.2 3.9 %shard_map.98 = (bf16[64,768]{1,0:T(8,128)(2,1)S(1)}, bf16[64,512]{1,0:T(8,128)(2,1)S(1)}) custom-call(bf16[1536,768]{1,0:T(8,128)(2,1)S(1)} %get-tuple-element.34.refs_0_, bf16[1536,768]{1,0:T(8,128)(2,1)S(1)} %get-tuple-element.35.refs_1_, bf16[176,3072]{1,0:T(8,128)(2,1)S(1)} %collective-permute-done.6.refs_2_.refs_6_, ...), custom_call_target="tpu_custom_call" | custom-call | tf_op jit(solution)/shard_map/pallas_call | solution.py:48
  82.1 1.2 %collective-permute-start.23 = (bf16[64,512]{1,0:T(8,128)(2,1)S(1)}, bf16[64,512]{1,0:T(8,128)(2,1)S(1)}, u32[]{:S(2)}, u32[]{:S(2)}) collective-permute-start(bf16[64,512]{1,0:T(8,128)(2,1)S(1)} %get-tuple-element.41), channel_id=1, source_target_pairs={{0,2},{1,3},{2,0},{3,1},{4,6},{5,7},{6,4},{7,5},{8,10},{9,11},{10,... | collective-permute-start | bytes 196616 | tf_op jit(solution)/shard_map/ppermute | solution.py:31
  83.4 0.9 collective-permute-start.18
  84.3 1.3 %collective-permute-start.19 = (bf16[64,768]{1,0:T(8,128)(2,1)S(1)}, bf16[64,768]{1,0:T(8,128)(2,1)S(1)}, u32[]{:S(2)}, u32[]{:S(2)}) collective-permute-start(bf16[64,768]{1,0:T(8,128)(2,1)S(1)} %get-tuple-element.39), channel_id=1, source_target_pairs={{0,18},{1,19},{2,16},{3,17},{4,22},{5,23},{6,20},{7,21},{8,26},{9,... | collective-permute-start | bytes 294920 | tf_op jit(solution)/shard_map/ppermute | solution.py:31
  85.6 1.5 %collective-permute-done.23 = bf16[64,512]{1,0:T(8,128)(2,1)S(1)} collective-permute-done((bf16[64,512]{1,0:T(8,128)(2,1)S(1)}, bf16[64,512]{1,0:T(8,128)(2,1)S(1)}, u32[]{:S(2)}, u32[]{:S(2)}) %collective-permute-start.23) | collective-permute-done | bytes 65568 | tf_op jit(solution)/shard_map/ppermute | solution.py:31
  87.9 2.8 %collective-permute-start.26 = (bf16[64,512]{1,0:T(8,128)(2,1)S(1)}, bf16[64,512]{1,0:T(8,128)(2,1)S(1)}, u32[]{:S(2)}, u32[]{:S(2)}) collective-permute-start(bf16[64,512]{1,0:T(8,128)(2,1)S(1)} %add_convert_fusion.3.refs_0_), channel_id=1, source_target_pairs={{0,12},{4,8},{8,4},{12,0},{16,28},{20,24},{24,20},{28,16},{1,13},{... | collective-permute-start | bytes 196616 | tf_op jit(solution)/shard_map/ppermute | solution.py:31
  90.7 1.0 collective-permute-done.19
  92.1 1.5 %collective-permute-done.26.refs_3_ = bf16[64,512]{1,0:T(8,128)(2,1)S(1)} collective-permute-done((bf16[64,512]{1,0:T(8,128)(2,1)S(1)}, bf16[64,512]{1,0:T(8,128)(2,1)S(1)}, u32[]{:S(2)}, u32[]{:S(2)}) %collective-permute-start.26) | collective-permute-done | bytes 65568 | tf_op jit(solution)/shard_map/ppermute | solution.py:31
  93.9 1.7 %collective-permute-start.27 = (bf16[64,768]{1,0:T(8,128)(2,1)S(1)}, bf16[64,768]{1,0:T(8,128)(2,1)S(1)}, u32[]{:S(2)}, u32[]{:S(2)}) collective-permute-start(bf16[64,768]{1,0:T(8,128)(2,1)S(1)} %shard_map.99), channel_id=1, source_target_pairs={{0,16},{4,20},{8,24},{12,28},{16,0},{20,4},{24,8},{28,12},{1,17},{... | collective-permute-start | bytes 294920 | tf_op jit(solution)/shard_map/ppermute | solution.py:31
  95.7 1.5 %collective-permute-start.20 = (bf16[64,1536]{1,0:T(8,128)(2,1)S(1)}, bf16[64,1536]{1,0:T(8,128)(2,1)S(1)}, u32[]{:S(2)}, u32[]{:S(2)}) collective-permute-start(bf16[64,1536]{1,0:T(8,128)(2,1)S(1)} %pad_maximum_fusion.2.refs_0_), channel_id=1, source_target_pairs={{0,4},{4,0},{8,12},{12,8},{16,20},{20,16},{24,28},{28,24},{1,5},{5... | collective-permute-start | bytes 589832 | tf_op jit(solution)/shard_map/ppermute | solution.py:31
  97.6 1.6 %collective-permute-start.22 = (bf16[64,1536]{1,0:T(8,128)(2,1)S(1)}, bf16[64,1536]{1,0:T(8,128)(2,1)S(1)}, u32[]{:S(2)}, u32[]{:S(2)}) collective-permute-start(bf16[64,1536]{1,0:T(8,128)(2,1)S(1)} %pad_maximum_fusion.2.refs_0_), channel_id=1, source_target_pairs={{0,12},{4,8},{8,4},{12,0},{16,28},{20,24},{24,20},{28,16},{1,13},{... | collective-permute-start | bytes 589832 | tf_op jit(solution)/shard_map/ppermute | solution.py:31
  99.8 1.0 collective-permute-start.28
  100.8 3.8 %collective-permute-done.20.refs_1_ = bf16[64,1536]{1,0:T(8,128)(2,1)S(1)} collective-permute-done((bf16[64,1536]{1,0:T(8,128)(2,1)S(1)}, bf16[64,1536]{1,0:T(8,128)(2,1)S(1)}, u32[]{:S(2)}, u32[]{:S(2)}) %collective-permute-start.20) | collective-permute-done | bytes 196640 | tf_op jit(solution)/shard_map/ppermute | solution.py:31
  104.6 2.4 %collective-permute-done.22.refs_3_ = bf16[64,1536]{1,0:T(8,128)(2,1)S(1)} collective-permute-done((bf16[64,1536]{1,0:T(8,128)(2,1)S(1)}, bf16[64,1536]{1,0:T(8,128)(2,1)S(1)}, u32[]{:S(2)}, u32[]{:S(2)}) %collective-permute-start.22) | collective-permute-done | bytes 196640 | tf_op jit(solution)/shard_map/ppermute | solution.py:31
  107.7 1.4 %shard_map.100 = (f32[1,64,6144]{2,1,0:T(8,128)}, f32[1,64,1536]{2,1,0:T(8,128)}) custom-call(bf16[64,1536]{1,0:T(8,128)(2,1)S(1)} %pad_maximum_fusion.2.refs_0_, bf16[64,1536]{1,0:T(8,128)(2,1)S(1)} %collective-permute-done.20.refs_1_, bf16[64,1536]{1,0:T(8,128)(2,1)S(1)} %collective-permute-done.21.refs_2_, ...), custom_call_target="tpu_custom_call" | custom-call | tf_op jit(solution)/shard_map/pallas_call | solution.py:48
  (49 shorter events, 6.5 us)
Async XLA Ops:
  5.4 40.1 %copy-start.2 = (bf16[96,1536]{1,0:T(8,128)(2,1)S(1)}, bf16[96,1536]{1,0:T(8,128)(2,1)}, u32[]{:S(2)}) copy-start(bf16[96,1536]{1,0:T(8,128)(2,1)} %get-tuple-element.23.refs_0_) | copy-start | bytes 884740
  5.4 33.4 %collective-permute-start = (bf16[224,3072]{1,0:T(8,128)(2,1)}, bf16[224,3072]{1,0:T(8,128)(2,1)S(1)}, u32[]{:S(2)}, u32[]{:S(2)}) collective-permute-start(bf16[224,3072]{1,0:T(8,128)(2,1)} %get-tuple-element.24), channel_id=1, source_target_pairs={{0,4},{4,0},{8,12},{12,8},{16,20},{20,16},{24,28},{28,24},{1,5},{5... | collective-permute-start | bytes 4128776 | tf_op jit(solution)/shard_map/ppermute | solution.py:31
  8.4 32.1 %collective-permute-start.6 = (bf16[176,3072]{1,0:T(8,128)(2,1)}, bf16[176,3072]{1,0:T(8,128)(2,1)S(1)}, u32[]{:S(2)}, u32[]{:S(2)}) collective-permute-start(bf16[176,3072]{1,0:T(8,128)(2,1)} %get-tuple-element.29), channel_id=1, source_target_pairs={{0,2},{1,3},{2,0},{3,1},{4,6},{5,7},{6,4},{7,5},{8,10},{9,11},{10,... | collective-permute-start | bytes 3244040 | tf_op jit(solution)/shard_map/ppermute | solution.py:31
  9.9 25.3 %collective-permute-start.3 = (bf16[128,3072]{1,0:T(8,128)(2,1)}, bf16[128,3072]{1,0:T(8,128)(2,1)S(1)}, u32[]{:S(2)}, u32[]{:S(2)}) collective-permute-start(bf16[128,3072]{1,0:T(8,128)(2,1)} %get-tuple-element.26.refs_0_.refs_12_.refs_4_), channel_id=1, source_target_pairs={{0,8},{4,12},{8,0},{12,4},{16,24},{20,28},{24,16},{28,20},{1,9},{5... | collective-permute-start | bytes 2359304 | tf_op jit(solution)/shard_map/ppermute | solution.py:31
  11.5 30.6 %collective-permute-start.1 = (bf16[96,1536]{1,0:T(8,128)(2,1)}, bf16[96,1536]{1,0:T(8,128)(2,1)S(1)}, u32[]{:S(2)}, u32[]{:S(2)}) collective-permute-start(bf16[96,1536]{1,0:T(8,128)(2,1)} %get-tuple-element.23.refs_0_), channel_id=1, source_target_pairs={{0,16},{4,20},{8,24},{12,28},{16,0},{20,4},{24,8},{28,12},{1,17},{... | collective-permute-start | bytes 884744 | tf_op jit(solution)/shard_map/ppermute | solution.py:31
  14.1 31.4 %collective-permute-start.2 = (bf16[96,1536]{1,0:T(8,128)(2,1)}, bf16[96,1536]{1,0:T(8,128)(2,1)S(1)}, u32[]{:S(2)}, u32[]{:S(2)}) collective-permute-start(bf16[96,1536]{1,0:T(8,128)(2,1)} %get-tuple-element.27), channel_id=1, source_target_pairs={{0,24},{4,28},{8,16},{12,20},{16,8},{20,12},{24,0},{28,4},{1,25},{... | collective-permute-start | bytes 884744 | tf_op jit(solution)/shard_map/ppermute | solution.py:31
  35.2 18.6 %collective-permute-start.4 = (bf16[96,1536]{1,0:T(8,128)(2,1)}, bf16[96,1536]{1,0:T(8,128)(2,1)S(1)}, u32[]{:S(2)}, u32[]{:S(2)}) collective-permute-start(bf16[96,1536]{1,0:T(8,128)(2,1)} %get-tuple-element.27), channel_id=1, source_target_pairs={{0,8},{4,12},{8,0},{12,4},{16,24},{20,28},{24,16},{28,20},{1,9},{5... | collective-permute-start | bytes 884744 | tf_op jit(solution)/shard_map/ppermute | solution.py:31
  38.8 23.4 %collective-permute-start.13 = (bf16[128,3072]{1,0:T(8,128)(2,1)S(1)}, bf16[128,3072]{1,0:T(8,128)(2,1)S(1)}, u32[]{:S(2)}, u32[]{:S(2)}) collective-permute-start(bf16[128,3072]{1,0:T(8,128)(2,1)S(1)} %collective-permute-done.3.refs_2_.refs_14_.refs_6_), channel_id=1, source_target_pairs={{0,4},{4,0},{8,12},{12,8},{16,20},{20,16},{24,28},{28,24},{1,5},{5... | collective-permute-start | bytes 2359304 | tf_op jit(solution)/shard_map/ppermute | solution.py:31
  40.5 21.7 %collective-permute-start.15 = (bf16[128,3072]{1,0:T(8,128)(2,1)S(1)}, bf16[128,3072]{1,0:T(8,128)(2,1)S(1)}, u32[]{:S(2)}, u32[]{:S(2)}) collective-permute-start(bf16[128,3072]{1,0:T(8,128)(2,1)S(1)} %collective-permute-done.3.refs_2_.refs_14_.refs_6_), channel_id=1, source_target_pairs={{0,2},{1,3},{2,0},{3,1},{4,6},{5,7},{6,4},{7,5},{8,10},{9,11},{10,... | collective-permute-start | bytes 2359304 | tf_op jit(solution)/shard_map/ppermute | solution.py:31
  42.1 14.3 %collective-permute-start.5 = (bf16[96,1536]{1,0:T(8,128)(2,1)S(1)}, bf16[96,1536]{1,0:T(8,128)(2,1)S(1)}, u32[]{:S(2)}, u32[]{:S(2)}) collective-permute-start(bf16[96,1536]{1,0:T(8,128)(2,1)S(1)} %get-tuple-element.28.refs_1_), channel_id=1, source_target_pairs={{0,16},{4,20},{8,24},{12,28},{16,0},{20,4},{24,8},{28,12},{1,17},{... | collective-permute-start | bytes 884744 | tf_op jit(solution)/shard_map/ppermute | solution.py:31
  45.6 25.8 %collective-permute-start.9 = (bf16[4,96,1536]{2,1,0:T(8,128)(2,1)S(1)}, bf16[4,96,1536]{2,1,0:T(8,128)(2,1)S(1)}, u32[]{:S(2)}, u32[]{:S(2)}) collective-permute-start(bf16[4,96,1536]{2,1,0:T(8,128)(2,1)S(1)} %pad_maximum_fusion), channel_id=1, source_target_pairs={{0,1},{1,0},{2,3},{3,2},{4,5},{5,4},{6,7},{7,6},{8,9},{9,8},{10,11... | collective-permute-start | bytes 3538952 | tf_op jit(solution)/shard_map/ppermute | solution.py:31
  53.8 15.7 %copy-start = (bf16[128,3072]{1,0:T(8,128)(2,1)S(1)}, bf16[128,3072]{1,0:T(8,128)(2,1)}, u32[]{:S(2)}) copy-start(bf16[128,3072]{1,0:T(8,128)(2,1)} %get-tuple-element.26.refs_0_.refs_12_.refs_4_) | copy-start | bytes 2359300
  53.8 15.7 %copy-start.3 = (bf16[1,1536,64]{1,2,0:T(8,128)(2,1)S(1)}, bf16[1,1536,64]{1,2,0:T(8,128)(2,1)}, u32[]{:S(2)}) copy-start(bf16[1,1536,64]{1,2,0:T(8,128)(2,1)} %param.12) | copy-start | bytes 589828
  53.8 9.9 %collective-permute-start.7 = (bf16[96,1536]{1,0:T(8,128)(2,1)S(1)}, bf16[96,1536]{1,0:T(8,128)(2,1)S(1)}, u32[]{:S(2)}, u32[]{:S(2)}) collective-permute-start(bf16[96,1536]{1,0:T(8,128)(2,1)S(1)} %get-tuple-element.31), channel_id=1, source_target_pairs={{0,8},{4,12},{8,0},{12,4},{16,24},{20,28},{24,16},{28,20},{1,9},{5... | collective-permute-start | bytes 884744 | tf_op jit(solution)/shard_map/ppermute | solution.py:31
  56.5 12.5 %collective-permute-start.8 = (bf16[96,1536]{1,0:T(8,128)(2,1)S(1)}, bf16[96,1536]{1,0:T(8,128)(2,1)S(1)}, u32[]{:S(2)}, u32[]{:S(2)}) collective-permute-start(bf16[96,1536]{1,0:T(8,128)(2,1)S(1)} %get-tuple-element.31), channel_id=1, source_target_pairs={{0,24},{4,28},{8,16},{12,20},{16,8},{20,12},{24,0},{28,4},{1,25},{... | collective-permute-start | bytes 884744 | tf_op jit(solution)/shard_map/ppermute | solution.py:31
  62.2 16.0 %collective-permute-start.16 = (bf16[128,3072]{1,0:T(8,128)(2,1)S(1)}, bf16[128,3072]{1,0:T(8,128)(2,1)S(1)}, u32[]{:S(2)}, u32[]{:S(2)}) collective-permute-start(bf16[128,3072]{1,0:T(8,128)(2,1)S(1)} %slice.14), channel_id=1, source_target_pairs={{0,2},{1,3},{2,0},{3,1},{4,6},{5,7},{6,4},{7,5},{8,10},{9,11},{10,... | collective-permute-start | bytes 2359304 | tf_op jit(solution)/shard_map/ppermute | solution.py:31
  62.9 15.3 %collective-permute-start.17 = (bf16[128,3072]{1,0:T(8,128)(2,1)S(1)}, bf16[128,3072]{1,0:T(8,128)(2,1)S(1)}, u32[]{:S(2)}, u32[]{:S(2)}) collective-permute-start(bf16[128,3072]{1,0:T(8,128)(2,1)S(1)} %collective-permute-done.15.refs_4_), channel_id=1, source_target_pairs={{0,4},{4,0},{8,12},{12,8},{16,20},{20,16},{24,28},{28,24},{1,5},{5... | collective-permute-start | bytes 2359304 | tf_op jit(solution)/shard_map/ppermute | solution.py:31
  63.7 5.3 %collective-permute-start.11 = (bf16[96,1536]{1,0:T(8,128)(2,1)S(1)}, bf16[96,1536]{1,0:T(8,128)(2,1)S(1)}, u32[]{:S(2)}, u32[]{:S(2)}) collective-permute-start(bf16[96,1536]{1,0:T(8,128)(2,1)S(1)} %collective-permute-done.7.refs_6_), channel_id=1, source_target_pairs={{0,1},{1,0},{2,3},{3,2},{4,5},{5,4},{6,7},{7,6},{8,9},{9,8},{10,11... | collective-permute-start | bytes 884744 | tf_op jit(solution)/shard_map/ppermute | solution.py:31
  68.9 2.4 %collective-permute-start.10 = (bf16[2,96,1536]{2,1,0:T(8,128)(2,1)S(1)}, bf16[2,96,1536]{2,1,0:T(8,128)(2,1)S(1)}, u32[]{:S(2)}, u32[]{:S(2)}) collective-permute-start(bf16[2,96,1536]{2,1,0:T(8,128)(2,1)S(1)} %pad_maximum_fusion.1), channel_id=1, source_target_pairs={{0,1},{1,0},{2,3},{3,2},{4,5},{5,4},{6,7},{7,6},{8,9},{9,8},{10,11... | collective-permute-start | bytes 1769480 | tf_op jit(solution)/shard_map/ppermute | solution.py:31
  69.0 2.4 %collective-permute-start.12 = (bf16[96,1536]{1,0:T(8,128)(2,1)S(1)}, bf16[96,1536]{1,0:T(8,128)(2,1)S(1)}, u32[]{:S(2)}, u32[]{:S(2)}) collective-permute-start(bf16[96,1536]{1,0:T(8,128)(2,1)S(1)} %collective-permute-done.8.refs_7_), channel_id=1, source_target_pairs={{0,1},{1,0},{2,3},{3,2},{4,5},{5,4},{6,7},{7,6},{8,9},{9,8},{10,11... | collective-permute-start | bytes 884744 | tf_op jit(solution)/shard_map/ppermute | solution.py:31
  74.9 8.5 %collective-permute-start.14 = (bf16[64,768]{1,0:T(8,128)(2,1)S(1)}, bf16[64,768]{1,0:T(8,128)(2,1)S(1)}, u32[]{:S(2)}, u32[]{:S(2)}) collective-permute-start(bf16[64,768]{1,0:T(8,128)(2,1)S(1)} %get-tuple-element.33), channel_id=1, source_target_pairs={{0,16},{4,20},{8,24},{12,28},{16,0},{20,4},{24,8},{28,12},{1,17},{... | collective-permute-start | bytes 294920 | tf_op jit(solution)/shard_map/ppermute | solution.py:31
  82.1 5.0 %collective-permute-start.23 = (bf16[64,512]{1,0:T(8,128)(2,1)S(1)}, bf16[64,512]{1,0:T(8,128)(2,1)S(1)}, u32[]{:S(2)}, u32[]{:S(2)}) collective-permute-start(bf16[64,512]{1,0:T(8,128)(2,1)S(1)} %get-tuple-element.41), channel_id=1, source_target_pairs={{0,2},{1,3},{2,0},{3,1},{4,6},{5,7},{6,4},{7,5},{8,10},{9,11},{10,... | collective-permute-start | bytes 196616 | tf_op jit(solution)/shard_map/ppermute | solution.py:31
  83.4 7.3 %collective-permute-start.18 = (bf16[64,768]{1,0:T(8,128)(2,1)S(1)}, bf16[64,768]{1,0:T(8,128)(2,1)S(1)}, u32[]{:S(2)}, u32[]{:S(2)}) collective-permute-start(bf16[64,768]{1,0:T(8,128)(2,1)S(1)} %get-tuple-element.39), channel_id=1, source_target_pairs={{0,2},{1,3},{2,0},{3,1},{4,6},{5,7},{6,4},{7,5},{8,10},{9,11},{10,... | collective-permute-start | bytes 294920 | tf_op jit(solution)/shard_map/ppermute | solution.py:31
  84.3 7.4 %collective-permute-start.19 = (bf16[64,768]{1,0:T(8,128)(2,1)S(1)}, bf16[64,768]{1,0:T(8,128)(2,1)S(1)}, u32[]{:S(2)}, u32[]{:S(2)}) collective-permute-start(bf16[64,768]{1,0:T(8,128)(2,1)S(1)} %get-tuple-element.39), channel_id=1, source_target_pairs={{0,18},{1,19},{2,16},{3,17},{4,22},{5,23},{6,20},{7,21},{8,26},{9,... | collective-permute-start | bytes 294920 | tf_op jit(solution)/shard_map/ppermute | solution.py:31
  87.1 4.6 %collective-permute-start.24 = (bf16[64,512]{1,0:T(8,128)(2,1)S(1)}, bf16[64,512]{1,0:T(8,128)(2,1)S(1)}, u32[]{:S(2)}, u32[]{:S(2)}) collective-permute-start(bf16[64,512]{1,0:T(8,128)(2,1)S(1)} %add_convert_fusion.3.refs_0_), channel_id=1, source_target_pairs={{0,4},{4,0},{8,12},{12,8},{16,20},{20,16},{24,28},{28,24},{1,5},{5... | collective-permute-start | bytes 196616 | tf_op jit(solution)/shard_map/ppermute | solution.py:31
  87.7 4.4 %collective-permute-start.25 = (bf16[64,512]{1,0:T(8,128)(2,1)S(1)}, bf16[64,512]{1,0:T(8,128)(2,1)S(1)}, u32[]{:S(2)}, u32[]{:S(2)}) collective-permute-start(bf16[64,512]{1,0:T(8,128)(2,1)S(1)} %add_convert_fusion.3.refs_0_), channel_id=1, source_target_pairs={{0,8},{4,12},{8,0},{12,4},{16,24},{20,28},{24,16},{28,20},{1,9},{5... | collective-permute-start | bytes 196616 | tf_op jit(solution)/shard_map/ppermute | solution.py:31
  87.9 5.8 %collective-permute-start.26 = (bf16[64,512]{1,0:T(8,128)(2,1)S(1)}, bf16[64,512]{1,0:T(8,128)(2,1)S(1)}, u32[]{:S(2)}, u32[]{:S(2)}) collective-permute-start(bf16[64,512]{1,0:T(8,128)(2,1)S(1)} %add_convert_fusion.3.refs_0_), channel_id=1, source_target_pairs={{0,12},{4,8},{8,4},{12,0},{16,28},{20,24},{24,20},{28,16},{1,13},{... | collective-permute-start | bytes 196616 | tf_op jit(solution)/shard_map/ppermute | solution.py:31
  93.9 5.8 %collective-permute-start.27 = (bf16[64,768]{1,0:T(8,128)(2,1)S(1)}, bf16[64,768]{1,0:T(8,128)(2,1)S(1)}, u32[]{:S(2)}, u32[]{:S(2)}) collective-permute-start(bf16[64,768]{1,0:T(8,128)(2,1)S(1)} %shard_map.99), channel_id=1, source_target_pairs={{0,16},{4,20},{8,24},{12,28},{16,0},{20,4},{24,8},{28,12},{1,17},{... | collective-permute-start | bytes 294920 | tf_op jit(solution)/shard_map/ppermute | solution.py:31
  95.7 8.9 %collective-permute-start.20 = (bf16[64,1536]{1,0:T(8,128)(2,1)S(1)}, bf16[64,1536]{1,0:T(8,128)(2,1)S(1)}, u32[]{:S(2)}, u32[]{:S(2)}) collective-permute-start(bf16[64,1536]{1,0:T(8,128)(2,1)S(1)} %pad_maximum_fusion.2.refs_0_), channel_id=1, source_target_pairs={{0,4},{4,0},{8,12},{12,8},{16,20},{20,16},{24,28},{28,24},{1,5},{5... | collective-permute-start | bytes 589832 | tf_op jit(solution)/shard_map/ppermute | solution.py:31
  97.2 7.4 %collective-permute-start.21 = (bf16[64,1536]{1,0:T(8,128)(2,1)S(1)}, bf16[64,1536]{1,0:T(8,128)(2,1)S(1)}, u32[]{:S(2)}, u32[]{:S(2)}) collective-permute-start(bf16[64,1536]{1,0:T(8,128)(2,1)S(1)} %pad_maximum_fusion.2.refs_0_), channel_id=1, source_target_pairs={{0,8},{4,12},{8,0},{12,4},{16,24},{20,28},{24,16},{28,20},{1,9},{5... | collective-permute-start | bytes 589832 | tf_op jit(solution)/shard_map/ppermute | solution.py:31
  97.6 9.3 %collective-permute-start.22 = (bf16[64,1536]{1,0:T(8,128)(2,1)S(1)}, bf16[64,1536]{1,0:T(8,128)(2,1)S(1)}, u32[]{:S(2)}, u32[]{:S(2)}) collective-permute-start(bf16[64,1536]{1,0:T(8,128)(2,1)S(1)} %pad_maximum_fusion.2.refs_0_), channel_id=1, source_target_pairs={{0,12},{4,8},{8,4},{12,0},{16,28},{20,24},{24,20},{28,16},{1,13},{... | collective-permute-start | bytes 589832 | tf_op jit(solution)/shard_map/ppermute | solution.py:31
  99.8 7.9 %collective-permute-start.28 = (bf16[64,768]{1,0:T(8,128)(2,1)S(1)}, bf16[64,768]{1,0:T(8,128)(2,1)S(1)}, u32[]{:S(2)}, u32[]{:S(2)}) collective-permute-start(bf16[64,768]{1,0:T(8,128)(2,1)S(1)} %add_convert_fusion.refs_4_), channel_id=1, source_target_pairs={{0,4},{4,0},{8,12},{12,8},{16,20},{20,16},{24,28},{28,24},{1,5},{5... | collective-permute-start | bytes 294920 | tf_op jit(solution)/shard_map/ppermute | solution.py:31
  (1 other events, 7.9 us)
